TPU v7x, 32 devices: a whole 2x2x4 slice. The times are simulated.
32 devices in a mesh: gz: 2 (over x), row: 8 (over z, core), col: 2 (over y).
Axes of the slice: x: 2, y: 2, z: 4, core: 2. Of those that a mesh axis runs over, the one named last changes fastest.
Arguments:
- volume: bfloat16 [32, 512, 512], P('gz', 'row', 'col'), may hold values from -7 to 7
Outputs:
- tensor: float32 [6, 8, 128, 128], P(None, 'gz', 'row', 'col')
All inputs are finite; a program needn't handle non-finite values.
Results may differ from a plain program's by a relative error of at most 0.0028.
Values may be sent and summed in bfloat16 or wider, within the bound.
No kernel may reach another device: no remote copies, remote signals or barrier semaphores. Data moves between devices by JAX's collectives and lax.ppermute only.
A program may use at most 128 MiB of HBM per device.

v0:
```python
import jax
import jax.numpy as jnp
import ml_dtypes
import numpy as np
from jax import lax
from jax.experimental import pallas as pl
from jax.experimental.pallas import tpu as pltpu
from jax.sharding import PartitionSpec as P

R = 3
R2 = 8
HALO = 16
NEED = R + R2
NT = (((1,), (1,)), ((), ()))
F32 = jnp.float32
BF16 = jnp.bfloat16

pair_table = ((0, 0), (1, 1), (2, 2), (0, 1), (0, 2), (1, 2))


def gauss_taps(radius):
    offsets = np.arange(-radius, radius + 1).astype(np.float32)
    spread = np.float32(radius / 3.0)
    smooth = np.exp(-offsets * offsets / (np.float32(2.0) * spread * spread))
    smooth = smooth / np.sum(smooth)
    slopes = offsets * smooth
    slopes = slopes / np.sum(offsets * slopes)
    as_f32 = lambda t: t.astype(ml_dtypes.bfloat16).astype(np.float32)
    return as_f32(smooth), as_f32(slopes)


SMOOTH_D, SLOPE_D = gauss_taps(R)
SMOOTH_I, _ = gauss_taps(R2)


def band(taps, sources, targets):
    radius = len(taps) // 2
    gap = np.asarray(sources)[:, None] - np.asarray(targets)[None, :]
    return np.where(np.abs(gap) <= radius, taps[np.clip(gap + radius, 0, 2 * radius)], 0.0)


def weight_table(depth, rows, cols):
    ext = rows + 2 * HALO
    grad_rows = rows + 16
    far = 10**6
    y_in = np.arange(ext) - HALO
    y_out = np.arange(grad_rows) - R2
    smooth_y = band(SMOOTH_D, y_in, y_out).T
    slope_y = band(SLOPE_D, y_in, y_out).T
    zero = np.zeros_like(smooth_y)
    wy = np.block([[smooth_y, zero], [slope_y, zero], [zero, smooth_y]])
    x_all = np.arange(cols)
    slot_in = np.full(32, far)
    slot_in[0:8] = cols + np.arange(8)
    slot_in[8:14] = np.arange(6)
    slot_in[14:20] = cols - 6 + np.arange(6)
    slot_in[21:32] = np.arange(-11, 0)
    slot_out = np.full(32, -far)
    slot_out[0:11] = np.arange(-8, 3)
    slot_out[11:19] = cols - 3 + np.arange(8)
    eye8 = np.eye(8)
    inner = np.where((x_all >= R) & (x_all < cols - R), x_all, far)
    quarter = cols // 4
    coarse_edge = np.full(8, 3 * far)
    coarse_edge[0:5] = [0, 1, 2, quarter - 2, quarter - 1]
    xs_edge = band(SMOOTH_I, slot_out, 4 * coarse_edge)
    ys = band(SMOOTH_I, y_out, 4 * np.arange(rows // 4)).T
    own = np.zeros((32, cols))
    for slot in range(8, 20):
        own[slot, slot_in[slot]] = 1.0
    right = (x_all[None, :] == cols - HALO + np.arange(HALO)[:, None]).astype(np.float32)
    left = (x_all[None, :] == np.arange(HALO)[:, None]).astype(np.float32)
    zq = 4 * (np.arange(depth // 4 + 4) - 2)
    zs = band(SMOOTH_I, np.arange(depth), zq)
    place = np.zeros((8, 128))
    for j in range(5):
        place[j, coarse_edge[j]] = 1.0
    g = np.einsum("zq,jx->zjqx", zs, place).reshape(depth * 8, len(zq) * 128)
    parts = {
        "wy": wy,
        "wy_slope": smooth_y,
        "wxd": band(SLOPE_D, x_all, x_all),
        "wxs": band(SMOOTH_D, x_all, x_all),
        "bdd": np.kron(eye8, band(SLOPE_D, slot_in, slot_out)),
        "bds": np.kron(eye8, band(SMOOTH_D, slot_in, slot_out)),
        "ysm": np.kron(np.eye(3), ys),
        "xsm": band(SMOOTH_I, inner, 4 * np.arange(quarter)),
        "bdx": np.kron(eye8, xs_edge),
        "sel_right": right,
        "sel_left": left,
        "sel_own": own,
        "g0": g[:, 0:256],
        "g1": g[:, 256:512],
        "g2": g[:, 512:768],
        "g3": g[:, 768:1024],
    }
    place_of, blocks, at = {}, [], 0
    for name, part in parts.items():
        height = -(-part.shape[0] // 16) * 16
        block = np.zeros((height, 256), np.float32)
        block[: part.shape[0], : part.shape[1]] = part
        place_of[name] = (at, part.shape[0], part.shape[1])
        blocks.append(block)
        at += height
    return np.concatenate(blocks).astype(ml_dtypes.bfloat16), place_of, zs


def z_filter(v, count):
    for z in range(count):
        w = v[z : z + 7]
        smooth = w[3] * float(SMOOTH_D[3])
        slope = None
        for s in (1, 2, 3):
            smooth = smooth + (w[3 + s] + w[3 - s]) * float(SMOOTH_D[3 + s])
            term = (w[3 + s] - w[3 - s]) * float(SLOPE_D[3 + s])
            slope = term if slope is None else slope + term
        yield z, smooth.astype(BF16), slope.astype(BF16)


def getter(place_of, w):
    def get(name, width=None):
        at, height, own_width = place_of[name]
        return w[at : at + height, 0 : (width or own_width)]

    return get


def spread_rows(first, transposed):
    shape = (16 * HALO, 16 * NEED) if transposed else (16 * NEED, 16 * HALO)
    packed = lax.broadcasted_iota(jnp.int32, shape, 1 if transposed else 0)
    full = lax.broadcasted_iota(jnp.int32, shape, 0 if transposed else 1)
    z = lax.shift_right_logical(packed * 373, 12)
    return jnp.where(full == packed + z * (HALO - NEED) + first, 1.0, 0.0).astype(BF16)


def load_kernel(n_row, vol, s1, s2, zmsg):
    depth, rows, cols = vol.shape
    odd = lax.rem(lax.axis_index("row"), 2) == 1
    base = jnp.where(lax.axis_index("gz") == 0, depth - R, 0)
    top = vol[:, 0:HALO, :].reshape(depth * HALO, cols)
    bottom = vol[:, rows - HALO : rows, :].reshape(depth * HALO, cols)
    to_before = jnp.dot(spread_rows(0, False), top, preferred_element_type=F32).astype(BF16)
    to_after = jnp.dot(
        spread_rows(HALO - NEED, False), bottom, preferred_element_type=F32
    ).astype(BF16)
    s1[...] = jnp.where(odd, to_before, to_after)
    s2[...] = jnp.where(odd, to_after, to_before)
    zmsg[...] = vol[pl.ds(base, R)]


def stage_kernel(vol, w, vol_out, w_out, sems):
    copies = [
        pltpu.make_async_copy(vol, vol_out, sems.at[0]),
        pltpu.make_async_copy(w, w_out, sems.at[1]),
    ]
    for copy in copies:
        copy.start()
    for copy in copies:
        copy.wait()


def pack_kernel(place_of, n_row, n_col, vol, r1, r2, w, *refs):
    n_side = 1 if n_col == 2 else 2
    yud, zcorner, strips = refs[0:3]
    xmsgs, zxmsgs = refs[3 : 3 + n_side], refs[3 + n_side : 3 + 2 * n_side]
    ext = refs[3 + 2 * n_side]
    depth, rows, cols = vol.shape
    gz, row = lax.axis_index("gz"), lax.axis_index("row")
    odd = lax.rem(row, 2) == 1
    base = jnp.where(gz == 0, depth - R, 0)
    none = jnp.zeros((), BF16)
    got1, got2 = r1[...], r2[...]
    from_before = jnp.where(odd, got1, jnp.where(row == 0, none, got2))
    from_after = jnp.where(odd, jnp.where(row == n_row - 1, none, got2), got1)
    above = jnp.dot(
        spread_rows(HALO - NEED, True), from_before, preferred_element_type=F32
    ).astype(BF16).reshape(depth, HALO, cols)
    below = jnp.dot(
        spread_rows(0, True), from_after, preferred_element_type=F32
    ).astype(BF16).reshape(depth, HALO, cols)
    yud[:, 0:HALO, :] = above
    yud[:, HALO:, :] = below
    zcorner[...] = yud[pl.ds(base, R)]
    ext[:, 0:HALO, :] = above
    ext[:, HALO : HALO + rows, :] = vol[...]
    ext[:, HALO + rows : 2 * HALO + rows, :] = below
    ext[:, 2 * HALO + rows :, :] = jnp.zeros((depth, 128 - rows - 2 * HALO, cols), BF16)
    get = getter(place_of, w)
    if n_col == 2:
        col = lax.axis_index("col")
        at_r, at_l = place_of["sel_right"][0], place_of["sel_left"][0]
        at = pl.multiple_of(jnp.where(col == 0, at_r, at_l), 16)
        selects = [get("sel_own"), w[pl.ds(at, HALO), :]]
    else:
        selects = [get("sel_own"), get("sel_right"), get("sel_left")]
    select = jnp.concatenate(selects, axis=0)
    for z in range(depth):
        picked = lax.dot_general(select, ext[z], NT, preferred_element_type=F32).astype(BF16)
        strips[z] = picked[0:32]
        for side in range(n_side):
            xmsgs[side][z] = picked[32 + 16 * side : 48 + 16 * side]
    for side in range(n_side):
        zxmsgs[side][...] = xmsgs[side][pl.ds(base, R)]


def row_mask(get, n_row, rows, gr, quarter_rows):
    row = lax.axis_index("row")
    lane = lax.broadcasted_iota(jnp.int32, (3 * quarter_rows, 3 * gr), 1)
    y_out = lax.rem(lane, gr) - R2
    outside = ((row == 0) & (y_out < 0)) | ((row == n_row - 1) & (y_out >= rows))
    return jnp.where(outside, 0.0, get("ysm").astype(F32)).astype(BF16)


def layers_to_sums(get, ysm, load, count, shape, u_ref, zf, planes, prod, sm):
    rows, cols = shape
    ext = rows + 2 * HALO
    gr = rows + 16
    n_rows = 6 * (rows // 4)
    half_rows = n_rows // 2
    for tile in range(cols // 128):
        lanes = slice(tile * 128, tile * 128 + 128)
        for at in range(0, ext, 16):
            for z, smooth, slope in z_filter(load(at, lanes), count):
                zf[z, at : at + 16, lanes] = smooth
                zf[z, ext + at : ext + at + 16, lanes] = slope
    wy = get("wy")
    for z in range(count):
        out = jnp.dot(wy, zf[z], preferred_element_type=F32).astype(BF16)
        planes[0, z] = out[0:gr]
        planes[1, z] = out[gr : 2 * gr]
        planes[2, z] = out[2 * gr :]
    group = 4 if count % 4 == 0 else count
    for at in range(0, count, group):
        grads = []
        for f, name in enumerate(("wxd", "wxs", "wxs")):
            part = planes[f, at : at + group].reshape(group * gr, cols)
            out = jnp.dot(part, get(name), preferred_element_type=F32)
            grads.append(out.astype(BF16).reshape(group, gr, cols))
        for c, (a, b) in enumerate(pair_table):
            prod[at : at + group, c * gr : (c + 1) * gr] = grads[a] * grads[b]
    for z in range(count):
        for half in range(2):
            part = prod[z, half * 3 * gr : (half + 1) * 3 * gr]
            out = jnp.dot(ysm, part, preferred_element_type=F32)
            sm[z, half * half_rows : (half + 1) * half_rows] = out.astype(BF16)
    out = jnp.dot(
        sm[...].reshape(count * n_rows, cols), get("xsm"), preferred_element_type=F32
    )
    u_ref[...] = out.reshape(count, n_rows, cols // 4)


def block_loader(vol, yud, rows):
    def layer(z, at, lanes):
        if at < HALO:
            return yud[z, at : at + 16, lanes].astype(F32)
        if at < HALO + rows:
            return vol[z, at - HALO : at - HALO + 16, lanes].astype(F32)
        return yud[z, at - rows : at - rows + 16, lanes].astype(F32)

    return layer


FIRST = 8
EDGE = R
LAST = 5


def first_kernel(place_of, n_row, vol, yud, w, u_ref, *scratch):
    depth, rows, cols = vol.shape
    get = getter(place_of, w)
    ysm = row_mask(get, n_row, rows, rows + 16, rows // 4)
    base = jnp.where(lax.axis_index("gz") == 0, depth - EDGE - FIRST - R, 0)
    layer = block_loader(vol, yud, rows)
    load = lambda at, lanes: [layer(base + k, at, lanes) for k in range(FIRST + 2 * R)]
    layers_to_sums(get, ysm, load, FIRST, (rows, cols), u_ref, *scratch)


def strip_sums(place_of, n_col, ysm, w, layers, shape, hs, hd, pstrip):
    rows, cols = shape
    gr = rows + 16
    quarter_rows = rows // 4
    get = getter(place_of, w)
    col = lax.axis_index("col")
    for z, smooth, slope in z_filter(layers, 8):
        hs[32 * z : 32 * z + 32] = smooth
        hd[32 * z : 32 * z + 32] = slope
    at = place_of["wy"][0]
    wy_strip = w[at : at + 2 * gr, 0:128]
    p01 = lax.dot_general(wy_strip, hs[...], NT, preferred_element_type=F32).astype(BF16)
    wy_slope = get("wy_slope", 128)
    p2 = lax.dot_general(wy_slope, hd[...], NT, preferred_element_type=F32).astype(BF16)
    slot = lax.rem(lax.broadcasted_iota(jnp.int32, (3 * quarter_rows, 256), 1), 32)
    outside_x = ((col == 0) & (slot < 8)) | ((col == n_col - 1) & (slot >= 14))
    g0 = jnp.dot(p01[0:gr], get("bdd"), preferred_element_type=F32).astype(BF16)
    g1 = jnp.dot(p01[gr:], get("bds"), preferred_element_type=F32).astype(BF16)
    g2 = jnp.dot(p2, get("bds"), preferred_element_type=F32).astype(BF16)
    grads = [g0, g1, g2]
    for c, (a, b) in enumerate(pair_table):
        pstrip[c * gr : (c + 1) * gr] = grads[a] * grads[b]
    halves = []
    for half in range(2):
        rows_of = slice(half * 3 * gr, (half + 1) * 3 * gr)
        out = jnp.dot(ysm, pstrip[rows_of], preferred_element_type=F32)
        halves.append(jnp.where(outside_x, 0.0, out).astype(BF16))
    smoothed = jnp.concatenate(halves, axis=0)
    return jnp.dot(smoothed, get("bdx"), preferred_element_type=F32)


def split(array):
    high = array.astype(BF16)
    return high, (array - high.astype(F32)).astype(BF16)


def strip_joiner(n_col, strips_shape):
    slots = lax.broadcasted_iota(jnp.int32, strips_shape, 0)
    col = lax.axis_index("col")
    if n_col == 2:
        keep = ((slots < 8) & (col == 0)) | ((slots >= 21) & (col == 1))
        sides = lambda refs, z: (refs[0][z], refs[0][z])
    else:
        keep = (slots < 8) | (slots >= 21)
        sides = lambda refs, z: (refs[1][z], refs[0][z])

    def join(own_part, refs, z):
        both = jnp.concatenate([part.astype(F32) for part in sides(refs, z)], axis=0)
        return jnp.where(keep, both, own_part)

    return join


def edge_kernel(place_of, zs, n_row, n_col, vol, yud, zown, zcorner, strips, xh, zxh, u1, w,
                u_ref, us_ref, send_ref, zext, hs, hd, pstrip, *scratch):
    depth, rows, cols = vol.shape
    ext = rows + 2 * HALO
    quarter_rows, quarter = rows // 4, cols // 4
    n_zq = zs.shape[1]
    get = getter(place_of, w)
    low = lax.axis_index("gz") == 0
    ysm = row_mask(get, n_row, rows, rows + 16, quarter_rows)

    zext[:, 0:HALO] = zcorner[:, 0:HALO]
    zext[:, HALO : HALO + rows] = zown[...]
    zext[:, HALO + rows : ext] = zcorner[:, HALO:]
    zext[:, ext:] = jnp.zeros((R, 128 - ext, cols), BF16)

    join = strip_joiner(n_col, (32, 128))
    halo = lax.dot_general(
        get("sel_own"), zext[...].reshape(R * 128, cols), NT, preferred_element_type=F32
    )
    halo = [join(halo[:, 128 * k : 128 * k + 128], zxh, k) for k in range(R)]
    own = lambda z: join(strips[z].astype(F32), xh, z)
    layers = [jnp.where(low, own(depth - 11 + k), halo[k]) for k in range(R)]
    layers += [own(jnp.where(low, depth - 11, -R) + k) for k in range(R, 11)]
    layers += [jnp.where(low, halo[k - 11], own(k - R)) for k in range(11, 14)]
    u_strip = strip_sums(place_of, n_col, ysm, w, layers, (rows, cols), hs, hd, pstrip)
    us_ref[...] = u_strip
    g_last = place_of["g%d" % (n_zq // 2 - 1)][0] + 64
    at = pl.multiple_of(jnp.where(low, g_last, place_of["g0"][0]), 16)
    g = w[pl.ds(at, 64), :]
    strip_send = sum(jnp.dot(part, g, preferred_element_type=F32) for part in split(u_strip))

    layer = block_loader(vol, yud, rows)
    start = jnp.where(low, depth - R, 0)
    outer = jnp.where(low, depth - 2 * R, R)

    def load(at, lanes):
        beyond = [zext[k, at : at + 16, lanes].astype(F32) for k in range(R)]
        inner = [layer(outer + k, at, lanes) for k in range(R)]
        middle = [layer(start + k, at, lanes) for k in range(R)]
        before = [jnp.where(low, inner[k], beyond[k]) for k in range(R)]
        after = [jnp.where(low, beyond[k], inner[k]) for k in range(R)]
        return before + middle + after

    layers_to_sums(get, ysm, load, EDGE, (rows, cols), u_ref, *scratch)

    sends = []
    for k in range(2):
        total = strip_send[:, 128 * k : 128 * k + quarter]
        for i in range(FIRST + EDGE):
            from_low = depth - EDGE - FIRST + i
            from_high = EDGE + i if i < FIRST else i - FIRST
            a = float(zs[from_low, n_zq - 2 + k])
            b = float(zs[from_high, k])
            if a == 0.0 and b == 0.0:
                continue
            u = u1[i] if i < FIRST else u_ref[i - FIRST]
            total = total + u * jnp.where(low, a, b)
        sends.append(total)
    send_ref[...] = jnp.concatenate(sends, axis=1).astype(BF16)


def last_kernel(place_of, zs, n_row, n_col, vol, yud, strips, xh, u1, u2, us, w,
                own_ref, u3, hs, hd, pstrip, *scratch):
    depth, rows, cols = vol.shape
    quarter_rows, quarter = rows // 4, cols // 4
    get = getter(place_of, w)
    low = lax.axis_index("gz") == 0
    ysm = row_mask(get, n_row, rows, rows + 16, quarter_rows)
    join = strip_joiner(n_col, (32, 128))
    own = lambda z: join(strips[z].astype(F32), xh, z)
    strip_layers = [jnp.where(low, 0.0, own(depth - 11 + k)) for k in range(R)]
    strip_layers += [own(jnp.where(low, -R, depth - 11) + k) for k in range(R, 11)]
    strip_layers += [jnp.where(low, own(k - R), 0.0) for k in range(11, 14)]
    other = strip_sums(place_of, n_col, ysm, w, strip_layers, (rows, cols), hs, hd, pstrip)
    both = jnp.where(
        low,
        jnp.concatenate([other, us[...]], axis=1),
        jnp.concatenate([us[...], other], axis=1),
    )
    parts = split(both)
    v = []
    for name in ("g1", "g2"):
        out = sum(jnp.dot(part, get(name), preferred_element_type=F32) for part in parts)
        v += [out[:, 0:quarter], out[:, 128 : 128 + quarter]]
    layer = block_loader(vol, yud, rows)
    base = jnp.where(low, -R, depth - LAST - R)
    before_on = jnp.where(low, 0.0, 1.0)
    after_on = jnp.where(low, 1.0, 0.0)

    def load(at, lanes):
        out = []
        for k in range(LAST + 2 * R):
            block = layer(jnp.clip(base + k, 0, depth - 1), at, lanes)
            if k < R:
                block = block * before_on
            elif k >= LAST + R:
                block = block * after_on
            out.append(block)
        return out

    layers_to_sums(get, ysm, load, LAST, (rows, cols), u3, *scratch)
    for q in range(depth // 4):
        total = v[q]
        for i in range(depth):
            if i < FIRST:
                u, from_low, from_high = u1[i], depth - EDGE - FIRST + i, EDGE + i
            elif i < FIRST + EDGE:
                k = i - FIRST
                u, from_low, from_high = u2[k], depth - EDGE + k, k
            else:
                k = i - FIRST - EDGE
                u, from_low, from_high = u3[k], k, depth - LAST + k
            a, b = float(zs[from_low, q + 2]), float(zs[from_high, q + 2])
            if a == 0.0 and b == 0.0:
                continue
            total = total + u * jnp.where(low, a, b)
        own_ref[:, q] = total.reshape(6, quarter_rows, quarter)


def add_kernel(own, got, out):
    n_q, quarter = own.shape[1], own.shape[3]
    low = lax.axis_index("gz") == 0
    parts = [
        got[:, k * quarter : (k + 1) * quarter].astype(F32).reshape(own.shape[0], -1, quarter)
        for k in range(2)
    ]
    for q in range(n_q):
        total = own[:, q]
        if q < 2:
            total = total + parts[q] * jnp.where(low, 0.0, 1.0)
        if q >= n_q - 2:
            total = total + parts[q - n_q + 2] * jnp.where(low, 1.0, 0.0)
        out[:, q] = total


def call(body, outs, operands, scratch, name, in_hbm=False, flops=0):
    vmem = pl.BlockSpec(memory_space=pltpu.VMEM)
    source = pl.BlockSpec(memory_space=pltpu.HBM) if in_hbm else vmem
    moved = sum(o.size * o.dtype.itemsize for o in list(outs) + list(operands))
    return pl.pallas_call(
        body,
        out_shape=list(outs),
        in_specs=[source] * len(operands),
        out_specs=[vmem] * len(outs),
        scratch_shapes=scratch,
        compiler_params=pltpu.CompilerParams(vmem_limit_bytes=24 * 2**20),
        cost_estimate=pl.CostEstimate(flops=flops, bytes_accessed=moved, transcendentals=0),
        name=name,
    )(*operands)


def per_device(volume):
    depth, rows, cols = volume.shape
    n_row, n_col = lax.axis_size("row"), lax.axis_size("col")
    table, place_of, zs = weight_table(depth, rows, cols)
    ext = rows + 2 * HALO
    gr = rows + 16
    quarter_rows, quarter = rows // 4, cols // 4
    n_rows = 6 * quarter_rows
    sds = jax.ShapeDtypeStruct
    dma = pltpu.SemaphoreType.DMA

    def scratch_for(count):
        return [
            pltpu.VMEM((count, 2 * ext, cols), BF16),
            pltpu.VMEM((3, count, gr, cols), BF16),
            pltpu.VMEM((count, 6 * gr, cols), BF16),
            pltpu.VMEM((count, n_rows, cols), BF16),
        ]

    layer_flops = 2 * cols * (3 * gr * 2 * ext + 3 * gr * cols + n_rows * 3 * gr + n_rows * quarter)

    s1, s2, zmsg = call(
        lambda *refs: load_kernel(n_row, *refs),
        [sds((depth * NEED, cols), BF16)] * 2 + [sds((R, rows, cols), BF16)],
        [volume], [], "load",
    )
    inner = [(i, i + 1) for i in range(1, n_row - 1, 2)]
    inner = inner + [(j, i) for i, j in inner] + [(0, 0), (n_row - 1, n_row - 1)]
    r2 = lax.ppermute(s2, "row", inner)
    r1 = lax.ppermute(s1, "row", [(i, i ^ 1) for i in range(n_row)])
    swap = [(0, 1), (1, 0)]
    zown = lax.ppermute(zmsg, "gz", swap)
    vol, w = call(
        stage_kernel,
        [sds(volume.shape, BF16), sds(table.shape, BF16)],
        [volume, jnp.asarray(table)], [dma((2,))], "stage", in_hbm=True,
    )

    n_side = 1 if n_col == 2 else 2
    packed = call(
        lambda *refs: pack_kernel(place_of, n_row, n_col, *refs),
        [sds((depth, 2 * HALO, cols), BF16), sds((R, 2 * HALO, cols), BF16)]
        + [sds((depth, 32, 128), BF16)]
        + [sds((depth, HALO, 128), BF16)] * n_side
        + [sds((R, HALO, 128), BF16)] * n_side,
        [vol, r1, r2, w], [pltpu.VMEM((depth, 128, cols), BF16)], "pack",
    )
    yud, zcmsg, strips = packed[0:3]
    xmsgs, zxmsgs = packed[3 : 3 + n_side], packed[3 + n_side :]
    zcorner = lax.ppermute(zcmsg, "gz", swap)
    if n_col == 2:
        xh = [lax.ppermute(xmsgs[0], "col", swap)]
        zxh = [lax.ppermute(zxmsgs[0], ("gz", "col"), [(i, 3 - i) for i in range(4)])]
    else:
        xh, zxh = [], []
        for side, step in enumerate((1, -1)):
            line = [(i, i + step) for i in range(n_col) if 0 <= i + step < n_col]
            both = [
                (z * n_col + i, (1 - z) * n_col + j) for z in range(2) for i, j in line
            ]
            xh.append(lax.ppermute(xmsgs[side], "col", line))
            zxh.append(lax.ppermute(zxmsgs[side], ("gz", "col"), both))

    (u1,) = call(
        lambda *refs: first_kernel(place_of, n_row, *refs),
        [sds((FIRST, n_rows, quarter), F32)],
        [vol, yud, w], scratch_for(FIRST), "first", flops=FIRST * layer_flops,
    )

    def edge_body(*refs):
        x_refs = refs[5 : 5 + n_side]
        zx_refs = refs[5 + n_side : 5 + 2 * n_side]
        edge_kernel(
            place_of, zs, n_row, n_col, *refs[0:5], x_refs, zx_refs, *refs[5 + 2 * n_side :]
        )

    strip_scratch = [
        pltpu.VMEM((8 * 32, 128), BF16),
        pltpu.VMEM((8 * 32, 128), BF16),
        pltpu.VMEM((6 * gr, 8 * 32), BF16),
    ]
    u2, us, send = call(
        edge_body,
        [
            sds((EDGE, n_rows, quarter), F32),
            sds((n_rows, 64), F32),
            sds((n_rows, 2 * quarter), BF16),
        ],
        [vol, yud, zown, zcorner, strips] + xh + zxh + [u1, w],
        [pltpu.VMEM((R, 128, cols), BF16)] + strip_scratch + scratch_for(EDGE),
        "edge", flops=2 * EDGE * layer_flops,
    )
    got = lax.ppermute(send, "gz", swap)

    def last_body(*refs):
        last_kernel(
            place_of, zs, n_row, n_col, *refs[0:3], refs[3 : 3 + n_side], *refs[3 + n_side :]
        )

    (own,) = call(
        last_body,
        [sds((6, depth // 4, quarter_rows, quarter), F32)],
        [vol, yud, strips] + xh + [u1, u2, us, w],
        [pltpu.VMEM((LAST, n_rows, quarter), F32)] + strip_scratch + scratch_for(LAST),
        "last", flops=LAST * layer_flops,
    )
    (out,) = call(add_kernel, [sds(own.shape, F32)], [own, got], [], "add")
    return out


def solution(mesh):
    return jax.shard_map(
        per_device,
        mesh=mesh,
        in_specs=(P("gz", "row", "col"),),
        out_specs=P(None, "gz", "row", "col"),
        check_vma=False,
    )
```

profile of v0, /device:TPU:8, one launch (start us, length us, event | category | flops | bytes accessed | tf_op | source)
XLA Modules:
  0.0 21.3 jit_solution(7569492549073337621)
XLA Ops:
  0.0 0.0 copy-start
  0.0 1.0 %copy-done = bf16[16,64,256]{2,1,0:T(8,128)(2,1)S(1)} copy-done((bf16[16,64,256]{2,1,0:T(8,128)(2,1)S(1)}, bf16[16,64,256]{2,1,0:T(8,128)(2,1)}, u32[]{:S(2)}) %copy-start) | copy-done | bytes 524312
  1.0 0.2 load.1
  1.3 0.1 collective-permute-start
  1.3 1.9 %collective-permute-start.1 = (bf16[176,256]{1,0:T(8,128)(2,1)S(1)}, bf16[176,256]{1,0:T(8,128)(2,1)S(1)}, u32[]{:S(2)}, u32[]{:S(2)}) collective-permute-start(bf16[176,256]{1,0:T(8,128)(2,1)S(1)} %get-tuple-element.20), channel_id=1, source_target_pairs={{2,4},{6,8},{10,12},{4,2},{8,6},{12,10},{0,0},{14,14},{3,5},{7,9},... | collective-permute-start | bytes 270344 | tf_op jit(solution)/shard_map/ppermute | solution.py:510
  3.3 2.1 %collective-permute-start.3 = (bf16[3,64,256]{2,1,0:T(8,128)(2,1)S(1)}, bf16[3,64,256]{2,1,0:T(8,128)(2,1)S(1)}, u32[]{:S(2)}, u32[]{:S(2)}) collective-permute-start(bf16[3,64,256]{2,1,0:T(8,128)(2,1)S(1)} %get-tuple-element.25), channel_id=1, source_target_pairs={{0,16},{16,0},{1,17},{17,1},{2,18},{18,2},{3,19},{19,3},{4,20},{20... | collective-permute-start | bytes 294920 | tf_op jit(solution)/shard_map/ppermute | solution.py:513
  5.4 1.3 %copy-done.1 = bf16[2480,256]{1,0:T(8,128)(2,1)S(1)} copy-done((bf16[2480,256]{1,0:T(8,128)(2,1)S(1)}, bf16[2480,256]{1,0:T(8,128)(2,1)}, u32[]{:S(2)}) %copy-start.1) | copy-done | bytes 1269784
  6.7 0.4 %stage.1 = (bf16[16,64,256]{2,1,0:T(8,128)(2,1)S(1)}, bf16[2480,256]{1,0:T(8,128)(2,1)S(1)}) custom-call(bf16[16,64,256]{2,1,0:T(8,128)(2,1)S(1)} %copy-done, bf16[2480,256]{1,0:T(8,128)(2,1)S(1)} %copy-done.1), custom_call_target="tpu_custom_call" | custom-call | bytes 3588096 | tf_op jit(solution)/shard_map/stage/pallas_call | solution.py:470
  7.1 0.0 collective-permute-done.refs_1_
  7.1 0.1 collective-permute-done.1.refs_2_
  7.2 0.7 %pack.1 = (bf16[16,32,256]{2,1,0:T(8,128)(2,1)S(1)}, bf16[3,32,256]{2,1,0:T(8,128)(2,1)S(1)}, bf16[16,32,128]{2,1,0:T(8,128)(2,1)S(1)}, bf16[16,16,128]{2,1,0:T(8,128)(2,1)S(1)}, bf16[3,16,128]{2,1,0:T(8,128)(2,1)S(1)}) custom-call(bf16[16,64,256]{2,1,0:T(8,128)(2,1)S(1)} %get-tuple-element.18.refs_0_, bf16[176,256]{1,0:T(8,128)(2,1)S(1)} %collective-permute-done.refs_1_, ...), custom_call_target="tpu_custom_call" | custom-call | bytes 2494464 | tf_op jit(solution)/shard_map/pack/pallas_call | solution.py:470
  7.8 1.6 %collective-permute-start.2 = (bf16[16,16,128]{2,1,0:T(8,128)(2,1)S(1)}, bf16[16,16,128]{2,1,0:T(8,128)(2,1)S(1)}, u32[]{:S(2)}, u32[]{:S(2)}) collective-permute-start(bf16[16,16,128]{2,1,0:T(8,128)(2,1)S(1)} %get-tuple-element.24), channel_id=1, source_target_pairs={{0,1},{1,0},{2,3},{3,2},{4,5},{5,4},{6,7},{7,6},{8,9},{9,8},{10,11... | collective-permute-start | bytes 196616 | tf_op jit(solution)/shard_map/ppermute | solution.py:533
  9.4 1.4 %collective-permute-start.5 = (bf16[3,16,128]{2,1,0:T(8,128)(2,1)S(1)}, bf16[3,16,128]{2,1,0:T(8,128)(2,1)S(1)}, u32[]{:S(2)}, u32[]{:S(2)}) collective-permute-start(bf16[3,16,128]{2,1,0:T(8,128)(2,1)S(1)} %get-tuple-element.27), channel_id=1, source_target_pairs={{0,17},{1,16},{16,1},{17,0},{2,19},{3,18},{18,3},{19,2},{4,21},{5,... | collective-permute-start | bytes 36872 | tf_op jit(solution)/shard_map/ppermute | solution.py:534
  10.9 0.5 %collective-permute-start.4 = (bf16[3,32,256]{2,1,0:T(8,128)(2,1)S(1)}, bf16[3,32,256]{2,1,0:T(8,128)(2,1)S(1)}, u32[]{:S(2)}, u32[]{:S(2)}) collective-permute-start(bf16[3,32,256]{2,1,0:T(8,128)(2,1)S(1)} %get-tuple-element.26), channel_id=1, source_target_pairs={{0,16},{16,0},{1,17},{17,1},{2,18},{18,2},{3,19},{19,3},{4,20},{20... | collective-permute-start | bytes 147464 | tf_op jit(solution)/shard_map/ppermute | solution.py:531
  11.4 1.6 %first.1.refs_7_.refs_4_ = f32[8,96,64]{2,1,0:T(8,128)S(1)} custom-call(bf16[16,64,256]{2,1,0:T(8,128)(2,1)S(1)} %get-tuple-element.18.refs_0_, bf16[16,32,256]{2,1,0:T(8,128)(2,1)S(1)} %get-tuple-element.22.refs_1_, bf16[2480,256]{1,0:T(8,128)(2,1)S(1)} %get-tuple-element.21.refs_3_.refs_2_.refs_8_.refs_7_), custom_call_target="tpu_custom_call" | custom-call | flops 559939584 | bytes 2252800 | tf_op jit(solution)/shard_map/first/pallas_call | solution.py:470
  13.0 0.0 collective-permute-done.3.refs_2_
  13.0 1.0 %collective-permute-done.5.refs_6_ = bf16[3,16,128]{2,1,0:T(8,128)(2,1)S(1)} collective-permute-done((bf16[3,16,128]{2,1,0:T(8,128)(2,1)S(1)}, bf16[3,16,128]{2,1,0:T(8,128)(2,1)S(1)}, u32[]{:S(2)}, u32[]{:S(2)}) %collective-permute-start.5) | collective-permute-done | bytes 12320 | tf_op jit(solution)/shard_map/ppermute | solution.py:534
  14.0 0.9 %collective-permute-done.4.refs_3_ = bf16[3,32,256]{2,1,0:T(8,128)(2,1)S(1)} collective-permute-done((bf16[3,32,256]{2,1,0:T(8,128)(2,1)S(1)}, bf16[3,32,256]{2,1,0:T(8,128)(2,1)S(1)}, u32[]{:S(2)}, u32[]{:S(2)}) %collective-permute-start.4) | collective-permute-done | bytes 49184 | tf_op jit(solution)/shard_map/ppermute | solution.py:531
  14.9 0.0 collective-permute-done.2.refs_5_.refs_3_
  14.9 1.7 %edge.1 = (f32[3,96,64]{2,1,0:T(8,128)S(1)}, f32[96,64]{1,0:T(8,128)S(1)}, bf16[96,128]{1,0:T(8,128)(2,1)S(1)}) custom-call(bf16[16,64,256]{2,1,0:T(8,128)(2,1)S(1)} %get-tuple-element.18.refs_0_, bf16[16,32,256]{2,1,0:T(8,128)(2,1)S(1)} %get-tuple-element.22.refs_1_, bf16[3,64,256]{2,1,0:T(8,128)(2,1)S(1)} %collective-permute-done.3.refs_2_, ...), custom_call_target="tpu_custom_call" | custom-call | flops 419954688 | bytes 2732032 | tf_op jit(solution)/shard_map/edge/pallas_call | solution.py:470
  16.6 0.8 %collective-permute-start.6 = (bf16[96,128]{1,0:T(8,128)(2,1)S(1)}, bf16[96,128]{1,0:T(8,128)(2,1)S(1)}, u32[]{:S(2)}, u32[]{:S(2)}) collective-permute-start(bf16[96,128]{1,0:T(8,128)(2,1)S(1)} %get-tuple-element.30), channel_id=1, source_target_pairs={{0,16},{16,0},{1,17},{17,1},{2,18},{18,2},{3,19},{19,3},{4,20},{20... | collective-permute-start | bytes 73736 | tf_op jit(solution)/shard_map/ppermute | solution.py:574
  17.4 2.0 %last.1.own = f32[6,4,16,64]{3,2,1,0:T(8,128)S(1)} custom-call(bf16[16,64,256]{2,1,0:T(8,128)(2,1)S(1)} %get-tuple-element.18.refs_0_, bf16[16,32,256]{2,1,0:T(8,128)(2,1)S(1)} %get-tuple-element.22.refs_1_, bf16[16,32,128]{2,1,0:T(8,128)(2,1)S(1)} %get-tuple-element.23.refs_4_.refs_2_, bf16[16,16,128]{2,1,0:T(8,128)(2,1)S(1)} %collective-permute-done.2.refs_5_.refs_3_, ...), custom_call_target="tpu_custom_call" | custom-call | flops 349962240 | bytes 2646016 | tf_op jit(solution)/shard_map/last/pallas_call | solution.py:470
  19.4 1.1 %collective-permute-done.6.got = bf16[96,128]{1,0:T(8,128)(2,1)S(1)} collective-permute-done((bf16[96,128]{1,0:T(8,128)(2,1)S(1)}, bf16[96,128]{1,0:T(8,128)(2,1)S(1)}, u32[]{:S(2)}, u32[]{:S(2)}) %collective-permute-start.6) | collective-permute-done | bytes 24608 | tf_op jit(solution)/shard_map/ppermute | solution.py:574
  20.5 0.8 %add.1 = f32[6,4,16,64]{3,2,1,0:T(8,128)} custom-call(f32[6,4,16,64]{3,2,1,0:T(8,128)S(1)} %last.1.own, bf16[96,128]{1,0:T(8,128)(2,1)S(1)} %collective-permute-done.6.got), custom_call_target="tpu_custom_call" | custom-call | bytes 221184 | tf_op jit(solution)/shard_map/add/pallas_call | solution.py:470
  (1 shorter events, 0.0 us)
Async XLA Ops:
  0.0 1.0 %copy-start = (bf16[16,64,256]{2,1,0:T(8,128)(2,1)S(1)}, bf16[16,64,256]{2,1,0:T(8,128)(2,1)}, u32[]{:S(2)}) copy-start(bf16[16,64,256]{2,1,0:T(8,128)(2,1)} %refs_0_.1) | copy-start | bytes 1572868
  1.3 5.8 %collective-permute-start = (bf16[176,256]{1,0:T(8,128)(2,1)S(1)}, bf16[176,256]{1,0:T(8,128)(2,1)S(1)}, u32[]{:S(2)}, u32[]{:S(2)}) collective-permute-start(bf16[176,256]{1,0:T(8,128)(2,1)S(1)} %get-tuple-element.19), channel_id=1, source_target_pairs={{0,2},{2,0},{4,6},{6,4},{8,10},{10,8},{12,14},{14,12},{1,3},{3,1},... | collective-permute-start | bytes 270344 | tf_op jit(solution)/shard_map/ppermute | solution.py:511
  1.3 5.8 %collective-permute-start.1 = (bf16[176,256]{1,0:T(8,128)(2,1)S(1)}, bf16[176,256]{1,0:T(8,128)(2,1)S(1)}, u32[]{:S(2)}, u32[]{:S(2)}) collective-permute-start(bf16[176,256]{1,0:T(8,128)(2,1)S(1)} %get-tuple-element.20), channel_id=1, source_target_pairs={{2,4},{6,8},{10,12},{4,2},{8,6},{12,10},{0,0},{14,14},{3,5},{7,9},... | collective-permute-start | bytes 270344 | tf_op jit(solution)/shard_map/ppermute | solution.py:510
  3.3 9.8 %collective-permute-start.3 = (bf16[3,64,256]{2,1,0:T(8,128)(2,1)S(1)}, bf16[3,64,256]{2,1,0:T(8,128)(2,1)S(1)}, u32[]{:S(2)}, u32[]{:S(2)}) collective-permute-start(bf16[3,64,256]{2,1,0:T(8,128)(2,1)S(1)} %get-tuple-element.25), channel_id=1, source_target_pairs={{0,16},{16,0},{1,17},{17,1},{2,18},{18,2},{3,19},{19,3},{4,20},{20... | collective-permute-start | bytes 294920 | tf_op jit(solution)/shard_map/ppermute | solution.py:513
  5.4 1.3 %copy-start.1 = (bf16[2480,256]{1,0:T(8,128)(2,1)S(1)}, bf16[2480,256]{1,0:T(8,128)(2,1)}, u32[]{:S(2)}) copy-start(bf16[2480,256]{1,0:T(8,128)(2,1)} %constant.2.clone.w) | copy-start | bytes 3809284
  7.8 7.1 %collective-permute-start.2 = (bf16[16,16,128]{2,1,0:T(8,128)(2,1)S(1)}, bf16[16,16,128]{2,1,0:T(8,128)(2,1)S(1)}, u32[]{:S(2)}, u32[]{:S(2)}) collective-permute-start(bf16[16,16,128]{2,1,0:T(8,128)(2,1)S(1)} %get-tuple-element.24), channel_id=1, source_target_pairs={{0,1},{1,0},{2,3},{3,2},{4,5},{5,4},{6,7},{7,6},{8,9},{9,8},{10,11... | collective-permute-start | bytes 196616 | tf_op jit(solution)/shard_map/ppermute | solution.py:533
  9.4 4.6 %collective-permute-start.5 = (bf16[3,16,128]{2,1,0:T(8,128)(2,1)S(1)}, bf16[3,16,128]{2,1,0:T(8,128)(2,1)S(1)}, u32[]{:S(2)}, u32[]{:S(2)}) collective-permute-start(bf16[3,16,128]{2,1,0:T(8,128)(2,1)S(1)} %get-tuple-element.27), channel_id=1, source_target_pairs={{0,17},{1,16},{16,1},{17,0},{2,19},{3,18},{18,3},{19,2},{4,21},{5,... | collective-permute-start | bytes 36872 | tf_op jit(solution)/shard_map/ppermute | solution.py:534
  10.9 4.1 %collective-permute-start.4 = (bf16[3,32,256]{2,1,0:T(8,128)(2,1)S(1)}, bf16[3,32,256]{2,1,0:T(8,128)(2,1)S(1)}, u32[]{:S(2)}, u32[]{:S(2)}) collective-permute-start(bf16[3,32,256]{2,1,0:T(8,128)(2,1)S(1)} %get-tuple-element.26), channel_id=1, source_target_pairs={{0,16},{16,0},{1,17},{17,1},{2,18},{18,2},{3,19},{19,3},{4,20},{20... | collective-permute-start | bytes 147464 | tf_op jit(solution)/shard_map/ppermute | solution.py:531
  16.6 3.9 %collective-permute-start.6 = (bf16[96,128]{1,0:T(8,128)(2,1)S(1)}, bf16[96,128]{1,0:T(8,128)(2,1)S(1)}, u32[]{:S(2)}, u32[]{:S(2)}) collective-permute-start(bf16[96,128]{1,0:T(8,128)(2,1)S(1)} %get-tuple-element.30), channel_id=1, source_target_pairs={{0,16},{16,0},{1,17},{17,1},{2,18},{18,2},{3,19},{19,3},{4,20},{20... | collective-permute-start | bytes 73736 | tf_op jit(solution)/shard_map/ppermute | solution.py:574
where the time goes:
time: 21.5 us; the launch traced here: 21.3 us
  starting transfers between devices  8.38 us (39%)
  Pallas kernels  7.35 us (34%)
  waiting for transfers between devices  3.15 us (15%)
  local copies, waits for them, and re-layouts  2.34 us (11%)
    pallas_call x7, Pallas kernels, call(): pl.pallas_call(body, out_shape=list(outs), in_specs=[source] * len(operan...  7.35 us
    unnamed x4, local copies, waits for them, and re-layouts  2.34 us
    ppermute x1, starting transfers between devices, per_device(): zown = lax.ppermute(zmsg, 'gz', swap)  2.09 us
    ppermute x1, starting transfers between devices, per_device(): r2 = lax.ppermute(s2, 'row', inner)  1.92 us
    ppermute x1, starting transfers between devices, per_device(): xh = [lax.ppermute(xmsgs[0], 'col', swap)]  1.58 us
    ppermute x1, starting transfers between devices, per_device(): lax.ppermute(zxmsgs[0], ('gz', 'col'), [(i, 3 - i) for i in range(4)])  1.44 us
    ppermute x1, waiting for transfers between devices, per_device(): got = lax.ppermute(send, 'gz', swap)  1.14 us
    ppermute x1, waiting for transfers between devices, per_device(): lax.ppermute(zxmsgs[0], ('gz', 'col'), [(i, 3 - i) for i in range(4)])  0.96 us
  transfers between devices with their start and end apart: 7, of which 4 were waited for; matrix products, arithmetic and copies ran while one was open for 0% of the time, Pallas kernels for 22%

commit v1 on v0

v1 whole, which is shorter than its diff:
```python
import jax
import jax.numpy as jnp
import ml_dtypes
import numpy as np
from jax import lax
from jax.experimental import pallas as pl
from jax.experimental.pallas import tpu as pltpu
from jax.sharding import PartitionSpec as P

R = 3
R2 = 8
HALO = 16
NEED = R + R2
EXTRA = 12
SLOTS = 32
NT = (((1,), (1,)), ((), ()))
F32 = jnp.float32
BF16 = jnp.bfloat16

pair_table = ((0, 0), (1, 1), (2, 2), (0, 1), (0, 2), (1, 2))


def gauss_taps(radius):
    offsets = np.arange(-radius, radius + 1).astype(np.float32)
    spread = np.float32(radius / 3.0)
    smooth = np.exp(-offsets * offsets / (np.float32(2.0) * spread * spread))
    smooth = smooth / np.sum(smooth)
    slopes = offsets * smooth
    slopes = slopes / np.sum(offsets * slopes)
    as_f32 = lambda t: t.astype(ml_dtypes.bfloat16).astype(np.float32)
    return as_f32(smooth), as_f32(slopes)


SMOOTH_D, SLOPE_D = gauss_taps(R)
SMOOTH_I, _ = gauss_taps(R2)


def band(taps, sources, targets):
    radius = len(taps) // 2
    gap = np.asarray(sources)[:, None] - np.asarray(targets)[None, :]
    return np.where(np.abs(gap) <= radius, taps[np.clip(gap + radius, 0, 2 * radius)], 0.0)


def weight_table(depth, rows, cols):
    ext = rows + 2 * HALO
    grad_rows = rows + 16
    far = 10**6
    y_in = np.arange(ext) - HALO
    y_out = np.arange(grad_rows) - R2
    smooth_y = band(SMOOTH_D, y_in, y_out).T
    slope_y = band(SLOPE_D, y_in, y_out).T
    zero = np.zeros_like(smooth_y)
    wy = np.block([[smooth_y, zero], [slope_y, zero], [zero, smooth_y]])
    order = np.concatenate([np.arange(rows), np.arange(HALO) - HALO, rows + np.arange(HALO)]) + HALO
    x_all = np.arange(cols)
    slot_in = np.full(SLOTS, far)
    slot_in[0:8] = cols + np.arange(8)
    slot_in[8:14] = np.arange(6)
    slot_in[14:20] = cols - 6 + np.arange(6)
    slot_in[21:32] = np.arange(-11, 0)
    slot_out = np.full(SLOTS, -far)
    slot_out[0:11] = np.arange(-8, 3)
    slot_out[11:19] = cols - 3 + np.arange(8)
    eye8 = np.eye(8)
    inner = np.where((x_all >= R) & (x_all < cols - R), x_all, far)
    quarter = cols // 4
    coarse_edge = np.full(8, 3 * far)
    coarse_edge[0:5] = [0, 1, 2, quarter - 2, quarter - 1]
    xs_edge = band(SMOOTH_I, slot_out, 4 * coarse_edge)
    ys = band(SMOOTH_I, y_out, 4 * np.arange(rows // 4)).T
    zs = band(SMOOTH_I, np.arange(depth), 4 * (np.arange(depth // 4 + 4) - 2))
    place = np.zeros((8, 128))
    for j in range(5):
        place[j, coarse_edge[j]] = 1.0
    own_z = 4 * np.arange(depth // 4)
    g = [
        np.einsum("zq,jx->zjqx", band(SMOOTH_I, np.arange(depth + 8) + first, own_z), place)
        for first in (0, -8)
    ]
    g = [t.reshape((depth + 8) * 8, len(own_z) * 128) for t in g]
    packed = np.arange(depth * NEED)
    above = np.zeros((depth * HALO, depth * NEED))
    above[packed + packed // NEED * (HALO - NEED) + HALO - NEED, packed] = 1.0
    below = np.zeros((depth * HALO, depth * NEED))
    below[packed + packed // NEED * (HALO - NEED), packed] = 1.0
    used = 2 * R + 13
    packed = np.arange(R * used)
    corner = np.zeros((64, R * 2 * HALO))
    corner[packed, packed + packed // used * (2 * HALO - used) + HALO - NEED] = 1.0
    parts = {
        "above": above,
        "below": below,
        "corner": corner,
        "corner_back": corner.T,
        "wy": wy,
        "wy_strip": np.concatenate([smooth_y, slope_y])[:, order],
        "wy_strip_slope": smooth_y[:, order],
        "wxd": band(SLOPE_D, x_all, x_all),
        "wxs": band(SMOOTH_D, x_all, x_all),
        "bdd": np.kron(eye8, band(SLOPE_D, slot_in, slot_out)),
        "bds": np.kron(eye8, band(SMOOTH_D, slot_in, slot_out)),
        "ysm": np.kron(np.eye(3), ys),
        "xsm": band(SMOOTH_I, inner, 4 * np.arange(quarter)),
        "bdx": np.kron(eye8, xs_edge),
        "g_low0": g[0][:, 0:256],
        "g_low1": g[0][:, 256:512],
        "g_high0": g[1][:, 0:256],
        "g_high1": g[1][:, 256:512],
    }
    place_of, blocks, at = {}, [], 0
    for name, part in parts.items():
        height = -(-part.shape[0] // 16) * 16
        block = np.zeros((height, 256), np.float32)
        block[: part.shape[0], : part.shape[1]] = part
        place_of[name] = (at, part.shape[0], part.shape[1])
        blocks.append(block)
        at += height
    return np.concatenate(blocks).astype(ml_dtypes.bfloat16), place_of, zs


def z_filter(v, count):
    for z in range(count):
        w = v[z : z + 7]
        smooth = w[3] * float(SMOOTH_D[3])
        slope = None
        for s in (1, 2, 3):
            smooth = smooth + (w[3 + s] + w[3 - s]) * float(SMOOTH_D[3 + s])
            term = (w[3 + s] - w[3 - s]) * float(SLOPE_D[3 + s])
            slope = term if slope is None else slope + term
        yield z, smooth.astype(BF16), slope.astype(BF16)


def getter(place_of, w):
    def get(name, width=None):
        at, height, own_width = place_of[name]
        return w[at : at + height, 0 : (width or own_width)]

    return get


def row_mask(get, n_row, rows, gr, quarter_rows):
    row = lax.axis_index("row")
    lane = lax.broadcasted_iota(jnp.int32, (3 * quarter_rows, 3 * gr), 1)
    y_out = lax.rem(lane, gr) - R2
    outside = ((row == 0) & (y_out < 0)) | ((row == n_row - 1) & (y_out >= rows))
    return jnp.where(outside, 0.0, get("ysm").astype(F32)).astype(BF16)


def layers_to_sums(get, ysm, load, count, shape, u_ref, zf, planes, prod, sm):
    rows, cols = shape
    ext = rows + 2 * HALO
    gr = rows + 16
    n_rows = 6 * (rows // 4)
    half_rows = n_rows // 2
    for tile in range(cols // 128):
        lanes = slice(tile * 128, tile * 128 + 128)
        for at in range(0, ext, 16):
            for z, smooth, slope in z_filter(load(at, lanes), count):
                zf[z, at : at + 16, lanes] = smooth
                zf[z, ext + at : ext + at + 16, lanes] = slope
    wy = get("wy")
    for z in range(count):
        out = jnp.dot(wy, zf[z], preferred_element_type=F32).astype(BF16)
        planes[0, z] = out[0:gr]
        planes[1, z] = out[gr : 2 * gr]
        planes[2, z] = out[2 * gr :]
    sides = []
    for first, n, name in ((0, 1, "wxd"), (1, 2, "wxs")):
        part = planes[first : first + n].reshape(n * count * gr, cols)
        out = jnp.dot(part, get(name), preferred_element_type=F32)
        sides.append(out.astype(BF16).reshape(n, count, gr, cols))
    grads = [sides[0][0], sides[1][0], sides[1][1]]
    for c, (a, b) in enumerate(pair_table):
        prod[:, c * gr : (c + 1) * gr] = grads[a] * grads[b]
    for z in range(count):
        for half in range(2):
            part = prod[z, half * 3 * gr : (half + 1) * 3 * gr]
            out = jnp.dot(ysm, part, preferred_element_type=F32)
            sm[z, half * half_rows : (half + 1) * half_rows] = out.astype(BF16)
    out = jnp.dot(
        sm[...].reshape(count * n_rows, cols), get("xsm"), preferred_element_type=F32
    )
    u_ref[...] = out.reshape(count, n_rows, cols // 4)


def block_loader(vol, yud, rows):
    def layer(z, at, lanes):
        if at < HALO:
            return yud[z, at : at + 16, lanes].astype(F32)
        if at < HALO + rows:
            return vol[z, at - HALO : at - HALO + 16, lanes].astype(F32)
        return yud[z, at - rows : at - rows + 16, lanes].astype(F32)

    return layer


def spread_rows(first):
    shape = (16 * NEED, 16 * HALO)
    packed = lax.broadcasted_iota(jnp.int32, shape, 0)
    full = lax.broadcasted_iota(jnp.int32, shape, 1)
    z = lax.shift_right_logical(packed * 373, 12)
    return jnp.where(full == packed + z * (HALO - NEED) + first, 1.0, 0.0).astype(BF16)


def load_kernel(vol, s1, s2):
    depth, rows, cols = vol.shape
    odd = lax.rem(lax.axis_index("row"), 2) == 1
    top = vol[:, 0:HALO, :].reshape(depth * HALO, cols)
    bottom = vol[:, rows - HALO : rows, :].reshape(depth * HALO, cols)
    to_before = jnp.dot(spread_rows(0), top, preferred_element_type=F32).astype(BF16)
    to_after = jnp.dot(
        spread_rows(HALO - NEED), bottom, preferred_element_type=F32
    ).astype(BF16)
    s1[...] = jnp.where(odd, to_before, to_after)
    s2[...] = jnp.where(odd, to_after, to_before)


def column_select(n_col, cols):
    n_side = 1 if n_col == 2 else 2
    shape = (SLOTS + 16 * n_side, cols)
    row = lax.broadcasted_iota(jnp.int32, shape, 0)
    lane = lax.broadcasted_iota(jnp.int32, shape, 1)
    picked = ((row >= 8) & (row < 14) & (lane == row - 8)) | (
        (row >= 14) & (row < 20) & (lane == row - 20 + cols)
    )
    for side in range(n_side):
        if n_col == 2:
            first = jnp.where(lax.axis_index("col") == 0, cols - HALO, 0)
        else:
            first = (cols - HALO, 0)[side]
        at = row - SLOTS - 16 * side
        picked = picked | ((at >= 0) & (at < 16) & (lane == at + first))
    return jnp.where(picked, 1.0, 0.0).astype(BF16)


def pick_columns(select, source):
    picked = lax.dot_general(select, source, NT, preferred_element_type=F32)
    messages = [picked[at : at + 16].astype(BF16) for at in range(SLOTS, picked.shape[0], 16)]
    return picked[0:SLOTS].astype(BF16), picked[8:24].astype(BF16), messages


def halve(chunk, at, value):
    n = value.shape[0]
    chunk[at : at + n] = value[:, 0:128]
    chunk[at + n : at + 2 * n] = value[:, 128:256]


def joined_halves(chunk, at, n):
    return jnp.concatenate([chunk[at : at + n], chunk[at + n : at + 2 * n]], axis=1)


def edges_kernel(n_col, vol, own, zmsg, *refs):
    depth, rows, cols = vol.shape
    gz = lax.axis_index("gz")
    select = column_select(n_col, cols)
    for b in range(depth // 2):
        source = vol[2 * b : 2 * b + 2].reshape(2 * rows, cols)
        slots, middle, messages = pick_columns(select, source)
        own[b] = slots
        for ref, message in zip(refs, [middle] + messages):
            ref[b] = message
    base = jnp.where(gz == 0, depth - R, 0)
    halve(zmsg, 0, vol[pl.ds(base, R)].reshape(R * rows, cols))
    first = jnp.where(gz == 0, (depth - EXTRA) // 2, 0)
    n = EXTRA // 2
    zmsg[2 * R * rows :] = refs[0][pl.ds(first, n)].reshape(n * 16, 128)


def pack_kernel(place_of, n_col, r1, r2, w, *refs):
    n_side = 1 if n_col == 2 else 2
    xown, (yud, halo, zcorner) = refs[:n_side], refs[n_side : n_side + 3]
    xmsgs, zxmsgs = refs[n_side + 3 : 2 * n_side + 3], refs[2 * n_side + 3 : 3 * n_side + 3]
    middles = refs[3 * n_side + 3]
    depth, cols = yud.shape[0], yud.shape[2]
    gz = lax.axis_index("gz")
    odd = lax.rem(lax.axis_index("row"), 2) == 1
    get = getter(place_of, w)
    got1, got2 = r1[...], r2[...]
    for at, name, part in (
        (0, "above", jnp.where(odd, got1, got2)),
        (HALO, "below", jnp.where(odd, got2, got1)),
    ):
        out = jnp.dot(get(name), part, preferred_element_type=F32).astype(BF16)
        yud[:, at : at + HALO, :] = out.reshape(depth, HALO, cols)
    select = column_select(n_col, cols)
    pairs, quads = depth // 2, depth // 4
    for b in range(quads):
        source = yud[4 * b : 4 * b + 4].reshape(4 * 2 * HALO, cols)
        slots, middle, messages = pick_columns(select, source)
        halo[b] = slots
        middles[b] = middle
        for ref, message in zip(xmsgs, messages):
            ref[pairs + b] = message
    for ref, part in zip(xmsgs, xown):
        ref[0:pairs] = part[...]
    base = jnp.where(gz == 0, depth - R, 0)
    edge = yud[pl.ds(base, R)].reshape(R * 2 * HALO, cols)
    halve(zcorner, 0, jnp.dot(get("corner"), edge, preferred_element_type=F32).astype(BF16))
    n2, n4 = EXTRA // 2, EXTRA // 4
    first2 = jnp.where(gz == 0, pairs - n2, 0)
    first4 = jnp.where(gz == 0, quads - n4, 0)
    zcorner[128:] = middles[pl.ds(first4, n4)].reshape(n4 * 16, 128)
    for ref, message in zip(zxmsgs, xmsgs):
        ref[0:n2] = message[pl.ds(first2, n2)]
        ref[n2:] = message[pl.ds(pairs + first4, n4)]


FIRST = 5
EDGE = R
LAST = 8


def first_kernel(place_of, n_row, vol, yud, w, u_ref, *scratch):
    depth, rows, cols = vol.shape
    get = getter(place_of, w)
    ysm = row_mask(get, n_row, rows, rows + 16, rows // 4)
    base = jnp.where(lax.axis_index("gz") == 0, depth - EDGE - FIRST - R, 0)
    layer = block_loader(vol, yud, rows)
    load = lambda at, lanes: [layer(base + k, at, lanes) for k in range(FIRST + 2 * R)]
    layers_to_sums(get, ysm, load, FIRST, (rows, cols), u_ref, *scratch)


def near_kernel(place_of, zs, n_row, vol, yud, zown, zcorner, u1, w, u_ref, send_ref, zext, *scratch):
    depth, rows, cols = vol.shape
    n_zq = zs.shape[1]
    get = getter(place_of, w)
    low = lax.axis_index("gz") == 0
    ysm = row_mask(get, n_row, rows, rows + 16, rows // 4)
    corner = jnp.dot(
        get("corner_back"), joined_halves(zcorner, 0, 64), preferred_element_type=F32
    ).astype(BF16).reshape(R, 2 * HALO, cols)
    zext[:, 0:HALO] = corner[:, 0:HALO]
    zext[:, HALO : HALO + rows] = joined_halves(zown, 0, R * rows).reshape(R, rows, cols)
    zext[:, HALO + rows :] = corner[:, HALO:]
    layer = block_loader(vol, yud, rows)
    start = jnp.where(low, depth - R, 0)
    outer = jnp.where(low, depth - 2 * R, R)

    def load(at, lanes):
        beyond = [zext[k, at : at + 16, lanes].astype(F32) for k in range(R)]
        inner = [layer(outer + k, at, lanes) for k in range(R)]
        middle = [layer(start + k, at, lanes) for k in range(R)]
        before = [jnp.where(low, inner[k], beyond[k]) for k in range(R)]
        after = [jnp.where(low, beyond[k], inner[k]) for k in range(R)]
        return before + middle + after

    layers_to_sums(get, ysm, load, EDGE, (rows, cols), u_ref, *scratch)
    sends = []
    for k in range(2):
        total = None
        for i in range(FIRST + EDGE):
            from_low = depth - EDGE - FIRST + i
            from_high = EDGE + i if i < FIRST else i - FIRST
            a = float(zs[from_low, n_zq - 2 + k])
            b = float(zs[from_high, k])
            if a == 0.0 and b == 0.0:
                continue
            term = (u1[i] if i < FIRST else u_ref[i - FIRST]) * jnp.where(low, a, b)
            total = term if total is None else total + term
        sends.append(total)
    send_ref[...] = jnp.concatenate(sends, axis=1).astype(BF16)


def last_layers(place_of, get, ysm, vol, yud, u_ref, *scratch):
    depth, rows, cols = vol.shape
    low = lax.axis_index("gz") == 0
    layer = block_loader(vol, yud, rows)
    base = jnp.where(low, -R, depth - LAST - R)
    before_on = jnp.where(low, 0.0, 1.0)
    after_on = jnp.where(low, 1.0, 0.0)

    def load(at, lanes):
        out = []
        for k in range(LAST + 2 * R):
            block = layer(jnp.clip(base + k, 0, depth - 1), at, lanes)
            if k < R:
                block = block * before_on
            elif k >= LAST + R:
                block = block * after_on
            out.append(block)
        return out

    layers_to_sums(get, ysm, load, LAST, (rows, cols), u_ref, *scratch)


def last_kernel(place_of, zs, n_row, n_col, vol, yud, own, halo, zown, zcorner, u1, u2, w,
                xs, zxs, own_ref, hs, hd, pstrip, u3, *scratch):
    depth, rows, cols = vol.shape
    gr = rows + 16
    quarter_rows, quarter = rows // 4, cols // 4
    get = getter(place_of, w)
    gz, col = lax.axis_index("gz"), lax.axis_index("col")
    low = gz == 0
    ysm = row_mask(get, n_row, rows, gr, quarter_rows)
    last_layers(place_of, get, ysm, vol, yud, u3, *scratch)
    slots = lax.broadcasted_iota(jnp.int32, (SLOTS, 128), 0)
    if n_col == 2:
        keep = ((slots < 8) & (col == 0)) | ((slots >= 21) & (col == 1))
    else:
        keep = (slots < 8) | (slots >= 21)

    def join(part, messages, b):
        sides = [messages[-1][b].astype(F32), messages[0][b].astype(F32)]
        return jnp.where(keep, jnp.concatenate(sides, axis=0), part)

    def from_middle(ref, at, b):
        rim = jnp.zeros((8, 128), F32)
        middle = ref[at + 16 * b : at + 16 * (b + 1)].astype(F32)
        return jnp.concatenate([rim, middle, rim], axis=0)

    lanes = lax.broadcasted_iota(jnp.int32, (SLOTS, 128), 1)

    def layers_of(pairs, quads):
        out = []
        for z in range(2 * len(pairs)):
            left, right = pairs[z // 2], quads[z // 4]
            if z % 2:
                left = pltpu.roll(left, 64, 1)
            turn = (rows - 32 * (z % 4)) % 128
            if turn:
                right = pltpu.roll(right, turn, 1)
            out.append(jnp.where(lanes < rows, left, right))
        return out

    n2, n4 = EXTRA // 2, EXTRA // 4
    own_layers = layers_of(
        [join(own[b].astype(F32), xs, b) for b in range(depth // 2)],
        [join(halo[b].astype(F32), xs, depth // 2 + b) for b in range(depth // 4)],
    )
    at = 2 * R * rows
    beyond = layers_of(
        [join(from_middle(zown, at, b), zxs, b) for b in range(n2)],
        [join(from_middle(zcorner, 128, b), zxs, n2 + b) for b in range(n4)],
    )
    count = depth + 8
    zero = [jnp.zeros((SLOTS, 128), F32)] * R
    at_low = zero + own_layers + beyond[0:11]
    at_high = beyond[1:12] + own_layers + zero
    layers = [jnp.where(low, a, b) for a, b in zip(at_low, at_high)]
    for z, smooth, slope in z_filter(layers, count):
        hs[SLOTS * z : SLOTS * (z + 1)] = smooth
        hd[SLOTS * z : SLOTS * (z + 1)] = slope
    p01 = lax.dot_general(
        get("wy_strip", 128), hs[...], NT, preferred_element_type=F32
    ).astype(BF16)
    p2 = lax.dot_general(
        get("wy_strip_slope", 128), hd[...], NT, preferred_element_type=F32
    ).astype(BF16)
    n = count // 8
    groups = [slice(256 * c, 256 * (c + 1)) for c in range(n)]
    stacks = [
        jnp.concatenate([p[:, g] for g in groups], axis=0) for p in (p01[0:gr], p01[gr:], p2)
    ]
    grads = [
        jnp.dot(stack, get(name), preferred_element_type=F32).astype(BF16).reshape(n, gr, 256)
        for stack, name in zip(stacks, ("bdd", "bds", "bds"))
    ]
    for c, (a, b) in enumerate(pair_table):
        pstrip[:, c * gr : (c + 1) * gr] = grads[a] * grads[b]
    slot = lax.rem(lax.broadcasted_iota(jnp.int32, (3 * quarter_rows, 256), 1), SLOTS)
    outside_x = ((col == 0) & (slot < 8)) | ((col == n_col - 1) & (slot >= 14))
    smoothed = []
    for c in range(n):
        for half in range(2):
            part = pstrip[c, half * 3 * gr : (half + 1) * 3 * gr]
            out = jnp.dot(ysm, part, preferred_element_type=F32)
            smoothed.append(jnp.where(outside_x, 0.0, out).astype(BF16))
    u = jnp.dot(jnp.concatenate(smoothed, axis=0), get("bdx"), preferred_element_type=F32)
    n_rows = 6 * quarter_rows
    u = u.astype(BF16)
    sums = []
    for name in ("0", "1"):
        at = jnp.where(low, place_of["g_low" + name][0], place_of["g_high" + name][0])
        total = None
        for c in range(n):
            g = w[pl.ds(pl.multiple_of(at + 64 * c, 16), 64), :]
            term = jnp.dot(u[n_rows * c : n_rows * (c + 1)], g, preferred_element_type=F32)
            total = term if total is None else total + term
        sums += [total[:, 0:quarter], total[:, 128 : 128 + quarter]]
    for q in range(depth // 4):
        total = sums[q]
        for i in range(depth):
            if i < FIRST:
                u, from_low, from_high = u1[i], depth - EDGE - FIRST + i, EDGE + i
            elif i < FIRST + EDGE:
                k = i - FIRST
                u, from_low, from_high = u2[k], depth - EDGE + k, k
            else:
                k = i - FIRST - EDGE
                u, from_low, from_high = u3[k], k, depth - LAST + k
            a, b = float(zs[from_low, q + 2]), float(zs[from_high, q + 2])
            if a == 0.0 and b == 0.0:
                continue
            total = total + u * jnp.where(low, a, b)
        own_ref[:, q] = total.reshape(6, quarter_rows, quarter)


def add_kernel(own, got, out):
    n_q, quarter = own.shape[1], own.shape[3]
    low = lax.axis_index("gz") == 0
    parts = [
        got[:, k * quarter : (k + 1) * quarter].astype(F32).reshape(own.shape[0], -1, quarter)
        for k in range(2)
    ]
    for q in range(n_q):
        total = own[:, q]
        if q < 2:
            total = total + parts[q] * jnp.where(low, 0.0, 1.0)
        if q >= n_q - 2:
            total = total + parts[q - n_q + 2] * jnp.where(low, 1.0, 0.0)
        out[:, q] = total


def call(body, outs, operands, scratch, name, flops=0):
    vmem = pl.BlockSpec(memory_space=pltpu.VMEM)
    moved = sum(o.size * o.dtype.itemsize for o in list(outs) + list(operands))
    return pl.pallas_call(
        body,
        out_shape=list(outs),
        in_specs=[vmem] * len(operands),
        out_specs=[vmem] * len(outs),
        scratch_shapes=scratch,
        compiler_params=pltpu.CompilerParams(vmem_limit_bytes=24 * 2**20),
        cost_estimate=pl.CostEstimate(flops=flops, bytes_accessed=moved, transcendentals=0),
        name=name,
    )(*operands)


def per_device(volume):
    depth, rows, cols = volume.shape
    n_row, n_col = lax.axis_size("row"), lax.axis_size("col")
    table, place_of, zs = weight_table(depth, rows, cols)
    ext = rows + 2 * HALO
    gr = rows + 16
    quarter_rows, quarter = rows // 4, cols // 4
    n_rows = 6 * quarter_rows
    n_side = 1 if n_col == 2 else 2
    pairs, quads = depth // 2, depth // 4
    n2, n4 = EXTRA // 2, EXTRA // 4
    sds = jax.ShapeDtypeStruct
    bf16 = lambda *shape: sds(shape, BF16)

    def scratch_for(count):
        return [
            pltpu.VMEM((count, 2 * ext, cols), BF16),
            pltpu.VMEM((3, count, gr, cols), BF16),
            pltpu.VMEM((count, 6 * gr, cols), BF16),
            pltpu.VMEM((count, n_rows, cols), BF16),
        ]

    layer_flops = 2 * cols * (3 * gr * 2 * ext + 3 * gr * cols + n_rows * 3 * gr + n_rows * quarter)

    s1, s2 = call(load_kernel, [bf16(depth * NEED, cols)] * 2, [volume], [], "load")
    inner = [(i, i + 1) for i in range(1, n_row - 1, 2)]
    inner = inner + [(j, i) for i, j in inner]
    r2 = lax.ppermute(s2, "row", inner)
    r1 = lax.ppermute(s1, "row", [(i, i ^ 1) for i in range(n_row)])
    vol, w = volume, jnp.asarray(table)
    own, zmsg, _, *xown = call(
        lambda *refs: edges_kernel(n_col, *refs),
        [bf16(pairs, SLOTS, 128), bf16(2 * R * rows + n2 * 16, 128)]
        + [bf16(pairs, HALO, 128)] * (n_side + 1),
        [volume], [], "edges",
    )
    swap = [(0, 1), (1, 0)]
    zown = lax.ppermute(zmsg, "gz", swap)

    yud, halo, zcmsg, *messages = call(
        lambda *refs: pack_kernel(place_of, n_col, *refs),
        [bf16(depth, 2 * HALO, cols), bf16(quads, SLOTS, 128), bf16(128 + n4 * 16, 128)]
        + [bf16(pairs + quads, HALO, 128)] * n_side
        + [bf16(n2 + n4, HALO, 128)] * n_side,
        [r1, r2, w] + xown, [pltpu.VMEM((quads, 16, 128), BF16)], "pack",
    )
    zcorner = lax.ppermute(zcmsg, "gz", swap)
    xs, zxs = [], []
    for side in range(n_side):
        step = 1 - 2 * side
        line = swap if n_col == 2 else [
            (i, i + step) for i in range(n_col) if 0 <= i + step < n_col
        ]
        both = [(z * n_col + i, (1 - z) * n_col + j) for z in range(2) for i, j in line]
        xs.append(lax.ppermute(messages[side], "col", line))
        zxs.append(lax.ppermute(messages[n_side + side], ("gz", "col"), both))

    (u1,) = call(
        lambda *refs: first_kernel(place_of, n_row, *refs),
        [sds((FIRST, n_rows, quarter), F32)],
        [vol, yud, w], scratch_for(FIRST), "first", flops=FIRST * layer_flops,
    )
    u2, send = call(
        lambda *refs: near_kernel(place_of, zs, n_row, *refs),
        [sds((EDGE, n_rows, quarter), F32), bf16(n_rows, 2 * quarter)],
        [vol, yud, zown, zcorner, u1, w],
        [pltpu.VMEM((R, ext, cols), BF16)] + scratch_for(EDGE),
        "near", flops=EDGE * layer_flops,
    )
    sums = lax.ppermute(send, "gz", swap)

    def last_body(*refs):
        head, x_refs, zx_refs = refs[0:9], refs[9 : 9 + n_side], refs[9 + n_side : 9 + 2 * n_side]
        last_kernel(
            place_of, zs, n_row, n_col, *head, x_refs, zx_refs, *refs[9 + 2 * n_side :]
        )

    count = depth + 8
    (result,) = call(
        last_body,
        [sds((6, depth // 4, quarter_rows, quarter), F32)],
        [vol, yud, own, halo, zown, zcorner, u1, u2, w] + xs + zxs,
        [
            pltpu.VMEM((count * SLOTS, 128), BF16),
            pltpu.VMEM((count * SLOTS, 128), BF16),
            pltpu.VMEM((count // 8, 6 * gr, 256), BF16),
            pltpu.VMEM((LAST, n_rows, quarter), F32),
        ]
        + scratch_for(LAST),
        "last", flops=(LAST + 3) * layer_flops,
    )
    (out,) = call(add_kernel, [sds(result.shape, F32)], [result, sums], [], "add")
    return out


def solution(mesh):
    return jax.shard_map(
        per_device,
        mesh=mesh,
        in_specs=(P("gz", "row", "col"),),
        out_specs=P(None, "gz", "row", "col"),
        check_vma=False,
    )
```

time: 21.5 us -> 21 us (0.977)
  the two profiles are of different devices: /device:TPU:8 before, /device:TPU:1 now
where the time goes in v1:
time: 21 us; the launch traced here: 20.8 us
  starting transfers between devices  10.4 us (50%)
  Pallas kernels  7.52 us (36%)
  local copies, waits for them, and re-layouts  2.53 us (12%)
  waiting for transfers between devices  0.33 us (2%)
    pallas_call x7, Pallas kernels, call(): pl.pallas_call(body, out_shape=list(outs), in_specs=[vmem] * len(operands...  7.52 us
    ppermute x1, starting transfers between devices, per_device(): r2 = lax.ppermute(s2, 'row', inner)  4.54 us
    unnamed x8, local copies, waits for them, and re-layouts  2.53 us
    ppermute x1, starting transfers between devices, per_device(): zcorner = lax.ppermute(zcmsg, 'gz', swap)  1.8 us
    ppermute x1, starting transfers between devices, per_device(): sums = lax.ppermute(send, 'gz', swap)  1.44 us
    ppermute x1, starting transfers between devices, per_device(): zown = lax.ppermute(zmsg, 'gz', swap)  1.22 us
    ppermute x1, starting transfers between devices, per_device(): zxs.append(lax.ppermute(messages[n_side + side], ('gz', 'col'), both))  1.22 us
  transfers between devices with their start and end apart: 7, of which 1 were waited for; matrix products, arithmetic and copies ran while one was open for 0% of the time, Pallas kernels for 31%

profile of v1, /device:TPU:1, one launch (start us, length us, event | category | flops | bytes accessed | tf_op | source)
XLA Modules:
  0.0 20.8 jit_solution(18054029312362138232)
XLA Ops:
  0.0 1.0 %copy-done.2 = bf16[16,64,256]{2,1,0:T(8,128)(2,1)S(1)} copy-done((bf16[16,64,256]{2,1,0:T(8,128)(2,1)S(1)}, bf16[16,64,256]{2,1,0:T(8,128)(2,1)}, u32[]{:S(2)}) %copy-start.2) | copy-done | bytes 524312
  1.0 0.2 load.1
  1.3 0.1 collective-permute-start
  1.4 4.5 %collective-permute-start.1 = (bf16[176,256]{1,0:T(8,128)(2,1)S(1)}, bf16[176,256]{1,0:T(8,128)(2,1)S(1)}, u32[]{:S(2)}, u32[]{:S(2)}) collective-permute-start(bf16[176,256]{1,0:T(8,128)(2,1)S(1)} %get-tuple-element.18), channel_id=1, source_target_pairs={{2,4},{6,8},{10,12},{4,2},{8,6},{12,10},{3,5},{7,9},{11,13},{5,3},... | collective-permute-start | bytes 270344 | tf_op jit(solution)/shard_map/ppermute | solution.py:556
  5.9 0.9 %edges.1 = (bf16[8,32,128]{2,1,0:T(8,128)(2,1)S(1)}, bf16[480,128]{1,0:T(8,128)(2,1)S(1)}, bf16[8,16,128]{2,1,0:T(8,128)(2,1)}, bf16[8,16,128]{2,1,0:T(8,128)(2,1)S(1)}) custom-call(bf16[16,64,256]{2,1,0:T(8,128)(2,1)S(1)} %copy-done.2), custom_call_target="tpu_custom_call" | custom-call | bytes 778240 | tf_op jit(solution)/shard_map/edges/pallas_call | solution.py:517
  6.8 1.2 %collective-permute-start.2 = (bf16[480,128]{1,0:T(8,128)(2,1)S(1)}, bf16[480,128]{1,0:T(8,128)(2,1)S(1)}, u32[]{:S(2)}, u32[]{:S(2)}) collective-permute-start(bf16[480,128]{1,0:T(8,128)(2,1)S(1)} %get-tuple-element.23), channel_id=1, source_target_pairs={{0,16},{16,0},{1,17},{17,1},{2,18},{18,2},{3,19},{19,3},{4,20},{20... | collective-permute-start | bytes 368648 | tf_op jit(solution)/shard_map/ppermute | solution.py:566
  8.1 0.0 collective-permute-done.refs_0_
  8.1 0.3 %collective-permute-done.1.refs_1_ = bf16[176,256]{1,0:T(8,128)(2,1)S(1)} collective-permute-done((bf16[176,256]{1,0:T(8,128)(2,1)S(1)}, bf16[176,256]{1,0:T(8,128)(2,1)S(1)}, u32[]{:S(2)}, u32[]{:S(2)}) %collective-permute-start.1) | collective-permute-done | bytes 90144 | tf_op jit(solution)/shard_map/ppermute | solution.py:556
  8.4 1.5 %copy-done = bf16[3504,256]{1,0:T(8,128)(2,1)S(1)} copy-done((bf16[3504,256]{1,0:T(8,128)(2,1)S(1)}, bf16[3504,256]{1,0:T(8,128)(2,1)}, u32[]{:S(2)}) %copy-start) | copy-done | bytes 1794072
  9.9 0.4 %pack.1 = (bf16[16,32,256]{2,1,0:T(8,128)(2,1)S(1)}, bf16[4,32,128]{2,1,0:T(8,128)(2,1)S(1)}, bf16[176,128]{1,0:T(8,128)(2,1)S(1)}, bf16[12,16,128]{2,1,0:T(8,128)(2,1)S(1)}, bf16[9,16,128]{2,1,0:T(8,128)(2,1)S(1)}) custom-call(bf16[176,256]{1,0:T(8,128)(2,1)S(1)} %collective-permute-done.refs_0_, bf16[176,256]{1,0:T(8,128)(2,1)S(1)} %collective-permute-done.1.refs_1_, ...), custom_call_target="tpu_custom_call" | custom-call | bytes 2433024 | tf_op jit(solution)/shard_map/pack/pallas_call | solution.py:517
  10.3 1.8 %collective-permute-start.3 = (bf16[176,128]{1,0:T(8,128)(2,1)S(1)}, bf16[176,128]{1,0:T(8,128)(2,1)S(1)}, u32[]{:S(2)}, u32[]{:S(2)}) collective-permute-start(bf16[176,128]{1,0:T(8,128)(2,1)S(1)} %get-tuple-element.24), channel_id=1, source_target_pairs={{0,16},{16,0},{1,17},{17,1},{2,18},{18,2},{3,19},{19,3},{4,20},{20... | collective-permute-start | bytes 135176 | tf_op jit(solution)/shard_map/ppermute | solution.py:575
  12.1 1.2 %collective-permute-start.5 = (bf16[9,16,128]{2,1,0:T(8,128)(2,1)S(1)}, bf16[9,16,128]{2,1,0:T(8,128)(2,1)S(1)}, u32[]{:S(2)}, u32[]{:S(2)}) collective-permute-start(bf16[9,16,128]{2,1,0:T(8,128)(2,1)S(1)} %get-tuple-element.27), channel_id=1, source_target_pairs={{0,17},{1,16},{16,1},{17,0},{2,19},{3,18},{18,3},{19,2},{4,21},{5,... | collective-permute-start | bytes 110600 | tf_op jit(solution)/shard_map/ppermute | solution.py:584
  13.3 0.0 collective-permute-start.4
  13.3 0.0 copy-done.3
  13.3 1.3 %first.1.refs_4_.refs_6_ = f32[5,96,64]{2,1,0:T(8,128)S(1)} custom-call(bf16[16,64,256]{2,1,0:T(8,128)(2,1)S(1)} %copy-done.3, bf16[16,32,256]{2,1,0:T(8,128)(2,1)S(1)} %get-tuple-element.20.refs_1_, bf16[3504,256]{1,0:T(8,128)(2,1)S(1)} %copy-done.1), custom_call_target="tpu_custom_call" | custom-call | flops 349962240 | bytes 2703360 | tf_op jit(solution)/shard_map/first/pallas_call | solution.py:517
  14.6 0.0 collective-permute-done.2.refs_2_.refs_4_
  14.6 0.0 collective-permute-done.3.refs_3_.refs_5_
  14.6 1.2 %near.1 = (f32[3,96,64]{2,1,0:T(8,128)S(1)}, bf16[96,128]{1,0:T(8,128)(2,1)S(1)}) custom-call(bf16[16,64,256]{2,1,0:T(8,128)(2,1)S(1)} %copy-done.3, bf16[16,32,256]{2,1,0:T(8,128)(2,1)S(1)} %get-tuple-element.20.refs_1_, bf16[480,128]{1,0:T(8,128)(2,1)S(1)} %collective-permute-done.2.refs_2_.refs_4_, ...), custom_call_target="tpu_custom_call" | custom-call | flops 209977344 | bytes 2969600 | tf_op jit(solution)/shard_map/near/pallas_call | solution.py:517
  15.9 1.4 %collective-permute-start.6 = (bf16[96,128]{1,0:T(8,128)(2,1)S(1)}, bf16[96,128]{1,0:T(8,128)(2,1)S(1)}, u32[]{:S(2)}, u32[]{:S(2)}) collective-permute-start(bf16[96,128]{1,0:T(8,128)(2,1)S(1)} %get-tuple-element.28), channel_id=1, source_target_pairs={{0,16},{16,0},{1,17},{17,1},{2,18},{18,2},{3,19},{19,3},{4,20},{20... | collective-permute-start | bytes 73736 | tf_op jit(solution)/shard_map/ppermute | solution.py:598
  17.3 0.0 collective-permute-done.5.refs_10_
  17.3 0.0 collective-permute-done.4.refs_9_
  17.3 2.7 %last.1.own = f32[6,4,16,64]{3,2,1,0:T(8,128)S(1)} custom-call(bf16[16,64,256]{2,1,0:T(8,128)(2,1)S(1)} %copy-done.3, bf16[16,32,256]{2,1,0:T(8,128)(2,1)S(1)} %get-tuple-element.20.refs_1_, bf16[8,32,128]{2,1,0:T(8,128)(2,1)S(1)} %get-tuple-element.21.refs_2_, bf16[4,32,128]{2,1,0:T(8,128)(2,1)S(1)} %get-tuple-element.22.refs_3_, ...), custom_call_target="tpu_custom_call" | custom-call | flops 769916928 | bytes 3227648 | tf_op jit(solution)/shard_map/last/pallas_call | solution.py:517
  20.0 0.0 collective-permute-done.6.got
  20.1 0.8 %add.1 = f32[6,4,16,64]{3,2,1,0:T(8,128)} custom-call(f32[6,4,16,64]{3,2,1,0:T(8,128)S(1)} %last.1.own, bf16[96,128]{1,0:T(8,128)(2,1)S(1)} %collective-permute-done.6.got), custom_call_target="tpu_custom_call" | custom-call | bytes 221184 | tf_op jit(solution)/shard_map/add/pallas_call | solution.py:517
  (5 shorter events, 0.0 us)
Async XLA Ops:
  0.0 1.0 %copy-start.2 = (bf16[16,64,256]{2,1,0:T(8,128)(2,1)S(1)}, bf16[16,64,256]{2,1,0:T(8,128)(2,1)}, u32[]{:S(2)}) copy-start(bf16[16,64,256]{2,1,0:T(8,128)(2,1)} %refs_0_.7) | copy-start | bytes 1572868
  1.0 12.3 %copy-start.3 = (bf16[16,64,256]{2,1,0:T(8,128)(2,1)S(1)}, bf16[16,64,256]{2,1,0:T(8,128)(2,1)}, u32[]{:S(2)}) copy-start(bf16[16,64,256]{2,1,0:T(8,128)(2,1)} %refs_0_.7) | copy-start | bytes 1572868
  1.3 6.8 %collective-permute-start = (bf16[176,256]{1,0:T(8,128)(2,1)S(1)}, bf16[176,256]{1,0:T(8,128)(2,1)S(1)}, u32[]{:S(2)}, u32[]{:S(2)}) collective-permute-start(bf16[176,256]{1,0:T(8,128)(2,1)S(1)} %get-tuple-element.17), channel_id=1, source_target_pairs={{0,2},{2,0},{4,6},{6,4},{8,10},{10,8},{12,14},{14,12},{1,3},{3,1},... | collective-permute-start | bytes 270344 | tf_op jit(solution)/shard_map/ppermute | solution.py:557
  1.4 7.0 %collective-permute-start.1 = (bf16[176,256]{1,0:T(8,128)(2,1)S(1)}, bf16[176,256]{1,0:T(8,128)(2,1)S(1)}, u32[]{:S(2)}, u32[]{:S(2)}) collective-permute-start(bf16[176,256]{1,0:T(8,128)(2,1)S(1)} %get-tuple-element.18), channel_id=1, source_target_pairs={{2,4},{6,8},{10,12},{4,2},{8,6},{12,10},{3,5},{7,9},{11,13},{5,3},... | collective-permute-start | bytes 270344 | tf_op jit(solution)/shard_map/ppermute | solution.py:556
  6.8 7.8 %collective-permute-start.2 = (bf16[480,128]{1,0:T(8,128)(2,1)S(1)}, bf16[480,128]{1,0:T(8,128)(2,1)S(1)}, u32[]{:S(2)}, u32[]{:S(2)}) collective-permute-start(bf16[480,128]{1,0:T(8,128)(2,1)S(1)} %get-tuple-element.23), channel_id=1, source_target_pairs={{0,16},{16,0},{1,17},{17,1},{2,18},{18,2},{3,19},{19,3},{4,20},{20... | collective-permute-start | bytes 368648 | tf_op jit(solution)/shard_map/ppermute | solution.py:566
  8.4 1.5 %copy-start = (bf16[3504,256]{1,0:T(8,128)(2,1)S(1)}, bf16[3504,256]{1,0:T(8,128)(2,1)}, u32[]{:S(2)}) copy-start(bf16[3504,256]{1,0:T(8,128)(2,1)} %constant.2.clone.refs_2_.refs_5_.refs_8_) | copy-start | bytes 5382148
  9.9 3.5 %copy-start.1 = (bf16[3504,256]{1,0:T(8,128)(2,1)S(1)}, bf16[3504,256]{1,0:T(8,128)(2,1)}, u32[]{:S(2)}) copy-start(bf16[3504,256]{1,0:T(8,128)(2,1)} %constant.2.clone.refs_2_.refs_5_.refs_8_) | copy-start | bytes 5382148
  10.3 4.4 %collective-permute-start.3 = (bf16[176,128]{1,0:T(8,128)(2,1)S(1)}, bf16[176,128]{1,0:T(8,128)(2,1)S(1)}, u32[]{:S(2)}, u32[]{:S(2)}) collective-permute-start(bf16[176,128]{1,0:T(8,128)(2,1)S(1)} %get-tuple-element.24), channel_id=1, source_target_pairs={{0,16},{16,0},{1,17},{17,1},{2,18},{18,2},{3,19},{19,3},{4,20},{20... | collective-permute-start | bytes 135176 | tf_op jit(solution)/shard_map/ppermute | solution.py:575
  12.1 5.2 %collective-permute-start.5 = (bf16[9,16,128]{2,1,0:T(8,128)(2,1)S(1)}, bf16[9,16,128]{2,1,0:T(8,128)(2,1)S(1)}, u32[]{:S(2)}, u32[]{:S(2)}) collective-permute-start(bf16[9,16,128]{2,1,0:T(8,128)(2,1)S(1)} %get-tuple-element.27), channel_id=1, source_target_pairs={{0,17},{1,16},{16,1},{17,0},{2,19},{3,18},{18,3},{19,2},{4,21},{5,... | collective-permute-start | bytes 110600 | tf_op jit(solution)/shard_map/ppermute | solution.py:584
  13.3 4.0 %collective-permute-start.4 = (bf16[12,16,128]{2,1,0:T(8,128)(2,1)S(1)}, bf16[12,16,128]{2,1,0:T(8,128)(2,1)S(1)}, u32[]{:S(2)}, u32[]{:S(2)}) collective-permute-start(bf16[12,16,128]{2,1,0:T(8,128)(2,1)S(1)} %get-tuple-element.26), channel_id=1, source_target_pairs={{0,1},{1,0},{2,3},{3,2},{4,5},{5,4},{6,7},{7,6},{8,9},{9,8},{10,11... | collective-permute-start | bytes 147464 | tf_op jit(solution)/shard_map/ppermute | solution.py:583
  15.9 4.2 %collective-permute-start.6 = (bf16[96,128]{1,0:T(8,128)(2,1)S(1)}, bf16[96,128]{1,0:T(8,128)(2,1)S(1)}, u32[]{:S(2)}, u32[]{:S(2)}) collective-permute-start(bf16[96,128]{1,0:T(8,128)(2,1)S(1)} %get-tuple-element.28), channel_id=1, source_target_pairs={{0,16},{16,0},{1,17},{17,1},{2,18},{18,2},{3,19},{19,3},{4,20},{20... | collective-permute-start | bytes 73736 | tf_op jit(solution)/shard_map/ppermute | solution.py:598

commit v2 on v1

--- a/solution.py
+++ b/solution.py
@@ -164,14 +164,15 @@
         planes[0, z] = out[0:gr]
         planes[1, z] = out[gr : 2 * gr]
         planes[2, z] = out[2 * gr :]
-    sides = []
-    for first, n, name in ((0, 1, "wxd"), (1, 2, "wxs")):
-        part = planes[first : first + n].reshape(n * count * gr, cols)
-        out = jnp.dot(part, get(name), preferred_element_type=F32)
-        sides.append(out.astype(BF16).reshape(n, count, gr, cols))
-    grads = [sides[0][0], sides[1][0], sides[1][1]]
-    for c, (a, b) in enumerate(pair_table):
-        prod[:, c * gr : (c + 1) * gr] = grads[a] * grads[b]
+    group = 4 if count % 4 == 0 else count
+    for at in range(0, count, group):
+        grads = []
+        for f, name in enumerate(("wxd", "wxs", "wxs")):
+            part = planes[f, at : at + group].reshape(group * gr, cols)
+            out = jnp.dot(part, get(name), preferred_element_type=F32)
+            grads.append(out.astype(BF16).reshape(group, gr, cols))
+        for c, (a, b) in enumerate(pair_table):
+            prod[at : at + group, c * gr : (c + 1) * gr] = grads[a] * grads[b]
     for z in range(count):
         for half in range(2):
             part = prod[z, half * 3 * gr : (half + 1) * 3 * gr]
@@ -202,17 +203,28 @@
     return jnp.where(full == packed + z * (HALO - NEED) + first, 1.0, 0.0).astype(BF16)
 
 
-def load_kernel(vol, s1, s2):
+def load_kernel(vol, s1, s2, vol_out, top, bottom, sems):
     depth, rows, cols = vol.shape
     odd = lax.rem(lax.axis_index("row"), 2) == 1
-    top = vol[:, 0:HALO, :].reshape(depth * HALO, cols)
-    bottom = vol[:, rows - HALO : rows, :].reshape(depth * HALO, cols)
-    to_before = jnp.dot(spread_rows(0), top, preferred_element_type=F32).astype(BF16)
+    copies = [
+        pltpu.make_async_copy(vol.at[:, 0:HALO, :], top, sems.at[0]),
+        pltpu.make_async_copy(vol.at[:, rows - HALO : rows, :], bottom, sems.at[1]),
+        pltpu.make_async_copy(vol, vol_out, sems.at[2]),
+    ]
+    for copy in copies:
+        copy.start()
+    first_rows, last_rows = spread_rows(0), spread_rows(HALO - NEED)
+    copies[0].wait()
+    copies[1].wait()
+    to_before = jnp.dot(
+        first_rows, top[...].reshape(depth * HALO, cols), preferred_element_type=F32
+    ).astype(BF16)
     to_after = jnp.dot(
-        spread_rows(HALO - NEED), bottom, preferred_element_type=F32
+        last_rows, bottom[...].reshape(depth * HALO, cols), preferred_element_type=F32
     ).astype(BF16)
     s1[...] = jnp.where(odd, to_before, to_after)
     s2[...] = jnp.where(odd, to_after, to_before)
+    copies[2].wait()
 
 
 def column_select(n_col, cols):
@@ -252,18 +264,19 @@
 def edges_kernel(n_col, vol, own, zmsg, *refs):
     depth, rows, cols = vol.shape
     gz = lax.axis_index("gz")
+    refs, middles = refs[:-1], refs[-1]
     select = column_select(n_col, cols)
     for b in range(depth // 2):
         source = vol[2 * b : 2 * b + 2].reshape(2 * rows, cols)
         slots, middle, messages = pick_columns(select, source)
-        own[b] = slots
-        for ref, message in zip(refs, [middle] + messages):
+        own[b], middles[b] = slots, middle
+        for ref, message in zip(refs, messages):
             ref[b] = message
     base = jnp.where(gz == 0, depth - R, 0)
     halve(zmsg, 0, vol[pl.ds(base, R)].reshape(R * rows, cols))
     first = jnp.where(gz == 0, (depth - EXTRA) // 2, 0)
     n = EXTRA // 2
-    zmsg[2 * R * rows :] = refs[0][pl.ds(first, n)].reshape(n * 16, 128)
+    zmsg[2 * R * rows :] = middles[pl.ds(first, n)].reshape(n * 16, 128)
 
 
 def pack_kernel(place_of, n_col, r1, r2, w, *refs):
@@ -303,6 +316,10 @@
     for ref, message in zip(zxmsgs, xmsgs):
         ref[0:n2] = message[pl.ds(first2, n2)]
         ref[n2:] = message[pl.ds(pairs + first4, n4)]
+
+
+def stage_kernel(w, w_out):
+    pass
 
 
 FIRST = 5
@@ -511,15 +528,21 @@
         out[:, q] = total
 
 
-def call(body, outs, operands, scratch, name, flops=0):
+def call(body, outs, operands, scratch, name, flops=0, aliases=None, n_hbm=0):
     vmem = pl.BlockSpec(memory_space=pltpu.VMEM)
+    hbm = pl.BlockSpec(memory_space=pltpu.HBM)
+    operands = [
+        pltpu.with_memory_space_constraint(o, pltpu.HBM) if i < n_hbm else o
+        for i, o in enumerate(operands)
+    ]
     moved = sum(o.size * o.dtype.itemsize for o in list(outs) + list(operands))
     return pl.pallas_call(
         body,
         out_shape=list(outs),
-        in_specs=[vmem] * len(operands),
+        in_specs=[hbm] * n_hbm + [vmem] * (len(operands) - n_hbm),
         out_specs=[vmem] * len(outs),
         scratch_shapes=scratch,
+        input_output_aliases=aliases or {},
         compiler_params=pltpu.CompilerParams(vmem_limit_bytes=24 * 2**20),
         cost_estimate=pl.CostEstimate(flops=flops, bytes_accessed=moved, transcendentals=0),
         name=name,
@@ -550,17 +573,24 @@
 
     layer_flops = 2 * cols * (3 * gr * 2 * ext + 3 * gr * cols + n_rows * 3 * gr + n_rows * quarter)
 
-    s1, s2 = call(load_kernel, [bf16(depth * NEED, cols)] * 2, [volume], [], "load")
+    dma = pltpu.SemaphoreType.DMA
+    s1, s2, vol = call(
+        load_kernel,
+        [bf16(depth * NEED, cols)] * 2 + [bf16(depth, rows, cols)],
+        [volume], [pltpu.VMEM((depth, HALO, cols), BF16)] * 2 + [dma((3,))], "load", n_hbm=1,
+    )
     inner = [(i, i + 1) for i in range(1, n_row - 1, 2)]
     inner = inner + [(j, i) for i, j in inner]
     r2 = lax.ppermute(s2, "row", inner)
     r1 = lax.ppermute(s1, "row", [(i, i ^ 1) for i in range(n_row)])
-    vol, w = volume, jnp.asarray(table)
-    own, zmsg, _, *xown = call(
+    (w,) = call(
+        stage_kernel, [bf16(*table.shape)], [jnp.asarray(table)], [], "stage", aliases={0: 0}
+    )
+    own, zmsg, *xown = call(
         lambda *refs: edges_kernel(n_col, *refs),
         [bf16(pairs, SLOTS, 128), bf16(2 * R * rows + n2 * 16, 128)]
-        + [bf16(pairs, HALO, 128)] * (n_side + 1),
-        [volume], [], "edges",
+        + [bf16(pairs, HALO, 128)] * n_side,
+        [vol], [pltpu.VMEM((pairs, 16, 128), BF16)], "edges",
     )
     swap = [(0, 1), (1, 0)]
     zown = lax.ppermute(zmsg, "gz", swap)

time: 21 us -> 19 us (0.905)
  local copies, waits for them, and re-layouts: 2.53 us -> 1.48 us
  starting transfers between devices: 10.4 us -> 9.6 us
  waiting for transfers between devices: 0.33 us -> 0.02 us
    ppermute x1, starting transfers between devices: 0.04 us -> 1.24 us  [per_device(): xs.append(lax.ppermute(messages[side], 'col', line))]
    unnamed x8 -> x1, local copies, waits for them, and re-layouts: 2.53 us -> 1.48 us
    ppermute x1, starting transfers between devices: 1.8 us -> 0.94 us  [per_device(): zcorner = lax.ppermute(zcmsg, 'gz', swap)]
    ppermute x1, starting transfers between devices: 1.22 us -> 0.54 us  [per_device(): zxs.append(lax.ppermute(messages[n_side + side], ('gz', 'col'), both))]
    ppermute x1, starting transfers between devices: 1.44 us -> 0.94 us  [per_device(): sums = lax.ppermute(send, 'gz', swap)]
    ppermute x1, waiting for transfers between devices: 0.31 us -> 0.01 us  [per_device(): r2 = lax.ppermute(s2, 'row', inner)]
    pallas_call x7 -> x8, Pallas kernels: 7.52 us -> 7.52 us  [call(): pl.pallas_call(body, out_shape=list(outs), in_specs=[hbm] * n_hbm + [vmem...]
  transfers between devices with their start and end apart: 7 -> 7, of which waited for: 1 -> 0; matrix products, arithmetic and copies ran while one was open for 0% -> 8% of each run, Pallas kernels for 31% -> 30%
where the time goes in v2:
time: 19 us; the launch traced here: 18.7 us
  starting transfers between devices  9.6 us (51%)
  Pallas kernels  7.52 us (40%)
  local copies, waits for them, and re-layouts  1.48 us (8%)
    pallas_call x8, Pallas kernels, call(): pl.pallas_call(body, out_shape=list(outs), in_specs=[hbm] * n_hbm + [vmem...  7.52 us
    ppermute x1, starting transfers between devices, per_device(): r2 = lax.ppermute(s2, 'row', inner)  4.55 us
    unnamed x1, local copies, waits for them, and re-layouts  1.48 us
    ppermute x1, starting transfers between devices, per_device(): zown = lax.ppermute(zmsg, 'gz', swap)  1.27 us
    ppermute x1, starting transfers between devices, per_device(): xs.append(lax.ppermute(messages[side], 'col', line))  1.24 us
    ppermute x1, starting transfers between devices, per_device(): sums = lax.ppermute(send, 'gz', swap)  0.94 us
    ppermute x1, starting transfers between devices, per_device(): zcorner = lax.ppermute(zcmsg, 'gz', swap)  0.94 us
    ppermute x1, starting transfers between devices, per_device(): zxs.append(lax.ppermute(messages[n_side + side], ('gz', 'col'), both))  0.54 us
  transfers between devices with their start and end apart: 7, of which 0 were waited for; matrix products, arithmetic and copies ran while one was open for 8% of the time, Pallas kernels for 30%

profile of v2, /device:TPU:1, one launch (start us, length us, event | category | flops | bytes accessed | tf_op | source)
XLA Modules:
  0.0 18.7 jit_solution(13500355518656020909)
XLA Ops:
  0.0 1.2 %load.1 = (bf16[176,256]{1,0:T(8,128)(2,1)S(1)}, bf16[176,256]{1,0:T(8,128)(2,1)S(1)}, bf16[16,64,256]{2,1,0:T(8,128)(2,1)S(1)}) custom-call(bf16[16,64,256]{2,1,0:T(8,128)(2,1)} %vol.1), custom_call_target="tpu_custom_call" | custom-call | bytes 1228800 | tf_op jit(solution)/shard_map/load/pallas_call | solution.py:539
  1.2 0.1 collective-permute-start
  1.3 4.6 %collective-permute-start.1 = (bf16[176,256]{1,0:T(8,128)(2,1)S(1)}, bf16[176,256]{1,0:T(8,128)(2,1)S(1)}, u32[]{:S(2)}, u32[]{:S(2)}) collective-permute-start(bf16[176,256]{1,0:T(8,128)(2,1)S(1)} %get-tuple-element.20), channel_id=1, source_target_pairs={{2,4},{6,8},{10,12},{4,2},{8,6},{12,10},{3,5},{7,9},{11,13},{5,3},... | collective-permute-start | bytes 270344 | tf_op jit(solution)/shard_map/ppermute | solution.py:584
  5.9 0.3 %edges.1 = (bf16[8,32,128]{2,1,0:T(8,128)(2,1)S(1)}, bf16[480,128]{1,0:T(8,128)(2,1)S(1)}, bf16[8,16,128]{2,1,0:T(8,128)(2,1)S(1)}) custom-call(bf16[16,64,256]{2,1,0:T(8,128)(2,1)S(1)} %get-tuple-element.18.refs_0_), custom_call_target="tpu_custom_call" | custom-call | bytes 745472 | tf_op jit(solution)/shard_map/edges/pallas_call | solution.py:539
  6.2 1.3 %collective-permute-start.2 = (bf16[480,128]{1,0:T(8,128)(2,1)S(1)}, bf16[480,128]{1,0:T(8,128)(2,1)S(1)}, u32[]{:S(2)}, u32[]{:S(2)}) collective-permute-start(bf16[480,128]{1,0:T(8,128)(2,1)S(1)} %get-tuple-element.25), channel_id=1, source_target_pairs={{0,16},{16,0},{1,17},{17,1},{2,18},{18,2},{3,19},{19,3},{4,20},{20... | collective-permute-start | bytes 368648 | tf_op jit(solution)/shard_map/ppermute | solution.py:596
  7.5 1.5 %copy.6.w = bf16[3504,256]{1,0:T(8,128)(2,1)S(1)} copy(bf16[3504,256]{1,0:T(8,128)(2,1)} %constant.2.clone) | data formatting | bytes 3588096
  9.0 0.0 collective-permute-done.refs_0_
  9.0 0.0 collective-permute-done.1.refs_1_
  9.0 0.4 %pack.1 = (bf16[16,32,256]{2,1,0:T(8,128)(2,1)S(1)}, bf16[4,32,128]{2,1,0:T(8,128)(2,1)S(1)}, bf16[176,128]{1,0:T(8,128)(2,1)S(1)}, bf16[12,16,128]{2,1,0:T(8,128)(2,1)S(1)}, bf16[9,16,128]{2,1,0:T(8,128)(2,1)S(1)}) custom-call(bf16[176,256]{1,0:T(8,128)(2,1)S(1)} %collective-permute-done.refs_0_, bf16[176,256]{1,0:T(8,128)(2,1)S(1)} %collective-permute-done.1.refs_1_, ...), custom_call_target="tpu_custom_call" | custom-call | bytes 2433024 | tf_op jit(solution)/shard_map/pack/pallas_call | solution.py:539
  9.4 0.9 %collective-permute-start.3 = (bf16[176,128]{1,0:T(8,128)(2,1)S(1)}, bf16[176,128]{1,0:T(8,128)(2,1)S(1)}, u32[]{:S(2)}, u32[]{:S(2)}) collective-permute-start(bf16[176,128]{1,0:T(8,128)(2,1)S(1)} %get-tuple-element.26), channel_id=1, source_target_pairs={{0,16},{16,0},{1,17},{17,1},{2,18},{18,2},{3,19},{19,3},{4,20},{20... | collective-permute-start | bytes 135176 | tf_op jit(solution)/shard_map/ppermute | solution.py:605
  10.3 1.2 %collective-permute-start.4 = (bf16[12,16,128]{2,1,0:T(8,128)(2,1)S(1)}, bf16[12,16,128]{2,1,0:T(8,128)(2,1)S(1)}, u32[]{:S(2)}, u32[]{:S(2)}) collective-permute-start(bf16[12,16,128]{2,1,0:T(8,128)(2,1)S(1)} %get-tuple-element.28), channel_id=1, source_target_pairs={{0,1},{1,0},{2,3},{3,2},{4,5},{5,4},{6,7},{7,6},{8,9},{9,8},{10,11... | collective-permute-start | bytes 147464 | tf_op jit(solution)/shard_map/ppermute | solution.py:613
  11.5 0.5 %collective-permute-start.5 = (bf16[9,16,128]{2,1,0:T(8,128)(2,1)S(1)}, bf16[9,16,128]{2,1,0:T(8,128)(2,1)S(1)}, u32[]{:S(2)}, u32[]{:S(2)}) collective-permute-start(bf16[9,16,128]{2,1,0:T(8,128)(2,1)S(1)} %get-tuple-element.29), channel_id=1, source_target_pairs={{0,17},{1,16},{16,1},{17,0},{2,19},{3,18},{18,3},{19,2},{4,21},{5,... | collective-permute-start | bytes 110600 | tf_op jit(solution)/shard_map/ppermute | solution.py:614
  12.1 1.2 %first.1.refs_4_.refs_6_ = f32[5,96,64]{2,1,0:T(8,128)S(1)} custom-call(bf16[16,64,256]{2,1,0:T(8,128)(2,1)S(1)} %get-tuple-element.18.refs_0_, bf16[16,32,256]{2,1,0:T(8,128)(2,1)S(1)} %get-tuple-element.22.refs_1_, bf16[3504,256]{1,0:T(8,128)(2,1)S(1)} %stage.1.refs_2_.refs_5_.refs_8_), custom_call_target="tpu_custom_call" | custom-call | flops 349962240 | bytes 2703360 | tf_op jit(solution)/shard_map/first/pallas_call | solution.py:539
  13.2 0.0 collective-permute-done.2.refs_2_.refs_4_
  13.3 0.0 collective-permute-done.3.refs_3_.refs_5_
  13.3 1.1 %near.1 = (f32[3,96,64]{2,1,0:T(8,128)S(1)}, bf16[96,128]{1,0:T(8,128)(2,1)S(1)}) custom-call(bf16[16,64,256]{2,1,0:T(8,128)(2,1)S(1)} %get-tuple-element.18.refs_0_, bf16[16,32,256]{2,1,0:T(8,128)(2,1)S(1)} %get-tuple-element.22.refs_1_, bf16[480,128]{1,0:T(8,128)(2,1)S(1)} %collective-permute-done.2.refs_2_.refs_4_, ...), custom_call_target="tpu_custom_call" | custom-call | flops 209977344 | bytes 2969600 | tf_op jit(solution)/shard_map/near/pallas_call | solution.py:539
  14.4 0.9 %collective-permute-start.6 = (bf16[96,128]{1,0:T(8,128)(2,1)S(1)}, bf16[96,128]{1,0:T(8,128)(2,1)S(1)}, u32[]{:S(2)}, u32[]{:S(2)}) collective-permute-start(bf16[96,128]{1,0:T(8,128)(2,1)S(1)} %get-tuple-element.30), channel_id=1, source_target_pairs={{0,16},{16,0},{1,17},{17,1},{2,18},{18,2},{3,19},{19,3},{4,20},{20... | collective-permute-start | bytes 73736 | tf_op jit(solution)/shard_map/ppermute | solution.py:628
  15.3 0.0 collective-permute-done.5.refs_10_
  15.3 0.0 collective-permute-done.4.refs_9_
  15.3 2.5 %last.1.own = f32[6,4,16,64]{3,2,1,0:T(8,128)S(1)} custom-call(bf16[16,64,256]{2,1,0:T(8,128)(2,1)S(1)} %get-tuple-element.18.refs_0_, bf16[16,32,256]{2,1,0:T(8,128)(2,1)S(1)} %get-tuple-element.22.refs_1_, bf16[8,32,128]{2,1,0:T(8,128)(2,1)S(1)} %get-tuple-element.23.refs_2_, bf16[4,32,128]{2,1,0:T(8,128)(2,1)S(1)} %get-tuple-element.24.refs_3_, ...), custom_call_target="tpu_custom_call" | custom-call | flops 769916928 | bytes 3227648 | tf_op jit(solution)/shard_map/last/pallas_call | solution.py:539
  17.9 0.0 collective-permute-done.6.got
  17.9 0.8 %add.1 = f32[6,4,16,64]{3,2,1,0:T(8,128)} custom-call(f32[6,4,16,64]{3,2,1,0:T(8,128)S(1)} %last.1.own, bf16[96,128]{1,0:T(8,128)(2,1)S(1)} %collective-permute-done.6.got), custom_call_target="tpu_custom_call" | custom-call | bytes 221184 | tf_op jit(solution)/shard_map/add/pallas_call | solution.py:539
  (1 shorter events, 0.0 us)
Async XLA Ops:
  1.2 7.7 %collective-permute-start = (bf16[176,256]{1,0:T(8,128)(2,1)S(1)}, bf16[176,256]{1,0:T(8,128)(2,1)S(1)}, u32[]{:S(2)}, u32[]{:S(2)}) collective-permute-start(bf16[176,256]{1,0:T(8,128)(2,1)S(1)} %get-tuple-element.19), channel_id=1, source_target_pairs={{0,2},{2,0},{4,6},{6,4},{8,10},{10,8},{12,14},{14,12},{1,3},{3,1},... | collective-permute-start | bytes 270344 | tf_op jit(solution)/shard_map/ppermute | solution.py:585
  1.3 7.6 %collective-permute-start.1 = (bf16[176,256]{1,0:T(8,128)(2,1)S(1)}, bf16[176,256]{1,0:T(8,128)(2,1)S(1)}, u32[]{:S(2)}, u32[]{:S(2)}) collective-permute-start(bf16[176,256]{1,0:T(8,128)(2,1)S(1)} %get-tuple-element.20), channel_id=1, source_target_pairs={{2,4},{6,8},{10,12},{4,2},{8,6},{12,10},{3,5},{7,9},{11,13},{5,3},... | collective-permute-start | bytes 270344 | tf_op jit(solution)/shard_map/ppermute | solution.py:584
  6.2 7.1 %collective-permute-start.2 = (bf16[480,128]{1,0:T(8,128)(2,1)S(1)}, bf16[480,128]{1,0:T(8,128)(2,1)S(1)}, u32[]{:S(2)}, u32[]{:S(2)}) collective-permute-start(bf16[480,128]{1,0:T(8,128)(2,1)S(1)} %get-tuple-element.25), channel_id=1, source_target_pairs={{0,16},{16,0},{1,17},{17,1},{2,18},{18,2},{3,19},{19,3},{4,20},{20... | collective-permute-start | bytes 368648 | tf_op jit(solution)/shard_map/ppermute | solution.py:596
  9.4 3.9 %collective-permute-start.3 = (bf16[176,128]{1,0:T(8,128)(2,1)S(1)}, bf16[176,128]{1,0:T(8,128)(2,1)S(1)}, u32[]{:S(2)}, u32[]{:S(2)}) collective-permute-start(bf16[176,128]{1,0:T(8,128)(2,1)S(1)} %get-tuple-element.26), channel_id=1, source_target_pairs={{0,16},{16,0},{1,17},{17,1},{2,18},{18,2},{3,19},{19,3},{4,20},{20... | collective-permute-start | bytes 135176 | tf_op jit(solution)/shard_map/ppermute | solution.py:605
  10.3 5.1 %collective-permute-start.4 = (bf16[12,16,128]{2,1,0:T(8,128)(2,1)S(1)}, bf16[12,16,128]{2,1,0:T(8,128)(2,1)S(1)}, u32[]{:S(2)}, u32[]{:S(2)}) collective-permute-start(bf16[12,16,128]{2,1,0:T(8,128)(2,1)S(1)} %get-tuple-element.28), channel_id=1, source_target_pairs={{0,1},{1,0},{2,3},{3,2},{4,5},{5,4},{6,7},{7,6},{8,9},{9,8},{10,11... | collective-permute-start | bytes 147464 | tf_op jit(solution)/shard_map/ppermute | solution.py:613
  11.5 3.8 %collective-permute-start.5 = (bf16[9,16,128]{2,1,0:T(8,128)(2,1)S(1)}, bf16[9,16,128]{2,1,0:T(8,128)(2,1)S(1)}, u32[]{:S(2)}, u32[]{:S(2)}) collective-permute-start(bf16[9,16,128]{2,1,0:T(8,128)(2,1)S(1)} %get-tuple-element.29), channel_id=1, source_target_pairs={{0,17},{1,16},{16,1},{17,0},{2,19},{3,18},{18,3},{19,2},{4,21},{5,... | collective-permute-start | bytes 110600 | tf_op jit(solution)/shard_map/ppermute | solution.py:614
  14.4 3.5 %collective-permute-start.6 = (bf16[96,128]{1,0:T(8,128)(2,1)S(1)}, bf16[96,128]{1,0:T(8,128)(2,1)S(1)}, u32[]{:S(2)}, u32[]{:S(2)}) collective-permute-start(bf16[96,128]{1,0:T(8,128)(2,1)S(1)} %get-tuple-element.30), channel_id=1, source_target_pairs={{0,16},{16,0},{1,17},{17,1},{2,18},{18,2},{3,19},{19,3},{4,20},{20... | collective-permute-start | bytes 73736 | tf_op jit(solution)/shard_map/ppermute | solution.py:628

commit v3 on v2

--- a/solution.py
+++ b/solution.py
@@ -127,7 +127,7 @@
             smooth = smooth + (w[3 + s] + w[3 - s]) * float(SMOOTH_D[3 + s])
             term = (w[3 + s] - w[3 - s]) * float(SLOPE_D[3 + s])
             slope = term if slope is None else slope + term
-        yield z, smooth.astype(BF16), slope.astype(BF16)
+        yield z, smooth, slope
 
 
 def getter(place_of, w):
@@ -152,12 +152,19 @@
     gr = rows + 16
     n_rows = 6 * (rows // 4)
     half_rows = n_rows // 2
+    rest = jnp.zeros((8, 128), F32)
     for tile in range(cols // 128):
         lanes = slice(tile * 128, tile * 128 + 128)
         for at in range(0, ext, 16):
-            for z, smooth, slope in z_filter(load(at, lanes), count):
-                zf[z, at : at + 16, lanes] = smooth
-                zf[z, ext + at : ext + at + 16, lanes] = slope
+            blocks = load(at, lanes)
+            if at == rows + HALO:
+                blocks = [block[0:8] for block in blocks]
+            for z, smooth, slope in z_filter(blocks, count):
+                if at == rows + HALO:
+                    smooth = jnp.concatenate([smooth, rest], axis=0)
+                    slope = jnp.concatenate([slope, rest], axis=0)
+                zf[z, at : at + 16, lanes] = smooth.astype(BF16)
+                zf[z, ext + at : ext + at + 16, lanes] = slope.astype(BF16)
     wy = get("wy")
     for z in range(count):
         out = jnp.dot(wy, zf[z], preferred_element_type=F32).astype(BF16)
@@ -322,9 +329,9 @@
     pass
 
 
-FIRST = 5
+FIRST = 7
 EDGE = R
-LAST = 8
+LAST = 6
 
 
 def first_kernel(place_of, n_row, vol, yud, w, u_ref, *scratch):
@@ -455,8 +462,8 @@
     at_high = beyond[1:12] + own_layers + zero
     layers = [jnp.where(low, a, b) for a, b in zip(at_low, at_high)]
     for z, smooth, slope in z_filter(layers, count):
-        hs[SLOTS * z : SLOTS * (z + 1)] = smooth
-        hd[SLOTS * z : SLOTS * (z + 1)] = slope
+        hs[SLOTS * z : SLOTS * (z + 1)] = smooth.astype(BF16)
+        hd[SLOTS * z : SLOTS * (z + 1)] = slope.astype(BF16)
     p01 = lax.dot_general(
         get("wy_strip", 128), hs[...], NT, preferred_element_type=F32
     ).astype(BF16)

time: 19 us -> 19.1 us (level)
  Pallas kernels: 7.52 us -> 7.8 us
    pallas_call x8, Pallas kernels: 7.52 us -> 7.8 us  [call(): pl.pallas_call(body, out_shape=list(outs), in_specs=[hbm] * n_hbm + [vmem...]
  transfers between devices with their start and end apart: 7 -> 7, of which waited for: 0 -> 0; matrix products, arithmetic and copies ran while one was open for 8% -> 8% of each run, Pallas kernels for 30% -> 31%
where the time goes in v3:
time: 19.1 us; the launch traced here: 19 us
  starting transfers between devices  9.6 us (50%)
  Pallas kernels  7.8 us (41%)
  local copies, waits for them, and re-layouts  1.48 us (8%)
    pallas_call x8, Pallas kernels, call(): pl.pallas_call(body, out_shape=list(outs), in_specs=[hbm] * n_hbm + [vmem...  7.8 us
    ppermute x1, starting transfers between devices, per_device(): r2 = lax.ppermute(s2, 'row', inner)  4.55 us
    unnamed x1, local copies, waits for them, and re-layouts  1.48 us
    ppermute x1, starting transfers between devices, per_device(): zown = lax.ppermute(zmsg, 'gz', swap)  1.27 us
    ppermute x1, starting transfers between devices, per_device(): xs.append(lax.ppermute(messages[side], 'col', line))  1.23 us
    ppermute x1, starting transfers between devices, per_device(): sums = lax.ppermute(send, 'gz', swap)  0.94 us
    ppermute x1, starting transfers between devices, per_device(): zcorner = lax.ppermute(zcmsg, 'gz', swap)  0.94 us
    ppermute x1, starting transfers between devices, per_device(): zxs.append(lax.ppermute(messages[n_side + side], ('gz', 'col'), both))  0.55 us
  transfers between devices with their start and end apart: 7, of which 0 were waited for; matrix products, arithmetic and copies ran while one was open for 8% of the time, Pallas kernels for 31%

profile of v3, /device:TPU:1, one launch (start us, length us, event | category | flops | bytes accessed | tf_op | source)
XLA Modules:
  0.0 19.0 jit_solution(9780851649084330549)
XLA Ops:
  0.0 1.2 %load.1 = (bf16[176,256]{1,0:T(8,128)(2,1)S(1)}, bf16[176,256]{1,0:T(8,128)(2,1)S(1)}, bf16[16,64,256]{2,1,0:T(8,128)(2,1)S(1)}) custom-call(bf16[16,64,256]{2,1,0:T(8,128)(2,1)} %vol.1), custom_call_target="tpu_custom_call" | custom-call | bytes 1228800 | tf_op jit(solution)/shard_map/load/pallas_call | solution.py:546
  1.2 0.1 collective-permute-start
  1.3 4.6 %collective-permute-start.1 = (bf16[176,256]{1,0:T(8,128)(2,1)S(1)}, bf16[176,256]{1,0:T(8,128)(2,1)S(1)}, u32[]{:S(2)}, u32[]{:S(2)}) collective-permute-start(bf16[176,256]{1,0:T(8,128)(2,1)S(1)} %get-tuple-element.20), channel_id=1, source_target_pairs={{2,4},{6,8},{10,12},{4,2},{8,6},{12,10},{3,5},{7,9},{11,13},{5,3},... | collective-permute-start | bytes 270344 | tf_op jit(solution)/shard_map/ppermute | solution.py:591
  5.9 0.3 %edges.1 = (bf16[8,32,128]{2,1,0:T(8,128)(2,1)S(1)}, bf16[480,128]{1,0:T(8,128)(2,1)S(1)}, bf16[8,16,128]{2,1,0:T(8,128)(2,1)S(1)}) custom-call(bf16[16,64,256]{2,1,0:T(8,128)(2,1)S(1)} %get-tuple-element.18.refs_0_), custom_call_target="tpu_custom_call" | custom-call | bytes 745472 | tf_op jit(solution)/shard_map/edges/pallas_call | solution.py:546
  6.2 1.3 %collective-permute-start.2 = (bf16[480,128]{1,0:T(8,128)(2,1)S(1)}, bf16[480,128]{1,0:T(8,128)(2,1)S(1)}, u32[]{:S(2)}, u32[]{:S(2)}) collective-permute-start(bf16[480,128]{1,0:T(8,128)(2,1)S(1)} %get-tuple-element.25), channel_id=1, source_target_pairs={{0,16},{16,0},{1,17},{17,1},{2,18},{18,2},{3,19},{19,3},{4,20},{20... | collective-permute-start | bytes 368648 | tf_op jit(solution)/shard_map/ppermute | solution.py:603
  7.5 1.5 %copy.6.w = bf16[3504,256]{1,0:T(8,128)(2,1)S(1)} copy(bf16[3504,256]{1,0:T(8,128)(2,1)} %constant.2.clone) | data formatting | bytes 3588096
  9.0 0.0 collective-permute-done.refs_0_
  9.0 0.0 collective-permute-done.1.refs_1_
  9.0 0.4 %pack.1 = (bf16[16,32,256]{2,1,0:T(8,128)(2,1)S(1)}, bf16[4,32,128]{2,1,0:T(8,128)(2,1)S(1)}, bf16[176,128]{1,0:T(8,128)(2,1)S(1)}, bf16[12,16,128]{2,1,0:T(8,128)(2,1)S(1)}, bf16[9,16,128]{2,1,0:T(8,128)(2,1)S(1)}) custom-call(bf16[176,256]{1,0:T(8,128)(2,1)S(1)} %collective-permute-done.refs_0_, bf16[176,256]{1,0:T(8,128)(2,1)S(1)} %collective-permute-done.1.refs_1_, ...), custom_call_target="tpu_custom_call" | custom-call | bytes 2433024 | tf_op jit(solution)/shard_map/pack/pallas_call | solution.py:546
  9.4 0.9 %collective-permute-start.3 = (bf16[176,128]{1,0:T(8,128)(2,1)S(1)}, bf16[176,128]{1,0:T(8,128)(2,1)S(1)}, u32[]{:S(2)}, u32[]{:S(2)}) collective-permute-start(bf16[176,128]{1,0:T(8,128)(2,1)S(1)} %get-tuple-element.26), channel_id=1, source_target_pairs={{0,16},{16,0},{1,17},{17,1},{2,18},{18,2},{3,19},{19,3},{4,20},{20... | collective-permute-start | bytes 135176 | tf_op jit(solution)/shard_map/ppermute | solution.py:612
  10.3 1.2 %collective-permute-start.4 = (bf16[12,16,128]{2,1,0:T(8,128)(2,1)S(1)}, bf16[12,16,128]{2,1,0:T(8,128)(2,1)S(1)}, u32[]{:S(2)}, u32[]{:S(2)}) collective-permute-start(bf16[12,16,128]{2,1,0:T(8,128)(2,1)S(1)} %get-tuple-element.28), channel_id=1, source_target_pairs={{0,1},{1,0},{2,3},{3,2},{4,5},{5,4},{6,7},{7,6},{8,9},{9,8},{10,11... | collective-permute-start | bytes 147464 | tf_op jit(solution)/shard_map/ppermute | solution.py:620
  11.5 0.5 %collective-permute-start.5 = (bf16[9,16,128]{2,1,0:T(8,128)(2,1)S(1)}, bf16[9,16,128]{2,1,0:T(8,128)(2,1)S(1)}, u32[]{:S(2)}, u32[]{:S(2)}) collective-permute-start(bf16[9,16,128]{2,1,0:T(8,128)(2,1)S(1)} %get-tuple-element.29), channel_id=1, source_target_pairs={{0,17},{1,16},{16,1},{17,0},{2,19},{3,18},{18,3},{19,2},{4,21},{5,... | collective-permute-start | bytes 110600 | tf_op jit(solution)/shard_map/ppermute | solution.py:621
  12.1 1.6 %first.1.refs_4_.refs_6_ = f32[7,96,64]{2,1,0:T(8,128)S(1)} custom-call(bf16[16,64,256]{2,1,0:T(8,128)(2,1)S(1)} %get-tuple-element.18.refs_0_, bf16[16,32,256]{2,1,0:T(8,128)(2,1)S(1)} %get-tuple-element.22.refs_1_, bf16[3504,256]{1,0:T(8,128)(2,1)S(1)} %stage.1.refs_2_.refs_5_.refs_8_), custom_call_target="tpu_custom_call" | custom-call | flops 489947136 | bytes 2752512 | tf_op jit(solution)/shard_map/first/pallas_call | solution.py:546
  13.7 0.0 collective-permute-done.2.refs_2_.refs_4_
  13.7 0.0 collective-permute-done.3.refs_3_.refs_5_
  13.7 1.1 %near.1 = (f32[3,96,64]{2,1,0:T(8,128)S(1)}, bf16[96,128]{1,0:T(8,128)(2,1)S(1)}) custom-call(bf16[16,64,256]{2,1,0:T(8,128)(2,1)S(1)} %get-tuple-element.18.refs_0_, bf16[16,32,256]{2,1,0:T(8,128)(2,1)S(1)} %get-tuple-element.22.refs_1_, bf16[480,128]{1,0:T(8,128)(2,1)S(1)} %collective-permute-done.2.refs_2_.refs_4_, ...), custom_call_target="tpu_custom_call" | custom-call | flops 209977344 | bytes 3018752 | tf_op jit(solution)/shard_map/near/pallas_call | solution.py:546
  14.9 0.9 %collective-permute-start.6 = (bf16[96,128]{1,0:T(8,128)(2,1)S(1)}, bf16[96,128]{1,0:T(8,128)(2,1)S(1)}, u32[]{:S(2)}, u32[]{:S(2)}) collective-permute-start(bf16[96,128]{1,0:T(8,128)(2,1)S(1)} %get-tuple-element.30), channel_id=1, source_target_pairs={{0,16},{16,0},{1,17},{17,1},{2,18},{18,2},{3,19},{19,3},{4,20},{20... | collective-permute-start | bytes 73736 | tf_op jit(solution)/shard_map/ppermute | solution.py:635
  15.8 0.0 collective-permute-done.5.refs_10_
  15.8 0.0 collective-permute-done.4.refs_9_
  15.8 2.4 %last.1.own = f32[6,4,16,64]{3,2,1,0:T(8,128)S(1)} custom-call(bf16[16,64,256]{2,1,0:T(8,128)(2,1)S(1)} %get-tuple-element.18.refs_0_, bf16[16,32,256]{2,1,0:T(8,128)(2,1)S(1)} %get-tuple-element.22.refs_1_, bf16[8,32,128]{2,1,0:T(8,128)(2,1)S(1)} %get-tuple-element.23.refs_2_, bf16[4,32,128]{2,1,0:T(8,128)(2,1)S(1)} %get-tuple-element.24.refs_3_, ...), custom_call_target="tpu_custom_call" | custom-call | flops 629932032 | bytes 3276800 | tf_op jit(solution)/shard_map/last/pallas_call | solution.py:546
  18.2 0.0 collective-permute-done.6.got
  18.2 0.8 %add.1 = f32[6,4,16,64]{3,2,1,0:T(8,128)} custom-call(f32[6,4,16,64]{3,2,1,0:T(8,128)S(1)} %last.1.own, bf16[96,128]{1,0:T(8,128)(2,1)S(1)} %collective-permute-done.6.got), custom_call_target="tpu_custom_call" | custom-call | bytes 221184 | tf_op jit(solution)/shard_map/add/pallas_call | solution.py:546
  (1 shorter events, 0.0 us)
Async XLA Ops:
  1.2 7.7 %collective-permute-start = (bf16[176,256]{1,0:T(8,128)(2,1)S(1)}, bf16[176,256]{1,0:T(8,128)(2,1)S(1)}, u32[]{:S(2)}, u32[]{:S(2)}) collective-permute-start(bf16[176,256]{1,0:T(8,128)(2,1)S(1)} %get-tuple-element.19), channel_id=1, source_target_pairs={{0,2},{2,0},{4,6},{6,4},{8,10},{10,8},{12,14},{14,12},{1,3},{3,1},... | collective-permute-start | bytes 270344 | tf_op jit(solution)/shard_map/ppermute | solution.py:592
  1.3 7.6 %collective-permute-start.1 = (bf16[176,256]{1,0:T(8,128)(2,1)S(1)}, bf16[176,256]{1,0:T(8,128)(2,1)S(1)}, u32[]{:S(2)}, u32[]{:S(2)}) collective-permute-start(bf16[176,256]{1,0:T(8,128)(2,1)S(1)} %get-tuple-element.20), channel_id=1, source_target_pairs={{2,4},{6,8},{10,12},{4,2},{8,6},{12,10},{3,5},{7,9},{11,13},{5,3},... | collective-permute-start | bytes 270344 | tf_op jit(solution)/shard_map/ppermute | solution.py:591
  6.2 7.5 %collective-permute-start.2 = (bf16[480,128]{1,0:T(8,128)(2,1)S(1)}, bf16[480,128]{1,0:T(8,128)(2,1)S(1)}, u32[]{:S(2)}, u32[]{:S(2)}) collective-permute-start(bf16[480,128]{1,0:T(8,128)(2,1)S(1)} %get-tuple-element.25), channel_id=1, source_target_pairs={{0,16},{16,0},{1,17},{17,1},{2,18},{18,2},{3,19},{19,3},{4,20},{20... | collective-permute-start | bytes 368648 | tf_op jit(solution)/shard_map/ppermute | solution.py:603
  9.4 4.4 %collective-permute-start.3 = (bf16[176,128]{1,0:T(8,128)(2,1)S(1)}, bf16[176,128]{1,0:T(8,128)(2,1)S(1)}, u32[]{:S(2)}, u32[]{:S(2)}) collective-permute-start(bf16[176,128]{1,0:T(8,128)(2,1)S(1)} %get-tuple-element.26), channel_id=1, source_target_pairs={{0,16},{16,0},{1,17},{17,1},{2,18},{18,2},{3,19},{19,3},{4,20},{20... | collective-permute-start | bytes 135176 | tf_op jit(solution)/shard_map/ppermute | solution.py:612
  10.3 5.5 %collective-permute-start.4 = (bf16[12,16,128]{2,1,0:T(8,128)(2,1)S(1)}, bf16[12,16,128]{2,1,0:T(8,128)(2,1)S(1)}, u32[]{:S(2)}, u32[]{:S(2)}) collective-permute-start(bf16[12,16,128]{2,1,0:T(8,128)(2,1)S(1)} %get-tuple-element.28), channel_id=1, source_target_pairs={{0,1},{1,0},{2,3},{3,2},{4,5},{5,4},{6,7},{7,6},{8,9},{9,8},{10,11... | collective-permute-start | bytes 147464 | tf_op jit(solution)/shard_map/ppermute | solution.py:620
  11.5 4.3 %collective-permute-start.5 = (bf16[9,16,128]{2,1,0:T(8,128)(2,1)S(1)}, bf16[9,16,128]{2,1,0:T(8,128)(2,1)S(1)}, u32[]{:S(2)}, u32[]{:S(2)}) collective-permute-start(bf16[9,16,128]{2,1,0:T(8,128)(2,1)S(1)} %get-tuple-element.29), channel_id=1, source_target_pairs={{0,17},{1,16},{16,1},{17,0},{2,19},{3,18},{18,3},{19,2},{4,21},{5,... | collective-permute-start | bytes 110600 | tf_op jit(solution)/shard_map/ppermute | solution.py:621
  14.9 3.3 %collective-permute-start.6 = (bf16[96,128]{1,0:T(8,128)(2,1)S(1)}, bf16[96,128]{1,0:T(8,128)(2,1)S(1)}, u32[]{:S(2)}, u32[]{:S(2)}) collective-permute-start(bf16[96,128]{1,0:T(8,128)(2,1)S(1)} %get-tuple-element.30), channel_id=1, source_target_pairs={{0,16},{16,0},{1,17},{17,1},{2,18},{18,2},{3,19},{19,3},{4,20},{20... | collective-permute-start | bytes 73736 | tf_op jit(solution)/shard_map/ppermute | solution.py:635

commit v4 on v3

--- a/solution.py
+++ b/solution.py
@@ -171,15 +171,15 @@
         planes[0, z] = out[0:gr]
         planes[1, z] = out[gr : 2 * gr]
         planes[2, z] = out[2 * gr :]
-    group = 4 if count % 4 == 0 else count
-    for at in range(0, count, group):
+    for at in range(0, count, GROUP):
+        n = min(GROUP, count - at)
         grads = []
         for f, name in enumerate(("wxd", "wxs", "wxs")):
-            part = planes[f, at : at + group].reshape(group * gr, cols)
+            part = planes[f, at : at + n].reshape(n * gr, cols)
             out = jnp.dot(part, get(name), preferred_element_type=F32)
-            grads.append(out.astype(BF16).reshape(group, gr, cols))
+            grads.append(out.astype(BF16).reshape(n, gr, cols))
         for c, (a, b) in enumerate(pair_table):
-            prod[at : at + group, c * gr : (c + 1) * gr] = grads[a] * grads[b]
+            prod[at : at + n, c * gr : (c + 1) * gr] = grads[a] * grads[b]
     for z in range(count):
         for half in range(2):
             part = prod[z, half * 3 * gr : (half + 1) * 3 * gr]
@@ -329,9 +329,10 @@
     pass
 
 
-FIRST = 7
+FIRST = 6
+GROUP = 2
 EDGE = R
-LAST = 6
+LAST = 7
 
 
 def first_kernel(place_of, n_row, vol, yud, w, u_ref, *scratch):

time: 19.1 us -> 18.9 us (0.990)
  Pallas kernels: 7.8 us -> 7.48 us
    pallas_call x8, Pallas kernels: 7.8 us -> 7.48 us  [call(): pl.pallas_call(body, out_shape=list(outs), in_specs=[hbm] * n_hbm + [vmem...]
  transfers between devices with their start and end apart: 7 -> 7, of which waited for: 0 -> 0; matrix products, arithmetic and copies ran while one was open for 8% -> 8% of each run, Pallas kernels for 31% -> 29%
where the time goes in v4:
time: 18.9 us; the launch traced here: 18.7 us
  starting transfers between devices  9.6 us (51%)
  Pallas kernels  7.48 us (40%)
  local copies, waits for them, and re-layouts  1.48 us (8%)
    pallas_call x8, Pallas kernels, call(): pl.pallas_call(body, out_shape=list(outs), in_specs=[hbm] * n_hbm + [vmem...  7.48 us
    ppermute x1, starting transfers between devices, per_device(): r2 = lax.ppermute(s2, 'row', inner)  4.55 us
    unnamed x1, local copies, waits for them, and re-layouts  1.48 us
    ppermute x1, starting transfers between devices, per_device(): zown = lax.ppermute(zmsg, 'gz', swap)  1.27 us
    ppermute x1, starting transfers between devices, per_device(): xs.append(lax.ppermute(messages[side], 'col', line))  1.24 us
    ppermute x1, starting transfers between devices, per_device(): zcorner = lax.ppermute(zcmsg, 'gz', swap)  0.94 us
    ppermute x1, starting transfers between devices, per_device(): sums = lax.ppermute(send, 'gz', swap)  0.94 us
    ppermute x1, starting transfers between devices, per_device(): zxs.append(lax.ppermute(messages[n_side + side], ('gz', 'col'), both))  0.54 us
  transfers between devices with their start and end apart: 7, of which 0 were waited for; matrix products, arithmetic and copies ran while one was open for 8% of the time, Pallas kernels for 29%

profile of v4, /device:TPU:1, one launch (start us, length us, event | category | flops | bytes accessed | tf_op | source)
XLA Modules:
  0.0 18.7 jit_solution(14498321138060388648)
XLA Ops:
  0.0 1.2 %load.1 = (bf16[176,256]{1,0:T(8,128)(2,1)S(1)}, bf16[176,256]{1,0:T(8,128)(2,1)S(1)}, bf16[16,64,256]{2,1,0:T(8,128)(2,1)S(1)}) custom-call(bf16[16,64,256]{2,1,0:T(8,128)(2,1)} %vol.1), custom_call_target="tpu_custom_call" | custom-call | bytes 1228800 | tf_op jit(solution)/shard_map/load/pallas_call | solution.py:547
  1.2 0.1 collective-permute-start
  1.3 4.6 %collective-permute-start.1 = (bf16[176,256]{1,0:T(8,128)(2,1)S(1)}, bf16[176,256]{1,0:T(8,128)(2,1)S(1)}, u32[]{:S(2)}, u32[]{:S(2)}) collective-permute-start(bf16[176,256]{1,0:T(8,128)(2,1)S(1)} %get-tuple-element.20), channel_id=1, source_target_pairs={{2,4},{6,8},{10,12},{4,2},{8,6},{12,10},{3,5},{7,9},{11,13},{5,3},... | collective-permute-start | bytes 270344 | tf_op jit(solution)/shard_map/ppermute | solution.py:592
  5.9 0.3 %edges.1 = (bf16[8,32,128]{2,1,0:T(8,128)(2,1)S(1)}, bf16[480,128]{1,0:T(8,128)(2,1)S(1)}, bf16[8,16,128]{2,1,0:T(8,128)(2,1)S(1)}) custom-call(bf16[16,64,256]{2,1,0:T(8,128)(2,1)S(1)} %get-tuple-element.18.refs_0_), custom_call_target="tpu_custom_call" | custom-call | bytes 745472 | tf_op jit(solution)/shard_map/edges/pallas_call | solution.py:547
  6.2 1.3 %collective-permute-start.2 = (bf16[480,128]{1,0:T(8,128)(2,1)S(1)}, bf16[480,128]{1,0:T(8,128)(2,1)S(1)}, u32[]{:S(2)}, u32[]{:S(2)}) collective-permute-start(bf16[480,128]{1,0:T(8,128)(2,1)S(1)} %get-tuple-element.25), channel_id=1, source_target_pairs={{0,16},{16,0},{1,17},{17,1},{2,18},{18,2},{3,19},{19,3},{4,20},{20... | collective-permute-start | bytes 368648 | tf_op jit(solution)/shard_map/ppermute | solution.py:604
  7.5 1.5 %copy.6.w = bf16[3504,256]{1,0:T(8,128)(2,1)S(1)} copy(bf16[3504,256]{1,0:T(8,128)(2,1)} %constant.2.clone) | data formatting | bytes 3588096
  9.0 0.0 collective-permute-done.refs_0_
  9.0 0.0 collective-permute-done.1.refs_1_
  9.0 0.4 %pack.1 = (bf16[16,32,256]{2,1,0:T(8,128)(2,1)S(1)}, bf16[4,32,128]{2,1,0:T(8,128)(2,1)S(1)}, bf16[176,128]{1,0:T(8,128)(2,1)S(1)}, bf16[12,16,128]{2,1,0:T(8,128)(2,1)S(1)}, bf16[9,16,128]{2,1,0:T(8,128)(2,1)S(1)}) custom-call(bf16[176,256]{1,0:T(8,128)(2,1)S(1)} %collective-permute-done.refs_0_, bf16[176,256]{1,0:T(8,128)(2,1)S(1)} %collective-permute-done.1.refs_1_, ...), custom_call_target="tpu_custom_call" | custom-call | bytes 2433024 | tf_op jit(solution)/shard_map/pack/pallas_call | solution.py:547
  9.4 0.9 %collective-permute-start.3 = (bf16[176,128]{1,0:T(8,128)(2,1)S(1)}, bf16[176,128]{1,0:T(8,128)(2,1)S(1)}, u32[]{:S(2)}, u32[]{:S(2)}) collective-permute-start(bf16[176,128]{1,0:T(8,128)(2,1)S(1)} %get-tuple-element.26), channel_id=1, source_target_pairs={{0,16},{16,0},{1,17},{17,1},{2,18},{18,2},{3,19},{19,3},{4,20},{20... | collective-permute-start | bytes 135176 | tf_op jit(solution)/shard_map/ppermute | solution.py:613
  10.3 1.2 %collective-permute-start.4 = (bf16[12,16,128]{2,1,0:T(8,128)(2,1)S(1)}, bf16[12,16,128]{2,1,0:T(8,128)(2,1)S(1)}, u32[]{:S(2)}, u32[]{:S(2)}) collective-permute-start(bf16[12,16,128]{2,1,0:T(8,128)(2,1)S(1)} %get-tuple-element.28), channel_id=1, source_target_pairs={{0,1},{1,0},{2,3},{3,2},{4,5},{5,4},{6,7},{7,6},{8,9},{9,8},{10,11... | collective-permute-start | bytes 147464 | tf_op jit(solution)/shard_map/ppermute | solution.py:621
  11.5 0.5 %collective-permute-start.5 = (bf16[9,16,128]{2,1,0:T(8,128)(2,1)S(1)}, bf16[9,16,128]{2,1,0:T(8,128)(2,1)S(1)}, u32[]{:S(2)}, u32[]{:S(2)}) collective-permute-start(bf16[9,16,128]{2,1,0:T(8,128)(2,1)S(1)} %get-tuple-element.29), channel_id=1, source_target_pairs={{0,17},{1,16},{16,1},{17,0},{2,19},{3,18},{18,3},{19,2},{4,21},{5,... | collective-permute-start | bytes 110600 | tf_op jit(solution)/shard_map/ppermute | solution.py:622
  12.1 1.2 %first.1.refs_4_.refs_6_ = f32[6,96,64]{2,1,0:T(8,128)S(1)} custom-call(bf16[16,64,256]{2,1,0:T(8,128)(2,1)S(1)} %get-tuple-element.18.refs_0_, bf16[16,32,256]{2,1,0:T(8,128)(2,1)S(1)} %get-tuple-element.22.refs_1_, bf16[3504,256]{1,0:T(8,128)(2,1)S(1)} %stage.1.refs_2_.refs_5_.refs_8_), custom_call_target="tpu_custom_call" | custom-call | flops 419954688 | bytes 2727936 | tf_op jit(solution)/shard_map/first/pallas_call | solution.py:547
  13.3 0.0 collective-permute-done.2.refs_2_.refs_4_
  13.3 0.0 collective-permute-done.3.refs_3_.refs_5_
  13.3 1.1 %near.1 = (f32[3,96,64]{2,1,0:T(8,128)S(1)}, bf16[96,128]{1,0:T(8,128)(2,1)S(1)}) custom-call(bf16[16,64,256]{2,1,0:T(8,128)(2,1)S(1)} %get-tuple-element.18.refs_0_, bf16[16,32,256]{2,1,0:T(8,128)(2,1)S(1)} %get-tuple-element.22.refs_1_, bf16[480,128]{1,0:T(8,128)(2,1)S(1)} %collective-permute-done.2.refs_2_.refs_4_, ...), custom_call_target="tpu_custom_call" | custom-call | flops 209977344 | bytes 2994176 | tf_op jit(solution)/shard_map/near/pallas_call | solution.py:547
  14.4 0.9 %collective-permute-start.6 = (bf16[96,128]{1,0:T(8,128)(2,1)S(1)}, bf16[96,128]{1,0:T(8,128)(2,1)S(1)}, u32[]{:S(2)}, u32[]{:S(2)}) collective-permute-start(bf16[96,128]{1,0:T(8,128)(2,1)S(1)} %get-tuple-element.30), channel_id=1, source_target_pairs={{0,16},{16,0},{1,17},{17,1},{2,18},{18,2},{3,19},{19,3},{4,20},{20... | collective-permute-start | bytes 73736 | tf_op jit(solution)/shard_map/ppermute | solution.py:636
  15.4 0.0 collective-permute-done.5.refs_10_
  15.4 0.0 collective-permute-done.4.refs_9_
  15.4 2.5 %last.1.own = f32[6,4,16,64]{3,2,1,0:T(8,128)S(1)} custom-call(bf16[16,64,256]{2,1,0:T(8,128)(2,1)S(1)} %get-tuple-element.18.refs_0_, bf16[16,32,256]{2,1,0:T(8,128)(2,1)S(1)} %get-tuple-element.22.refs_1_, bf16[8,32,128]{2,1,0:T(8,128)(2,1)S(1)} %get-tuple-element.23.refs_2_, bf16[4,32,128]{2,1,0:T(8,128)(2,1)S(1)} %get-tuple-element.24.refs_3_, ...), custom_call_target="tpu_custom_call" | custom-call | flops 699924480 | bytes 3252224 | tf_op jit(solution)/shard_map/last/pallas_call | solution.py:547
  17.9 0.0 collective-permute-done.6.got
  17.9 0.8 %add.1 = f32[6,4,16,64]{3,2,1,0:T(8,128)} custom-call(f32[6,4,16,64]{3,2,1,0:T(8,128)S(1)} %last.1.own, bf16[96,128]{1,0:T(8,128)(2,1)S(1)} %collective-permute-done.6.got), custom_call_target="tpu_custom_call" | custom-call | bytes 221184 | tf_op jit(solution)/shard_map/add/pallas_call | solution.py:547
  (1 shorter events, 0.0 us)
Async XLA Ops:
  1.2 7.7 %collective-permute-start = (bf16[176,256]{1,0:T(8,128)(2,1)S(1)}, bf16[176,256]{1,0:T(8,128)(2,1)S(1)}, u32[]{:S(2)}, u32[]{:S(2)}) collective-permute-start(bf16[176,256]{1,0:T(8,128)(2,1)S(1)} %get-tuple-element.19), channel_id=1, source_target_pairs={{0,2},{2,0},{4,6},{6,4},{8,10},{10,8},{12,14},{14,12},{1,3},{3,1},... | collective-permute-start | bytes 270344 | tf_op jit(solution)/shard_map/ppermute | solution.py:593
  1.3 7.6 %collective-permute-start.1 = (bf16[176,256]{1,0:T(8,128)(2,1)S(1)}, bf16[176,256]{1,0:T(8,128)(2,1)S(1)}, u32[]{:S(2)}, u32[]{:S(2)}) collective-permute-start(bf16[176,256]{1,0:T(8,128)(2,1)S(1)} %get-tuple-element.20), channel_id=1, source_target_pairs={{2,4},{6,8},{10,12},{4,2},{8,6},{12,10},{3,5},{7,9},{11,13},{5,3},... | collective-permute-start | bytes 270344 | tf_op jit(solution)/shard_map/ppermute | solution.py:592
  6.2 7.1 %collective-permute-start.2 = (bf16[480,128]{1,0:T(8,128)(2,1)S(1)}, bf16[480,128]{1,0:T(8,128)(2,1)S(1)}, u32[]{:S(2)}, u32[]{:S(2)}) collective-permute-start(bf16[480,128]{1,0:T(8,128)(2,1)S(1)} %get-tuple-element.25), channel_id=1, source_target_pairs={{0,16},{16,0},{1,17},{17,1},{2,18},{18,2},{3,19},{19,3},{4,20},{20... | collective-permute-start | bytes 368648 | tf_op jit(solution)/shard_map/ppermute | solution.py:604
  9.4 4.0 %collective-permute-start.3 = (bf16[176,128]{1,0:T(8,128)(2,1)S(1)}, bf16[176,128]{1,0:T(8,128)(2,1)S(1)}, u32[]{:S(2)}, u32[]{:S(2)}) collective-permute-start(bf16[176,128]{1,0:T(8,128)(2,1)S(1)} %get-tuple-element.26), channel_id=1, source_target_pairs={{0,16},{16,0},{1,17},{17,1},{2,18},{18,2},{3,19},{19,3},{4,20},{20... | collective-permute-start | bytes 135176 | tf_op jit(solution)/shard_map/ppermute | solution.py:613
  10.3 5.1 %collective-permute-start.4 = (bf16[12,16,128]{2,1,0:T(8,128)(2,1)S(1)}, bf16[12,16,128]{2,1,0:T(8,128)(2,1)S(1)}, u32[]{:S(2)}, u32[]{:S(2)}) collective-permute-start(bf16[12,16,128]{2,1,0:T(8,128)(2,1)S(1)} %get-tuple-element.28), channel_id=1, source_target_pairs={{0,1},{1,0},{2,3},{3,2},{4,5},{5,4},{6,7},{7,6},{8,9},{9,8},{10,11... | collective-permute-start | bytes 147464 | tf_op jit(solution)/shard_map/ppermute | solution.py:621
  11.5 3.9 %collective-permute-start.5 = (bf16[9,16,128]{2,1,0:T(8,128)(2,1)S(1)}, bf16[9,16,128]{2,1,0:T(8,128)(2,1)S(1)}, u32[]{:S(2)}, u32[]{:S(2)}) collective-permute-start(bf16[9,16,128]{2,1,0:T(8,128)(2,1)S(1)} %get-tuple-element.29), channel_id=1, source_target_pairs={{0,17},{1,16},{16,1},{17,0},{2,19},{3,18},{18,3},{19,2},{4,21},{5,... | collective-permute-start | bytes 110600 | tf_op jit(solution)/shard_map/ppermute | solution.py:622
  14.4 3.4 %collective-permute-start.6 = (bf16[96,128]{1,0:T(8,128)(2,1)S(1)}, bf16[96,128]{1,0:T(8,128)(2,1)S(1)}, u32[]{:S(2)}, u32[]{:S(2)}) collective-permute-start(bf16[96,128]{1,0:T(8,128)(2,1)S(1)} %get-tuple-element.30), channel_id=1, source_target_pairs={{0,16},{16,0},{1,17},{17,1},{2,18},{18,2},{3,19},{19,3},{4,20},{20... | collective-permute-start | bytes 73736 | tf_op jit(solution)/shard_map/ppermute | solution.py:636

commit v5 on v3

--- a/solution.py
+++ b/solution.py
@@ -153,38 +153,53 @@
     n_rows = 6 * (rows // 4)
     half_rows = n_rows // 2
     rest = jnp.zeros((8, 128), F32)
-    for tile in range(cols // 128):
-        lanes = slice(tile * 128, tile * 128 + 128)
-        for at in range(0, ext, 16):
-            blocks = load(at, lanes)
-            if at == rows + HALO:
-                blocks = [block[0:8] for block in blocks]
-            for z, smooth, slope in z_filter(blocks, count):
+    wy = get("wy")
+
+    def z_filters(first, n):
+        for tile in range(cols // 128):
+            lanes = slice(tile * 128, tile * 128 + 128)
+            for at in range(0, ext, 16):
+                blocks = load(at, lanes, first, first + n + 2 * R)
                 if at == rows + HALO:
-                    smooth = jnp.concatenate([smooth, rest], axis=0)
-                    slope = jnp.concatenate([slope, rest], axis=0)
-                zf[z, at : at + 16, lanes] = smooth.astype(BF16)
-                zf[z, ext + at : ext + at + 16, lanes] = slope.astype(BF16)
-    wy = get("wy")
-    for z in range(count):
-        out = jnp.dot(wy, zf[z], preferred_element_type=F32).astype(BF16)
-        planes[0, z] = out[0:gr]
-        planes[1, z] = out[gr : 2 * gr]
-        planes[2, z] = out[2 * gr :]
-    group = 4 if count % 4 == 0 else count
-    for at in range(0, count, group):
+                    blocks = [block[0:8] for block in blocks]
+                for z, smooth, slope in z_filter(blocks, n):
+                    if at == rows + HALO:
+                        smooth = jnp.concatenate([smooth, rest], axis=0)
+                        slope = jnp.concatenate([slope, rest], axis=0)
+                    zf[first + z, at : at + 16, lanes] = smooth.astype(BF16)
+                    zf[first + z, ext + at : ext + at + 16, lanes] = slope.astype(BF16)
+
+    def y_filters(first, n):
+        for z in range(first, first + n):
+            out = jnp.dot(wy, zf[z], preferred_element_type=F32).astype(BF16)
+            planes[0, z] = out[0:gr]
+            planes[1, z] = out[gr : 2 * gr]
+            planes[2, z] = out[2 * gr :]
+
+    def x_filters(first, n):
         grads = []
         for f, name in enumerate(("wxd", "wxs", "wxs")):
-            part = planes[f, at : at + group].reshape(group * gr, cols)
+            part = planes[f, first : first + n].reshape(n * gr, cols)
             out = jnp.dot(part, get(name), preferred_element_type=F32)
-            grads.append(out.astype(BF16).reshape(group, gr, cols))
+            grads.append(out.astype(BF16).reshape(n, gr, cols))
         for c, (a, b) in enumerate(pair_table):
-            prod[at : at + group, c * gr : (c + 1) * gr] = grads[a] * grads[b]
-    for z in range(count):
-        for half in range(2):
-            part = prod[z, half * 3 * gr : (half + 1) * 3 * gr]
-            out = jnp.dot(ysm, part, preferred_element_type=F32)
-            sm[z, half * half_rows : (half + 1) * half_rows] = out.astype(BF16)
+            prod[first : first + n, c * gr : (c + 1) * gr] = grads[a] * grads[b]
+
+    def y_smoothing(first, n):
+        for z in range(first, first + n):
+            for half in range(2):
+                part = prod[z, half * 3 * gr : (half + 1) * 3 * gr]
+                out = jnp.dot(ysm, part, preferred_element_type=F32)
+                sm[z, half * half_rows : (half + 1) * half_rows] = out.astype(BF16)
+
+    n_group = -(-count // GROUP)
+    ends = [count * i // n_group for i in range(n_group + 1)]
+    stages = (z_filters, y_filters, x_filters, y_smoothing)
+    for step in range(n_group + len(stages) - 1):
+        for k, stage in enumerate(stages):
+            i = step - k
+            if 0 <= i < n_group:
+                stage(ends[i], ends[i + 1] - ends[i])
     out = jnp.dot(
         sm[...].reshape(count * n_rows, cols), get("xsm"), preferred_element_type=F32
     )
@@ -210,13 +225,13 @@
     return jnp.where(full == packed + z * (HALO - NEED) + first, 1.0, 0.0).astype(BF16)
 
 
-def load_kernel(vol, s1, s2, vol_out, top, bottom, sems):
+def load_kernel(vol, s1, s2, vol_out, sems):
     depth, rows, cols = vol.shape
     odd = lax.rem(lax.axis_index("row"), 2) == 1
+    parts = (slice(0, HALO), slice(rows - HALO, rows), slice(HALO, rows - HALO))
     copies = [
-        pltpu.make_async_copy(vol.at[:, 0:HALO, :], top, sems.at[0]),
-        pltpu.make_async_copy(vol.at[:, rows - HALO : rows, :], bottom, sems.at[1]),
-        pltpu.make_async_copy(vol, vol_out, sems.at[2]),
+        pltpu.make_async_copy(vol.at[:, part, :], vol_out.at[:, part, :], sems.at[i])
+        for i, part in enumerate(parts)
     ]
     for copy in copies:
         copy.start()
@@ -224,10 +239,10 @@
     copies[0].wait()
     copies[1].wait()
     to_before = jnp.dot(
-        first_rows, top[...].reshape(depth * HALO, cols), preferred_element_type=F32
+        first_rows, vol_out[:, 0:HALO].reshape(depth * HALO, cols), preferred_element_type=F32
     ).astype(BF16)
     to_after = jnp.dot(
-        last_rows, bottom[...].reshape(depth * HALO, cols), preferred_element_type=F32
+        last_rows, vol_out[:, rows - HALO :].reshape(depth * HALO, cols), preferred_element_type=F32
     ).astype(BF16)
     s1[...] = jnp.where(odd, to_before, to_after)
     s2[...] = jnp.where(odd, to_after, to_before)
@@ -330,6 +345,7 @@
 
 
 FIRST = 7
+GROUP = 3
 EDGE = R
 LAST = 6
 
@@ -340,7 +356,7 @@
     ysm = row_mask(get, n_row, rows, rows + 16, rows // 4)
     base = jnp.where(lax.axis_index("gz") == 0, depth - EDGE - FIRST - R, 0)
     layer = block_loader(vol, yud, rows)
-    load = lambda at, lanes: [layer(base + k, at, lanes) for k in range(FIRST + 2 * R)]
+    load = lambda at, lanes, lo, hi: [layer(base + k, at, lanes) for k in range(lo, hi)]
     layers_to_sums(get, ysm, load, FIRST, (rows, cols), u_ref, *scratch)
 
 
@@ -360,13 +376,18 @@
     start = jnp.where(low, depth - R, 0)
     outer = jnp.where(low, depth - 2 * R, R)
 
-    def load(at, lanes):
-        beyond = [zext[k, at : at + 16, lanes].astype(F32) for k in range(R)]
-        inner = [layer(outer + k, at, lanes) for k in range(R)]
-        middle = [layer(start + k, at, lanes) for k in range(R)]
-        before = [jnp.where(low, inner[k], beyond[k]) for k in range(R)]
-        after = [jnp.where(low, beyond[k], inner[k]) for k in range(R)]
-        return before + middle + after
+    def load(at, lanes, lo, hi):
+        out = []
+        for k in range(lo, hi):
+            if R <= k < 2 * R:
+                out.append(layer(start + k - R, at, lanes))
+                continue
+            i = k % R
+            inner = layer(outer + i, at, lanes)
+            beyond = zext[i, at : at + 16, lanes].astype(F32)
+            first, second = (inner, beyond) if k < R else (beyond, inner)
+            out.append(jnp.where(low, first, second))
+        return out
 
     layers_to_sums(get, ysm, load, EDGE, (rows, cols), u_ref, *scratch)
     sends = []
@@ -393,9 +414,9 @@
     before_on = jnp.where(low, 0.0, 1.0)
     after_on = jnp.where(low, 1.0, 0.0)
 
-    def load(at, lanes):
+    def load(at, lanes, lo, hi):
         out = []
-        for k in range(LAST + 2 * R):
+        for k in range(lo, hi):
             block = layer(jnp.clip(base + k, 0, depth - 1), at, lanes)
             if k < R:
                 block = block * before_on
@@ -584,7 +605,7 @@
     s1, s2, vol = call(
         load_kernel,
         [bf16(depth * NEED, cols)] * 2 + [bf16(depth, rows, cols)],
-        [volume], [pltpu.VMEM((depth, HALO, cols), BF16)] * 2 + [dma((3,))], "load", n_hbm=1,
+        [volume], [dma((3,))], "load", n_hbm=1,
     )
     inner = [(i, i + 1) for i in range(1, n_row - 1, 2)]
     inner = inner + [(j, i) for i, j in inner]

time: 19.1 us -> 18.9 us (0.990)
  transfers between devices with their start and end apart: 7 -> 7, of which waited for: 0 -> 0; matrix products, arithmetic and copies ran while one was open for 8% -> 8% of each run, Pallas kernels for 31% -> 30%
where the time goes in v5:
time: 18.9 us; the launch traced here: 18.8 us
  starting transfers between devices  9.58 us (51%)
  Pallas kernels  7.61 us (40%)
  local copies, waits for them, and re-layouts  1.48 us (8%)
    pallas_call x8, Pallas kernels, call(): pl.pallas_call(body, out_shape=list(outs), in_specs=[hbm] * n_hbm + [vmem...  7.61 us
    ppermute x1, starting transfers between devices, per_device(): r2 = lax.ppermute(s2, 'row', inner)  4.55 us
    unnamed x1, local copies, waits for them, and re-layouts  1.48 us
    ppermute x1, starting transfers between devices, per_device(): zown = lax.ppermute(zmsg, 'gz', swap)  1.27 us
    ppermute x1, starting transfers between devices, per_device(): xs.append(lax.ppermute(messages[side], 'col', line))  1.25 us
    ppermute x1, starting transfers between devices, per_device(): zcorner = lax.ppermute(zcmsg, 'gz', swap)  0.93 us
    ppermute x1, starting transfers between devices, per_device(): sums = lax.ppermute(send, 'gz', swap)  0.92 us
    ppermute x1, starting transfers between devices, per_device(): zxs.append(lax.ppermute(messages[n_side + side], ('gz', 'col'), both))  0.54 us
  transfers between devices with their start and end apart: 7, of which 0 were waited for; matrix products, arithmetic and copies ran while one was open for 8% of the time, Pallas kernels for 30%

profile of v5, /device:TPU:1, one launch (start us, length us, event | category | flops | bytes accessed | tf_op | source)
XLA Modules:
  0.0 18.8 jit_solution(7860513743408894376)
XLA Ops:
  0.0 1.2 %load.1 = (bf16[176,256]{1,0:T(8,128)(2,1)S(1)}, bf16[176,256]{1,0:T(8,128)(2,1)S(1)}, bf16[16,64,256]{2,1,0:T(8,128)(2,1)S(1)}) custom-call(bf16[16,64,256]{2,1,0:T(8,128)(2,1)} %vol.1), custom_call_target="tpu_custom_call" | custom-call | bytes 1228800 | tf_op jit(solution)/shard_map/load/pallas_call | solution.py:567
  1.2 0.1 collective-permute-start
  1.3 4.6 %collective-permute-start.1 = (bf16[176,256]{1,0:T(8,128)(2,1)S(1)}, bf16[176,256]{1,0:T(8,128)(2,1)S(1)}, u32[]{:S(2)}, u32[]{:S(2)}) collective-permute-start(bf16[176,256]{1,0:T(8,128)(2,1)S(1)} %get-tuple-element.20), channel_id=1, source_target_pairs={{2,4},{6,8},{10,12},{4,2},{8,6},{12,10},{3,5},{7,9},{11,13},{5,3},... | collective-permute-start | bytes 270344 | tf_op jit(solution)/shard_map/ppermute | solution.py:612
  5.9 0.3 %edges.1 = (bf16[8,32,128]{2,1,0:T(8,128)(2,1)S(1)}, bf16[480,128]{1,0:T(8,128)(2,1)S(1)}, bf16[8,16,128]{2,1,0:T(8,128)(2,1)S(1)}) custom-call(bf16[16,64,256]{2,1,0:T(8,128)(2,1)S(1)} %get-tuple-element.18.refs_0_), custom_call_target="tpu_custom_call" | custom-call | bytes 745472 | tf_op jit(solution)/shard_map/edges/pallas_call | solution.py:567
  6.2 1.3 %collective-permute-start.2 = (bf16[480,128]{1,0:T(8,128)(2,1)S(1)}, bf16[480,128]{1,0:T(8,128)(2,1)S(1)}, u32[]{:S(2)}, u32[]{:S(2)}) collective-permute-start(bf16[480,128]{1,0:T(8,128)(2,1)S(1)} %get-tuple-element.25), channel_id=1, source_target_pairs={{0,16},{16,0},{1,17},{17,1},{2,18},{18,2},{3,19},{19,3},{4,20},{20... | collective-permute-start | bytes 368648 | tf_op jit(solution)/shard_map/ppermute | solution.py:624
  7.5 1.5 %copy.6.w = bf16[3504,256]{1,0:T(8,128)(2,1)S(1)} copy(bf16[3504,256]{1,0:T(8,128)(2,1)} %constant.2.clone) | data formatting | bytes 3588096
  9.0 0.0 collective-permute-done.refs_0_
  9.0 0.0 collective-permute-done.1.refs_1_
  9.0 0.4 %pack.1 = (bf16[16,32,256]{2,1,0:T(8,128)(2,1)S(1)}, bf16[4,32,128]{2,1,0:T(8,128)(2,1)S(1)}, bf16[176,128]{1,0:T(8,128)(2,1)S(1)}, bf16[12,16,128]{2,1,0:T(8,128)(2,1)S(1)}, bf16[9,16,128]{2,1,0:T(8,128)(2,1)S(1)}) custom-call(bf16[176,256]{1,0:T(8,128)(2,1)S(1)} %collective-permute-done.refs_0_, bf16[176,256]{1,0:T(8,128)(2,1)S(1)} %collective-permute-done.1.refs_1_, ...), custom_call_target="tpu_custom_call" | custom-call | bytes 2433024 | tf_op jit(solution)/shard_map/pack/pallas_call | solution.py:567
  9.4 0.9 %collective-permute-start.3 = (bf16[176,128]{1,0:T(8,128)(2,1)S(1)}, bf16[176,128]{1,0:T(8,128)(2,1)S(1)}, u32[]{:S(2)}, u32[]{:S(2)}) collective-permute-start(bf16[176,128]{1,0:T(8,128)(2,1)S(1)} %get-tuple-element.26), channel_id=1, source_target_pairs={{0,16},{16,0},{1,17},{17,1},{2,18},{18,2},{3,19},{19,3},{4,20},{20... | collective-permute-start | bytes 135176 | tf_op jit(solution)/shard_map/ppermute | solution.py:633
  10.3 1.2 %collective-permute-start.4 = (bf16[12,16,128]{2,1,0:T(8,128)(2,1)S(1)}, bf16[12,16,128]{2,1,0:T(8,128)(2,1)S(1)}, u32[]{:S(2)}, u32[]{:S(2)}) collective-permute-start(bf16[12,16,128]{2,1,0:T(8,128)(2,1)S(1)} %get-tuple-element.28), channel_id=1, source_target_pairs={{0,1},{1,0},{2,3},{3,2},{4,5},{5,4},{6,7},{7,6},{8,9},{9,8},{10,11... | collective-permute-start | bytes 147464 | tf_op jit(solution)/shard_map/ppermute | solution.py:641
  11.5 0.5 %collective-permute-start.5 = (bf16[9,16,128]{2,1,0:T(8,128)(2,1)S(1)}, bf16[9,16,128]{2,1,0:T(8,128)(2,1)S(1)}, u32[]{:S(2)}, u32[]{:S(2)}) collective-permute-start(bf16[9,16,128]{2,1,0:T(8,128)(2,1)S(1)} %get-tuple-element.29), channel_id=1, source_target_pairs={{0,17},{1,16},{16,1},{17,0},{2,19},{3,18},{18,3},{19,2},{4,21},{5,... | collective-permute-start | bytes 110600 | tf_op jit(solution)/shard_map/ppermute | solution.py:642
  12.1 1.5 %first.1.refs_4_.refs_6_ = f32[7,96,64]{2,1,0:T(8,128)S(1)} custom-call(bf16[16,64,256]{2,1,0:T(8,128)(2,1)S(1)} %get-tuple-element.18.refs_0_, bf16[16,32,256]{2,1,0:T(8,128)(2,1)S(1)} %get-tuple-element.22.refs_1_, bf16[3504,256]{1,0:T(8,128)(2,1)S(1)} %stage.1.refs_2_.refs_5_.refs_8_), custom_call_target="tpu_custom_call" | custom-call | flops 489947136 | bytes 2752512 | tf_op jit(solution)/shard_map/first/pallas_call | solution.py:567
  13.5 0.0 collective-permute-done.2.refs_2_.refs_4_
  13.5 0.0 collective-permute-done.3.refs_3_.refs_5_
  13.6 1.1 %near.1 = (f32[3,96,64]{2,1,0:T(8,128)S(1)}, bf16[96,128]{1,0:T(8,128)(2,1)S(1)}) custom-call(bf16[16,64,256]{2,1,0:T(8,128)(2,1)S(1)} %get-tuple-element.18.refs_0_, bf16[16,32,256]{2,1,0:T(8,128)(2,1)S(1)} %get-tuple-element.22.refs_1_, bf16[480,128]{1,0:T(8,128)(2,1)S(1)} %collective-permute-done.2.refs_2_.refs_4_, ...), custom_call_target="tpu_custom_call" | custom-call | flops 209977344 | bytes 3018752 | tf_op jit(solution)/shard_map/near/pallas_call | solution.py:567
  14.7 0.9 %collective-permute-start.6 = (bf16[96,128]{1,0:T(8,128)(2,1)S(1)}, bf16[96,128]{1,0:T(8,128)(2,1)S(1)}, u32[]{:S(2)}, u32[]{:S(2)}) collective-permute-start(bf16[96,128]{1,0:T(8,128)(2,1)S(1)} %get-tuple-element.30), channel_id=1, source_target_pairs={{0,16},{16,0},{1,17},{17,1},{2,18},{18,2},{3,19},{19,3},{4,20},{20... | collective-permute-start | bytes 73736 | tf_op jit(solution)/shard_map/ppermute | solution.py:656
  15.6 0.0 collective-permute-done.5.refs_10_
  15.6 0.0 collective-permute-done.4.refs_9_
  15.6 2.4 %last.1.own = f32[6,4,16,64]{3,2,1,0:T(8,128)S(1)} custom-call(bf16[16,64,256]{2,1,0:T(8,128)(2,1)S(1)} %get-tuple-element.18.refs_0_, bf16[16,32,256]{2,1,0:T(8,128)(2,1)S(1)} %get-tuple-element.22.refs_1_, bf16[8,32,128]{2,1,0:T(8,128)(2,1)S(1)} %get-tuple-element.23.refs_2_, bf16[4,32,128]{2,1,0:T(8,128)(2,1)S(1)} %get-tuple-element.24.refs_3_, ...), custom_call_target="tpu_custom_call" | custom-call | flops 629932032 | bytes 3276800 | tf_op jit(solution)/shard_map/last/pallas_call | solution.py:567
  18.0 0.0 collective-permute-done.6.got
  18.0 0.8 %add.1 = f32[6,4,16,64]{3,2,1,0:T(8,128)} custom-call(f32[6,4,16,64]{3,2,1,0:T(8,128)S(1)} %last.1.own, bf16[96,128]{1,0:T(8,128)(2,1)S(1)} %collective-permute-done.6.got), custom_call_target="tpu_custom_call" | custom-call | bytes 221184 | tf_op jit(solution)/shard_map/add/pallas_call | solution.py:567
  (1 shorter events, 0.0 us)
Async XLA Ops:
  1.2 7.7 %collective-permute-start = (bf16[176,256]{1,0:T(8,128)(2,1)S(1)}, bf16[176,256]{1,0:T(8,128)(2,1)S(1)}, u32[]{:S(2)}, u32[]{:S(2)}) collective-permute-start(bf16[176,256]{1,0:T(8,128)(2,1)S(1)} %get-tuple-element.19), channel_id=1, source_target_pairs={{0,2},{2,0},{4,6},{6,4},{8,10},{10,8},{12,14},{14,12},{1,3},{3,1},... | collective-permute-start | bytes 270344 | tf_op jit(solution)/shard_map/ppermute | solution.py:613
  1.3 7.6 %collective-permute-start.1 = (bf16[176,256]{1,0:T(8,128)(2,1)S(1)}, bf16[176,256]{1,0:T(8,128)(2,1)S(1)}, u32[]{:S(2)}, u32[]{:S(2)}) collective-permute-start(bf16[176,256]{1,0:T(8,128)(2,1)S(1)} %get-tuple-element.20), channel_id=1, source_target_pairs={{2,4},{6,8},{10,12},{4,2},{8,6},{12,10},{3,5},{7,9},{11,13},{5,3},... | collective-permute-start | bytes 270344 | tf_op jit(solution)/shard_map/ppermute | solution.py:612
  6.2 7.3 %collective-permute-start.2 = (bf16[480,128]{1,0:T(8,128)(2,1)S(1)}, bf16[480,128]{1,0:T(8,128)(2,1)S(1)}, u32[]{:S(2)}, u32[]{:S(2)}) collective-permute-start(bf16[480,128]{1,0:T(8,128)(2,1)S(1)} %get-tuple-element.25), channel_id=1, source_target_pairs={{0,16},{16,0},{1,17},{17,1},{2,18},{18,2},{3,19},{19,3},{4,20},{20... | collective-permute-start | bytes 368648 | tf_op jit(solution)/shard_map/ppermute | solution.py:624
  9.4 4.2 %collective-permute-start.3 = (bf16[176,128]{1,0:T(8,128)(2,1)S(1)}, bf16[176,128]{1,0:T(8,128)(2,1)S(1)}, u32[]{:S(2)}, u32[]{:S(2)}) collective-permute-start(bf16[176,128]{1,0:T(8,128)(2,1)S(1)} %get-tuple-element.26), channel_id=1, source_target_pairs={{0,16},{16,0},{1,17},{17,1},{2,18},{18,2},{3,19},{19,3},{4,20},{20... | collective-permute-start | bytes 135176 | tf_op jit(solution)/shard_map/ppermute | solution.py:633
  10.3 5.3 %collective-permute-start.4 = (bf16[12,16,128]{2,1,0:T(8,128)(2,1)S(1)}, bf16[12,16,128]{2,1,0:T(8,128)(2,1)S(1)}, u32[]{:S(2)}, u32[]{:S(2)}) collective-permute-start(bf16[12,16,128]{2,1,0:T(8,128)(2,1)S(1)} %get-tuple-element.28), channel_id=1, source_target_pairs={{0,1},{1,0},{2,3},{3,2},{4,5},{5,4},{6,7},{7,6},{8,9},{9,8},{10,11... | collective-permute-start | bytes 147464 | tf_op jit(solution)/shard_map/ppermute | solution.py:641
  11.5 4.1 %collective-permute-start.5 = (bf16[9,16,128]{2,1,0:T(8,128)(2,1)S(1)}, bf16[9,16,128]{2,1,0:T(8,128)(2,1)S(1)}, u32[]{:S(2)}, u32[]{:S(2)}) collective-permute-start(bf16[9,16,128]{2,1,0:T(8,128)(2,1)S(1)} %get-tuple-element.29), channel_id=1, source_target_pairs={{0,17},{1,16},{16,1},{17,0},{2,19},{3,18},{18,3},{19,2},{4,21},{5,... | collective-permute-start | bytes 110600 | tf_op jit(solution)/shard_map/ppermute | solution.py:642
  14.7 3.3 %collective-permute-start.6 = (bf16[96,128]{1,0:T(8,128)(2,1)S(1)}, bf16[96,128]{1,0:T(8,128)(2,1)S(1)}, u32[]{:S(2)}, u32[]{:S(2)}) collective-permute-start(bf16[96,128]{1,0:T(8,128)(2,1)S(1)} %get-tuple-element.30), channel_id=1, source_target_pairs={{0,16},{16,0},{1,17},{17,1},{2,18},{18,2},{3,19},{19,3},{4,20},{20... | collective-permute-start | bytes 73736 | tf_op jit(solution)/shard_map/ppermute | solution.py:656

commit v6 on v5

--- a/solution.py
+++ b/solution.py
@@ -46,12 +46,14 @@
     grad_rows = rows + 16
     far = 10**6
     y_in = np.arange(ext) - HALO
+    y_in[0:HALO] = far
+    y_in[0:NEED] = np.arange(-NEED, 0)
     y_out = np.arange(grad_rows) - R2
     smooth_y = band(SMOOTH_D, y_in, y_out).T
     slope_y = band(SLOPE_D, y_in, y_out).T
     zero = np.zeros_like(smooth_y)
     wy = np.block([[smooth_y, zero], [slope_y, zero], [zero, smooth_y]])
-    order = np.concatenate([np.arange(rows), np.arange(HALO) - HALO, rows + np.arange(HALO)]) + HALO
+    order = np.concatenate([np.arange(rows) + HALO, np.arange(HALO), rows + HALO + np.arange(HALO)])
     x_all = np.arange(cols)
     slot_in = np.full(SLOTS, far)
     slot_in[0:8] = cols + np.arange(8)
@@ -69,7 +71,7 @@
     xs_edge = band(SMOOTH_I, slot_out, 4 * coarse_edge)
     ys = band(SMOOTH_I, y_out, 4 * np.arange(rows // 4)).T
     zs = band(SMOOTH_I, np.arange(depth), 4 * (np.arange(depth // 4 + 4) - 2))
-    place = np.zeros((8, 128))
+    place = np.zeros((8, quarter))
     for j in range(5):
         place[j, coarse_edge[j]] = 1.0
     own_z = 4 * np.arange(depth // 4)
@@ -77,42 +79,39 @@
         np.einsum("zq,jx->zjqx", band(SMOOTH_I, np.arange(depth + 8) + first, own_z), place)
         for first in (0, -8)
     ]
-    g = [t.reshape((depth + 8) * 8, len(own_z) * 128) for t in g]
+    g = [t.reshape((depth + 8) * 8, len(own_z) * quarter) for t in g]
     packed = np.arange(depth * NEED)
-    above = np.zeros((depth * HALO, depth * NEED))
-    above[packed + packed // NEED * (HALO - NEED) + HALO - NEED, packed] = 1.0
-    below = np.zeros((depth * HALO, depth * NEED))
-    below[packed + packed // NEED * (HALO - NEED), packed] = 1.0
-    used = 2 * R + 13
+    spread = np.zeros((depth * HALO, depth * NEED))
+    spread[packed + packed // NEED * (HALO - NEED), packed] = 1.0
+    used = NEED + 8
     packed = np.arange(R * used)
     corner = np.zeros((64, R * 2 * HALO))
-    corner[packed, packed + packed // used * (2 * HALO - used) + HALO - NEED] = 1.0
-    parts = {
-        "above": above,
-        "below": below,
-        "corner": corner,
-        "corner_back": corner.T,
-        "wy": wy,
-        "wy_strip": np.concatenate([smooth_y, slope_y])[:, order],
-        "wy_strip_slope": smooth_y[:, order],
-        "wxd": band(SLOPE_D, x_all, x_all),
-        "wxs": band(SMOOTH_D, x_all, x_all),
-        "bdd": np.kron(eye8, band(SLOPE_D, slot_in, slot_out)),
-        "bds": np.kron(eye8, band(SMOOTH_D, slot_in, slot_out)),
-        "ysm": np.kron(np.eye(3), ys),
-        "xsm": band(SMOOTH_I, inner, 4 * np.arange(quarter)),
-        "bdx": np.kron(eye8, xs_edge),
-        "g_low0": g[0][:, 0:256],
-        "g_low1": g[0][:, 256:512],
-        "g_high0": g[1][:, 0:256],
-        "g_high1": g[1][:, 256:512],
-    }
+    below = (packed % used >= NEED) * (HALO - NEED)
+    corner[packed, packed + packed // used * (2 * HALO - used) + below] = 1.0
+    groups = [
+        {"spread": spread},
+        {"corner": corner, "corner_back": corner.T},
+        {"wy": wy},
+        {
+            "wy_strip": np.concatenate([smooth_y, slope_y])[:, order],
+            "wy_strip_slope": smooth_y[:, order],
+        },
+        {"wxd": band(SLOPE_D, x_all, x_all)},
+        {"wxs": band(SMOOTH_D, x_all, x_all)},
+        {"bdd": np.kron(eye8, band(SLOPE_D, slot_in, slot_out))},
+        {"bds": np.kron(eye8, band(SMOOTH_D, slot_in, slot_out))},
+        {"ysm": np.kron(np.eye(3), ys)},
+        {"xsm": band(SMOOTH_I, inner, 4 * np.arange(quarter)), "bdx": np.kron(eye8, xs_edge)},
+        {"g_low": g[0]},
+        {"g_high": g[1]},
+    ]
     place_of, blocks, at = {}, [], 0
-    for name, part in parts.items():
-        height = -(-part.shape[0] // 16) * 16
+    for group in groups:
+        height = max(-(-part.shape[0] // 16) * 16 for part in group.values())
         block = np.zeros((height, 256), np.float32)
-        block[: part.shape[0], : part.shape[1]] = part
-        place_of[name] = (at, part.shape[0], part.shape[1])
+        for lane, (name, part) in zip((0, 128), group.items()):
+            block[: part.shape[0], lane : lane + part.shape[1]] = part
+            place_of[name] = (at, lane) + part.shape
         blocks.append(block)
         at += height
     return np.concatenate(blocks).astype(ml_dtypes.bfloat16), place_of, zs
@@ -132,8 +131,8 @@
 
 def getter(place_of, w):
     def get(name, width=None):
-        at, height, own_width = place_of[name]
-        return w[at : at + height, 0 : (width or own_width)]
+        at, lane, height, own_width = place_of[name]
+        return w[at : at + height, lane : lane + (width or own_width)]
 
     return get
 
@@ -311,11 +310,11 @@
     odd = lax.rem(lax.axis_index("row"), 2) == 1
     get = getter(place_of, w)
     got1, got2 = r1[...], r2[...]
-    for at, name, part in (
-        (0, "above", jnp.where(odd, got1, got2)),
-        (HALO, "below", jnp.where(odd, got2, got1)),
+    for at, part in (
+        (0, jnp.where(odd, got1, got2)),
+        (HALO, jnp.where(odd, got2, got1)),
     ):
-        out = jnp.dot(get(name), part, preferred_element_type=F32).astype(BF16)
+        out = jnp.dot(get("spread"), part, preferred_element_type=F32).astype(BF16)
         yud[:, at : at + HALO, :] = out.reshape(depth, HALO, cols)
     select = column_select(n_col, cols)
     pairs, quads = depth // 2, depth // 4
@@ -344,10 +343,10 @@
     pass
 
 
-FIRST = 7
-GROUP = 3
+FIRST = 5
+GROUP = 4
 EDGE = R
-LAST = 6
+LAST = 8
 
 
 def first_kernel(place_of, n_row, vol, yud, w, u_ref, *scratch):
@@ -428,16 +427,8 @@
     layers_to_sums(get, ysm, load, LAST, (rows, cols), u_ref, *scratch)
 
 
-def last_kernel(place_of, zs, n_row, n_col, vol, yud, own, halo, zown, zcorner, u1, u2, w,
-                xs, zxs, own_ref, hs, hd, pstrip, u3, *scratch):
-    depth, rows, cols = vol.shape
-    gr = rows + 16
-    quarter_rows, quarter = rows // 4, cols // 4
-    get = getter(place_of, w)
-    gz, col = lax.axis_index("gz"), lax.axis_index("col")
-    low = gz == 0
-    ysm = row_mask(get, n_row, rows, gr, quarter_rows)
-    last_layers(place_of, get, ysm, vol, yud, u3, *scratch)
+def strip_tools(n_col, rows):
+    col = lax.axis_index("col")
     slots = lax.broadcasted_iota(jnp.int32, (SLOTS, 128), 0)
     if n_col == 2:
         keep = ((slots < 8) & (col == 0)) | ((slots >= 21) & (col == 1))
@@ -447,11 +438,6 @@
     def join(part, messages, b):
         sides = [messages[-1][b].astype(F32), messages[0][b].astype(F32)]
         return jnp.where(keep, jnp.concatenate(sides, axis=0), part)
-
-    def from_middle(ref, at, b):
-        rim = jnp.zeros((8, 128), F32)
-        middle = ref[at + 16 * b : at + 16 * (b + 1)].astype(F32)
-        return jnp.concatenate([rim, middle, rim], axis=0)
 
     lanes = lax.broadcasted_iota(jnp.int32, (SLOTS, 128), 1)
 
@@ -467,16 +453,42 @@
             out.append(jnp.where(lanes < rows, left, right))
         return out
 
+    return join, layers_of
+
+
+def beyond_kernel(n_col, rows, zown, zcorner, zxs, out):
+    join, layers_of = strip_tools(n_col, rows)
+
+    def from_middle(ref, at, b):
+        rim = jnp.zeros((8, 128), F32)
+        middle = ref[at + 16 * b : at + 16 * (b + 1)].astype(F32)
+        return jnp.concatenate([rim, middle, rim], axis=0)
+
     n2, n4 = EXTRA // 2, EXTRA // 4
+    layers = layers_of(
+        [join(from_middle(zown, 2 * R * rows, b), zxs, b) for b in range(n2)],
+        [join(from_middle(zcorner, 128, b), zxs, n2 + b) for b in range(n4)],
+    )
+    for k, layer in enumerate(layers):
+        out[k] = layer.astype(BF16)
+
+
+def last_kernel(place_of, zs, n_row, n_col, vol, yud, own, halo, far, u1, u2, w, xs, own_ref,
+                hs, hd, pstrip, u3, *scratch):
+    depth, rows, cols = vol.shape
+    gr = rows + 16
+    quarter_rows, quarter = rows // 4, cols // 4
+    get = getter(place_of, w)
+    gz, col = lax.axis_index("gz"), lax.axis_index("col")
+    low = gz == 0
+    ysm = row_mask(get, n_row, rows, gr, quarter_rows)
+    last_layers(place_of, get, ysm, vol, yud, u3, *scratch)
+    join, layers_of = strip_tools(n_col, rows)
     own_layers = layers_of(
         [join(own[b].astype(F32), xs, b) for b in range(depth // 2)],
         [join(halo[b].astype(F32), xs, depth // 2 + b) for b in range(depth // 4)],
     )
-    at = 2 * R * rows
-    beyond = layers_of(
-        [join(from_middle(zown, at, b), zxs, b) for b in range(n2)],
-        [join(from_middle(zcorner, 128, b), zxs, n2 + b) for b in range(n4)],
-    )
+    beyond = [far[k].astype(F32) for k in range(EXTRA)]
     count = depth + 8
     zero = [jnp.zeros((SLOTS, 128), F32)] * R
     at_low = zero + own_layers + beyond[0:11]
@@ -513,15 +525,13 @@
     u = jnp.dot(jnp.concatenate(smoothed, axis=0), get("bdx"), preferred_element_type=F32)
     n_rows = 6 * quarter_rows
     u = u.astype(BF16)
-    sums = []
-    for name in ("0", "1"):
-        at = jnp.where(low, place_of["g_low" + name][0], place_of["g_high" + name][0])
-        total = None
-        for c in range(n):
-            g = w[pl.ds(pl.multiple_of(at + 64 * c, 16), 64), :]
-            term = jnp.dot(u[n_rows * c : n_rows * (c + 1)], g, preferred_element_type=F32)
-            total = term if total is None else total + term
-        sums += [total[:, 0:quarter], total[:, 128 : 128 + quarter]]
+    at = jnp.where(low, place_of["g_low"][0], place_of["g_high"][0])
+    total = None
+    for c in range(n):
+        g = w[pl.ds(pl.multiple_of(at + 64 * c, 16), 64), :]
+        term = jnp.dot(u[n_rows * c : n_rows * (c + 1)], g, preferred_element_type=F32)
+        total = term if total is None else total + term
+    sums = [total[:, quarter * q : quarter * (q + 1)] for q in range(depth // 4)]
     for q in range(depth // 4):
         total = sums[q]
         for i in range(depth):
@@ -655,17 +665,22 @@
     )
     sums = lax.ppermute(send, "gz", swap)
 
+    (far,) = call(
+        lambda zown, zcorner, *refs: beyond_kernel(
+            n_col, rows, zown, zcorner, refs[:n_side], refs[n_side]
+        ),
+        [bf16(EXTRA, SLOTS, 128)], [zown, zcorner] + zxs, [], "beyond", flops=EDGE * layer_flops,
+    )
+
     def last_body(*refs):
-        head, x_refs, zx_refs = refs[0:9], refs[9 : 9 + n_side], refs[9 + n_side : 9 + 2 * n_side]
-        last_kernel(
-            place_of, zs, n_row, n_col, *head, x_refs, zx_refs, *refs[9 + 2 * n_side :]
-        )
+        head, x_refs, tail = refs[0:8], refs[8 : 8 + n_side], refs[8 + n_side :]
+        last_kernel(place_of, zs, n_row, n_col, *head, x_refs, *tail)
 
     count = depth + 8
     (result,) = call(
         last_body,
         [sds((6, depth // 4, quarter_rows, quarter), F32)],
-        [vol, yud, own, halo, zown, zcorner, u1, u2, w] + xs + zxs,
+        [vol, yud, own, halo, far, u1, u2, w] + xs,
         [
             pltpu.VMEM((count * SLOTS, 128), BF16),
             pltpu.VMEM((count * SLOTS, 128), BF16),

time: 18.9 us -> 19.3 us (1.021)
  starting transfers between devices: 9.58 us -> 10.1 us
    ppermute x1, starting transfers between devices: 1.25 us -> 0.23 us  [per_device(): xs.append(lax.ppermute(messages[side], 'col', line))]
    ppermute x1, starting transfers between devices: 0.54 us -> 1.07 us  [per_device(): zxs.append(lax.ppermute(messages[n_side + side], ('gz', 'col'), both))]
    ppermute x1, starting transfers between devices: 0.92 us -> 1.42 us  [per_device(): sums = lax.ppermute(send, 'gz', swap)]
    ppermute x1, starting transfers between devices: 0.93 us -> 1.42 us  [per_device(): zcorner = lax.ppermute(zcmsg, 'gz', swap)]
    pallas_call x8 -> x9, Pallas kernels: 7.61 us -> 7.65 us  [call(): pl.pallas_call(body, out_shape=list(outs), in_specs=[hbm] * n_hbm + [vmem...]
  transfers between devices with their start and end apart: 7 -> 7, of which waited for: 0 -> 0; matrix products, arithmetic and copies ran while one was open for 8% -> 7% of each run, Pallas kernels for 30% -> 30%
where the time goes in v6:
time: 19.3 us; the launch traced here: 19.1 us
  starting transfers between devices  10.1 us (52%)
  Pallas kernels  7.65 us (40%)
  local copies, waits for them, and re-layouts  1.3 us (7%)
    pallas_call x9, Pallas kernels, call(): pl.pallas_call(body, out_shape=list(outs), in_specs=[hbm] * n_hbm + [vmem...  7.65 us
    ppermute x1, starting transfers between devices, per_device(): r2 = lax.ppermute(s2, 'row', inner)  4.55 us
    ppermute x1, starting transfers between devices, per_device(): sums = lax.ppermute(send, 'gz', swap)  1.42 us
    ppermute x1, starting transfers between devices, per_device(): zcorner = lax.ppermute(zcmsg, 'gz', swap)  1.42 us
    unnamed x1, local copies, waits for them, and re-layouts  1.3 us
    ppermute x1, starting transfers between devices, per_device(): zown = lax.ppermute(zmsg, 'gz', swap)  1.27 us
    ppermute x1, starting transfers between devices, per_device(): zxs.append(lax.ppermute(messages[n_side + side], ('gz', 'col'), both))  1.07 us
  transfers between devices with their start and end apart: 7, of which 0 were waited for; matrix products, arithmetic and copies ran while one was open for 7% of the time, Pallas kernels for 30%

profile of v6, /device:TPU:1, one launch (start us, length us, event | category | flops | bytes accessed | tf_op | source)
XLA Modules:
  0.0 19.1 jit_solution(11453509071678448322)
XLA Ops:
  0.0 1.2 %load.1 = (bf16[176,256]{1,0:T(8,128)(2,1)S(1)}, bf16[176,256]{1,0:T(8,128)(2,1)S(1)}, bf16[16,64,256]{2,1,0:T(8,128)(2,1)S(1)}) custom-call(bf16[16,64,256]{2,1,0:T(8,128)(2,1)} %vol.1), custom_call_target="tpu_custom_call" | custom-call | bytes 1228800 | tf_op jit(solution)/shard_map/load/pallas_call | solution.py:577
  1.2 0.1 collective-permute-start
  1.3 4.6 %collective-permute-start.1 = (bf16[176,256]{1,0:T(8,128)(2,1)S(1)}, bf16[176,256]{1,0:T(8,128)(2,1)S(1)}, u32[]{:S(2)}, u32[]{:S(2)}) collective-permute-start(bf16[176,256]{1,0:T(8,128)(2,1)S(1)} %get-tuple-element.20), channel_id=1, source_target_pairs={{2,4},{6,8},{10,12},{4,2},{8,6},{12,10},{3,5},{7,9},{11,13},{5,3},... | collective-permute-start | bytes 270344 | tf_op jit(solution)/shard_map/ppermute | solution.py:622
  5.9 0.3 %edges.1 = (bf16[8,32,128]{2,1,0:T(8,128)(2,1)S(1)}, bf16[480,128]{1,0:T(8,128)(2,1)S(1)}, bf16[8,16,128]{2,1,0:T(8,128)(2,1)S(1)}) custom-call(bf16[16,64,256]{2,1,0:T(8,128)(2,1)S(1)} %get-tuple-element.18.refs_0_), custom_call_target="tpu_custom_call" | custom-call | bytes 745472 | tf_op jit(solution)/shard_map/edges/pallas_call | solution.py:577
  6.2 1.3 %collective-permute-start.2 = (bf16[480,128]{1,0:T(8,128)(2,1)S(1)}, bf16[480,128]{1,0:T(8,128)(2,1)S(1)}, u32[]{:S(2)}, u32[]{:S(2)}) collective-permute-start(bf16[480,128]{1,0:T(8,128)(2,1)S(1)} %get-tuple-element.25), channel_id=1, source_target_pairs={{0,16},{16,0},{1,17},{17,1},{2,18},{18,2},{3,19},{19,3},{4,20},{20... | collective-permute-start | bytes 368648 | tf_op jit(solution)/shard_map/ppermute | solution.py:634
  7.5 1.3 %copy.6.w = bf16[2464,256]{1,0:T(8,128)(2,1)S(1)} copy(bf16[2464,256]{1,0:T(8,128)(2,1)} %constant.2.clone) | data formatting | bytes 2523136
  8.8 0.0 collective-permute-done.refs_0_
  8.8 0.0 collective-permute-done.1.refs_1_
  8.8 0.4 %pack.1 = (bf16[16,32,256]{2,1,0:T(8,128)(2,1)S(1)}, bf16[4,32,128]{2,1,0:T(8,128)(2,1)S(1)}, bf16[176,128]{1,0:T(8,128)(2,1)S(1)}, bf16[12,16,128]{2,1,0:T(8,128)(2,1)S(1)}, bf16[9,16,128]{2,1,0:T(8,128)(2,1)S(1)}) custom-call(bf16[176,256]{1,0:T(8,128)(2,1)S(1)} %collective-permute-done.refs_0_, bf16[176,256]{1,0:T(8,128)(2,1)S(1)} %collective-permute-done.1.refs_1_, ...), custom_call_target="tpu_custom_call" | custom-call | bytes 1900544 | tf_op jit(solution)/shard_map/pack/pallas_call | solution.py:577
  9.2 1.4 %collective-permute-start.3 = (bf16[176,128]{1,0:T(8,128)(2,1)S(1)}, bf16[176,128]{1,0:T(8,128)(2,1)S(1)}, u32[]{:S(2)}, u32[]{:S(2)}) collective-permute-start(bf16[176,128]{1,0:T(8,128)(2,1)S(1)} %get-tuple-element.26), channel_id=1, source_target_pairs={{0,16},{16,0},{1,17},{17,1},{2,18},{18,2},{3,19},{19,3},{4,20},{20... | collective-permute-start | bytes 135176 | tf_op jit(solution)/shard_map/ppermute | solution.py:643
  10.6 1.1 %collective-permute-start.4 = (bf16[9,16,128]{2,1,0:T(8,128)(2,1)S(1)}, bf16[9,16,128]{2,1,0:T(8,128)(2,1)S(1)}, u32[]{:S(2)}, u32[]{:S(2)}) collective-permute-start(bf16[9,16,128]{2,1,0:T(8,128)(2,1)S(1)} %get-tuple-element.27), channel_id=1, source_target_pairs={{0,17},{1,16},{16,1},{17,0},{2,19},{3,18},{18,3},{19,2},{4,21},{5,... | collective-permute-start | bytes 110600 | tf_op jit(solution)/shard_map/ppermute | solution.py:652
  11.7 0.2 %collective-permute-start.5 = (bf16[12,16,128]{2,1,0:T(8,128)(2,1)S(1)}, bf16[12,16,128]{2,1,0:T(8,128)(2,1)S(1)}, u32[]{:S(2)}, u32[]{:S(2)}) collective-permute-start(bf16[12,16,128]{2,1,0:T(8,128)(2,1)S(1)} %get-tuple-element.29), channel_id=1, source_target_pairs={{0,1},{1,0},{2,3},{3,2},{4,5},{5,4},{6,7},{7,6},{8,9},{9,8},{10,11... | collective-permute-start | bytes 147464 | tf_op jit(solution)/shard_map/ppermute | solution.py:651
  11.9 1.1 %first.1.refs_4_.refs_5_ = f32[5,96,64]{2,1,0:T(8,128)S(1)} custom-call(bf16[16,64,256]{2,1,0:T(8,128)(2,1)S(1)} %get-tuple-element.18.refs_0_, bf16[16,32,256]{2,1,0:T(8,128)(2,1)S(1)} %get-tuple-element.22.refs_1_, bf16[2464,256]{1,0:T(8,128)(2,1)S(1)} %stage.1.refs_2_.refs_5_.refs_7_), custom_call_target="tpu_custom_call" | custom-call | flops 349962240 | bytes 2170880 | tf_op jit(solution)/shard_map/first/pallas_call | solution.py:577
  13.0 0.0 collective-permute-done.2.zown.refs_2_
  13.0 0.0 collective-permute-done.3.zcorner.refs_3_
  13.0 1.1 %near.1 = (f32[3,96,64]{2,1,0:T(8,128)S(1)}, bf16[96,128]{1,0:T(8,128)(2,1)S(1)}) custom-call(bf16[16,64,256]{2,1,0:T(8,128)(2,1)S(1)} %get-tuple-element.18.refs_0_, bf16[16,32,256]{2,1,0:T(8,128)(2,1)S(1)} %get-tuple-element.22.refs_1_, bf16[480,128]{1,0:T(8,128)(2,1)S(1)} %collective-permute-done.2.zown.refs_2_, ...), custom_call_target="tpu_custom_call" | custom-call | flops 209977344 | bytes 2437120 | tf_op jit(solution)/shard_map/near/pallas_call | solution.py:577
  14.1 1.4 %collective-permute-start.6 = (bf16[96,128]{1,0:T(8,128)(2,1)S(1)}, bf16[96,128]{1,0:T(8,128)(2,1)S(1)}, u32[]{:S(2)}, u32[]{:S(2)}) collective-permute-start(bf16[96,128]{1,0:T(8,128)(2,1)S(1)} %get-tuple-element.30), channel_id=1, source_target_pairs={{0,16},{16,0},{1,17},{17,1},{2,18},{18,2},{3,19},{19,3},{4,20},{20... | collective-permute-start | bytes 73736 | tf_op jit(solution)/shard_map/ppermute | solution.py:666
  15.5 0.0 collective-permute-done.4.refs_0_
  15.6 0.1 beyond.1.refs_4_
  15.7 0.0 collective-permute-done.5.refs_8_
  15.7 2.7 %last.1.own = f32[6,4,16,64]{3,2,1,0:T(8,128)S(1)} custom-call(bf16[16,64,256]{2,1,0:T(8,128)(2,1)S(1)} %get-tuple-element.18.refs_0_, bf16[16,32,256]{2,1,0:T(8,128)(2,1)S(1)} %get-tuple-element.22.refs_1_, bf16[8,32,128]{2,1,0:T(8,128)(2,1)S(1)} %get-tuple-element.23.refs_2_, bf16[4,32,128]{2,1,0:T(8,128)(2,1)S(1)} %get-tuple-element.24.refs_3_, ...), custom_call_target="tpu_custom_call" | custom-call | flops 769916928 | bytes 2588672 | tf_op jit(solution)/shard_map/last/pallas_call | solution.py:577
  18.3 0.0 collective-permute-done.6.got
  18.4 0.8 %add.1 = f32[6,4,16,64]{3,2,1,0:T(8,128)} custom-call(f32[6,4,16,64]{3,2,1,0:T(8,128)S(1)} %last.1.own, bf16[96,128]{1,0:T(8,128)(2,1)S(1)} %collective-permute-done.6.got), custom_call_target="tpu_custom_call" | custom-call | bytes 221184 | tf_op jit(solution)/shard_map/add/pallas_call | solution.py:577
  (1 shorter events, 0.0 us)
Async XLA Ops:
  1.2 7.6 %collective-permute-start = (bf16[176,256]{1,0:T(8,128)(2,1)S(1)}, bf16[176,256]{1,0:T(8,128)(2,1)S(1)}, u32[]{:S(2)}, u32[]{:S(2)}) collective-permute-start(bf16[176,256]{1,0:T(8,128)(2,1)S(1)} %get-tuple-element.19), channel_id=1, source_target_pairs={{0,2},{2,0},{4,6},{6,4},{8,10},{10,8},{12,14},{14,12},{1,3},{3,1},... | collective-permute-start | bytes 270344 | tf_op jit(solution)/shard_map/ppermute | solution.py:623
  1.3 7.4 %collective-permute-start.1 = (bf16[176,256]{1,0:T(8,128)(2,1)S(1)}, bf16[176,256]{1,0:T(8,128)(2,1)S(1)}, u32[]{:S(2)}, u32[]{:S(2)}) collective-permute-start(bf16[176,256]{1,0:T(8,128)(2,1)S(1)} %get-tuple-element.20), channel_id=1, source_target_pairs={{2,4},{6,8},{10,12},{4,2},{8,6},{12,10},{3,5},{7,9},{11,13},{5,3},... | collective-permute-start | bytes 270344 | tf_op jit(solution)/shard_map/ppermute | solution.py:622
  6.2 6.8 %collective-permute-start.2 = (bf16[480,128]{1,0:T(8,128)(2,1)S(1)}, bf16[480,128]{1,0:T(8,128)(2,1)S(1)}, u32[]{:S(2)}, u32[]{:S(2)}) collective-permute-start(bf16[480,128]{1,0:T(8,128)(2,1)S(1)} %get-tuple-element.25), channel_id=1, source_target_pairs={{0,16},{16,0},{1,17},{17,1},{2,18},{18,2},{3,19},{19,3},{4,20},{20... | collective-permute-start | bytes 368648 | tf_op jit(solution)/shard_map/ppermute | solution.py:634
  9.2 3.8 %collective-permute-start.3 = (bf16[176,128]{1,0:T(8,128)(2,1)S(1)}, bf16[176,128]{1,0:T(8,128)(2,1)S(1)}, u32[]{:S(2)}, u32[]{:S(2)}) collective-permute-start(bf16[176,128]{1,0:T(8,128)(2,1)S(1)} %get-tuple-element.26), channel_id=1, source_target_pairs={{0,16},{16,0},{1,17},{17,1},{2,18},{18,2},{3,19},{19,3},{4,20},{20... | collective-permute-start | bytes 135176 | tf_op jit(solution)/shard_map/ppermute | solution.py:643
  10.6 5.0 %collective-permute-start.4 = (bf16[9,16,128]{2,1,0:T(8,128)(2,1)S(1)}, bf16[9,16,128]{2,1,0:T(8,128)(2,1)S(1)}, u32[]{:S(2)}, u32[]{:S(2)}) collective-permute-start(bf16[9,16,128]{2,1,0:T(8,128)(2,1)S(1)} %get-tuple-element.27), channel_id=1, source_target_pairs={{0,17},{1,16},{16,1},{17,0},{2,19},{3,18},{18,3},{19,2},{4,21},{5,... | collective-permute-start | bytes 110600 | tf_op jit(solution)/shard_map/ppermute | solution.py:652
  11.7 4.0 %collective-permute-start.5 = (bf16[12,16,128]{2,1,0:T(8,128)(2,1)S(1)}, bf16[12,16,128]{2,1,0:T(8,128)(2,1)S(1)}, u32[]{:S(2)}, u32[]{:S(2)}) collective-permute-start(bf16[12,16,128]{2,1,0:T(8,128)(2,1)S(1)} %get-tuple-element.29), channel_id=1, source_target_pairs={{0,1},{1,0},{2,3},{3,2},{4,5},{5,4},{6,7},{7,6},{8,9},{9,8},{10,11... | collective-permute-start | bytes 147464 | tf_op jit(solution)/shard_map/ppermute | solution.py:651
  14.1 4.2 %collective-permute-start.6 = (bf16[96,128]{1,0:T(8,128)(2,1)S(1)}, bf16[96,128]{1,0:T(8,128)(2,1)S(1)}, u32[]{:S(2)}, u32[]{:S(2)}) collective-permute-start(bf16[96,128]{1,0:T(8,128)(2,1)S(1)} %get-tuple-element.30), channel_id=1, source_target_pairs={{0,16},{16,0},{1,17},{17,1},{2,18},{18,2},{3,19},{19,3},{4,20},{20... | collective-permute-start | bytes 73736 | tf_op jit(solution)/shard_map/ppermute | solution.py:666

commit v7 on v5

--- a/solution.py
+++ b/solution.py
@@ -201,9 +201,9 @@
             if 0 <= i < n_group:
                 stage(ends[i], ends[i + 1] - ends[i])
     out = jnp.dot(
-        sm[...].reshape(count * n_rows, cols), get("xsm"), preferred_element_type=F32
-    )
-    u_ref[...] = out.reshape(count, n_rows, cols // 4)
+        sm[0:count].reshape(count * n_rows, cols), get("xsm"), preferred_element_type=F32
+    )
+    u_ref[0:count] = out.reshape(count, n_rows, cols // 4)
 
 
 def block_loader(vol, yud, rows):
@@ -344,27 +344,54 @@
     pass
 
 
-FIRST = 7
-GROUP = 3
+FIRST = {True: 5, False: 3}
+LAST = {True: 8, False: 10}
+GROUP = 4
 EDGE = R
-LAST = 6
+
+
+def by_half(body):
+    low = lax.axis_index("gz") == 0
+    pl.when(low)(lambda: body(True))
+    pl.when(jnp.logical_not(low))(lambda: body(False))
 
 
 def first_kernel(place_of, n_row, vol, yud, w, u_ref, *scratch):
     depth, rows, cols = vol.shape
     get = getter(place_of, w)
     ysm = row_mask(get, n_row, rows, rows + 16, rows // 4)
-    base = jnp.where(lax.axis_index("gz") == 0, depth - EDGE - FIRST - R, 0)
     layer = block_loader(vol, yud, rows)
-    load = lambda at, lanes, lo, hi: [layer(base + k, at, lanes) for k in range(lo, hi)]
-    layers_to_sums(get, ysm, load, FIRST, (rows, cols), u_ref, *scratch)
+
+    def body(low):
+        count = FIRST[low]
+        base = depth - EDGE - count - R if low else 0
+        load = lambda at, lanes, lo, hi: [layer(base + k, at, lanes) for k in range(lo, hi)]
+        layers_to_sums(get, ysm, load, count, (rows, cols), u_ref, *scratch)
+
+    by_half(body)
+
+
+def held_layers(depth, low):
+    if low:
+        near = depth - EDGE
+        return range(near - FIRST[low], near), range(near, depth), range(LAST[low])
+    last = EDGE + FIRST[low]
+    return range(EDGE, last), range(EDGE), range(last, depth)
+
+
+def weighted(total, refs, held, weights):
+    for ref, layers in zip(refs, held):
+        for k, z in enumerate(layers):
+            if weights[z] != 0.0:
+                term = ref[k] * float(weights[z])
+                total = term if total is None else total + term
+    return total
 
 
 def near_kernel(place_of, zs, n_row, vol, yud, zown, zcorner, u1, w, u_ref, send_ref, zext, *scratch):
     depth, rows, cols = vol.shape
     n_zq = zs.shape[1]
     get = getter(place_of, w)
-    low = lax.axis_index("gz") == 0
     ysm = row_mask(get, n_row, rows, rows + 16, rows // 4)
     corner = jnp.dot(
         get("corner_back"), joined_halves(zcorner, 0, 64), preferred_element_type=F32
@@ -373,71 +400,33 @@
     zext[:, HALO : HALO + rows] = joined_halves(zown, 0, R * rows).reshape(R, rows, cols)
     zext[:, HALO + rows :] = corner[:, HALO:]
     layer = block_loader(vol, yud, rows)
-    start = jnp.where(low, depth - R, 0)
-    outer = jnp.where(low, depth - 2 * R, R)
-
-    def load(at, lanes, lo, hi):
-        out = []
-        for k in range(lo, hi):
-            if R <= k < 2 * R:
-                out.append(layer(start + k - R, at, lanes))
-                continue
-            i = k % R
-            inner = layer(outer + i, at, lanes)
-            beyond = zext[i, at : at + 16, lanes].astype(F32)
-            first, second = (inner, beyond) if k < R else (beyond, inner)
-            out.append(jnp.where(low, first, second))
-        return out
-
-    layers_to_sums(get, ysm, load, EDGE, (rows, cols), u_ref, *scratch)
-    sends = []
-    for k in range(2):
-        total = None
-        for i in range(FIRST + EDGE):
-            from_low = depth - EDGE - FIRST + i
-            from_high = EDGE + i if i < FIRST else i - FIRST
-            a = float(zs[from_low, n_zq - 2 + k])
-            b = float(zs[from_high, k])
-            if a == 0.0 and b == 0.0:
-                continue
-            term = (u1[i] if i < FIRST else u_ref[i - FIRST]) * jnp.where(low, a, b)
-            total = term if total is None else total + term
-        sends.append(total)
-    send_ref[...] = jnp.concatenate(sends, axis=1).astype(BF16)
-
-
-def last_layers(place_of, get, ysm, vol, yud, u_ref, *scratch):
-    depth, rows, cols = vol.shape
-    low = lax.axis_index("gz") == 0
-    layer = block_loader(vol, yud, rows)
-    base = jnp.where(low, -R, depth - LAST - R)
-    before_on = jnp.where(low, 0.0, 1.0)
-    after_on = jnp.where(low, 1.0, 0.0)
-
-    def load(at, lanes, lo, hi):
-        out = []
-        for k in range(lo, hi):
-            block = layer(jnp.clip(base + k, 0, depth - 1), at, lanes)
-            if k < R:
-                block = block * before_on
-            elif k >= LAST + R:
-                block = block * after_on
-            out.append(block)
-        return out
-
-    layers_to_sums(get, ysm, load, LAST, (rows, cols), u_ref, *scratch)
-
-
-def last_kernel(place_of, zs, n_row, n_col, vol, yud, own, halo, zown, zcorner, u1, u2, w,
-                xs, zxs, own_ref, hs, hd, pstrip, u3, *scratch):
-    depth, rows, cols = vol.shape
-    gr = rows + 16
-    quarter_rows, quarter = rows // 4, cols // 4
-    get = getter(place_of, w)
-    gz, col = lax.axis_index("gz"), lax.axis_index("col")
-    low = gz == 0
-    ysm = row_mask(get, n_row, rows, gr, quarter_rows)
-    last_layers(place_of, get, ysm, vol, yud, u3, *scratch)
+
+    def body(low):
+        start = depth - R if low else 0
+        outer = depth - 2 * R if low else R
+
+        def load(at, lanes, lo, hi):
+            out = []
+            for k in range(lo, hi):
+                if R <= k < 2 * R:
+                    out.append(layer(start + k - R, at, lanes))
+                elif (k < R) == low:
+                    out.append(layer(outer + k % R, at, lanes))
+                else:
+                    out.append(zext[k % R, at : at + 16, lanes].astype(F32))
+            return out
+
+        layers_to_sums(get, ysm, load, EDGE, (rows, cols), u_ref, *scratch)
+        held = held_layers(depth, low)[0:2]
+        first_q = n_zq - 2 if low else 0
+        sends = [weighted(None, (u1, u_ref), held, zs[:, first_q + k]) for k in range(2)]
+        send_ref[...] = jnp.concatenate(sends, axis=1).astype(BF16)
+
+    by_half(body)
+
+
+def strip_tools(n_col, rows):
+    col = lax.axis_index("col")
     slots = lax.broadcasted_iota(jnp.int32, (SLOTS, 128), 0)
     if n_col == 2:
         keep = ((slots < 8) & (col == 0)) | ((slots >= 21) & (col == 1))
@@ -447,11 +436,6 @@
     def join(part, messages, b):
         sides = [messages[-1][b].astype(F32), messages[0][b].astype(F32)]
         return jnp.where(keep, jnp.concatenate(sides, axis=0), part)
-
-    def from_middle(ref, at, b):
-        rim = jnp.zeros((8, 128), F32)
-        middle = ref[at + 16 * b : at + 16 * (b + 1)].astype(F32)
-        return jnp.concatenate([rim, middle, rim], axis=0)
 
     lanes = lax.broadcasted_iota(jnp.int32, (SLOTS, 128), 1)
 
@@ -467,77 +451,105 @@
             out.append(jnp.where(lanes < rows, left, right))
         return out
 
+    return join, layers_of
+
+
+def beyond_kernel(n_col, rows, zown, zcorner, zxs, out):
+    join, layers_of = strip_tools(n_col, rows)
+
+    def from_middle(ref, at, b):
+        rim = jnp.zeros((8, 128), F32)
+        middle = ref[at + 16 * b : at + 16 * (b + 1)].astype(F32)
+        return jnp.concatenate([rim, middle, rim], axis=0)
+
     n2, n4 = EXTRA // 2, EXTRA // 4
-    own_layers = layers_of(
-        [join(own[b].astype(F32), xs, b) for b in range(depth // 2)],
-        [join(halo[b].astype(F32), xs, depth // 2 + b) for b in range(depth // 4)],
-    )
-    at = 2 * R * rows
-    beyond = layers_of(
-        [join(from_middle(zown, at, b), zxs, b) for b in range(n2)],
+    layers = layers_of(
+        [join(from_middle(zown, 2 * R * rows, b), zxs, b) for b in range(n2)],
         [join(from_middle(zcorner, 128, b), zxs, n2 + b) for b in range(n4)],
     )
-    count = depth + 8
-    zero = [jnp.zeros((SLOTS, 128), F32)] * R
-    at_low = zero + own_layers + beyond[0:11]
-    at_high = beyond[1:12] + own_layers + zero
-    layers = [jnp.where(low, a, b) for a, b in zip(at_low, at_high)]
-    for z, smooth, slope in z_filter(layers, count):
-        hs[SLOTS * z : SLOTS * (z + 1)] = smooth.astype(BF16)
-        hd[SLOTS * z : SLOTS * (z + 1)] = slope.astype(BF16)
-    p01 = lax.dot_general(
-        get("wy_strip", 128), hs[...], NT, preferred_element_type=F32
-    ).astype(BF16)
-    p2 = lax.dot_general(
-        get("wy_strip_slope", 128), hd[...], NT, preferred_element_type=F32
-    ).astype(BF16)
-    n = count // 8
-    groups = [slice(256 * c, 256 * (c + 1)) for c in range(n)]
-    stacks = [
-        jnp.concatenate([p[:, g] for g in groups], axis=0) for p in (p01[0:gr], p01[gr:], p2)
-    ]
-    grads = [
-        jnp.dot(stack, get(name), preferred_element_type=F32).astype(BF16).reshape(n, gr, 256)
-        for stack, name in zip(stacks, ("bdd", "bds", "bds"))
-    ]
-    for c, (a, b) in enumerate(pair_table):
-        pstrip[:, c * gr : (c + 1) * gr] = grads[a] * grads[b]
+    for k, layer in enumerate(layers):
+        out[k] = layer.astype(BF16)
+
+
+def last_kernel(place_of, zs, n_row, n_col, vol, yud, own, halo, far, u1, u2, w, xs, own_ref,
+                hs, hd, pstrip, u3, *scratch):
+    depth, rows, cols = vol.shape
+    gr = rows + 16
+    quarter_rows, quarter = rows // 4, cols // 4
+    get = getter(place_of, w)
+    col = lax.axis_index("col")
+    ysm = row_mask(get, n_row, rows, gr, quarter_rows)
+    join, layers_of = strip_tools(n_col, rows)
+    layer = block_loader(vol, yud, rows)
     slot = lax.rem(lax.broadcasted_iota(jnp.int32, (3 * quarter_rows, 256), 1), SLOTS)
     outside_x = ((col == 0) & (slot < 8)) | ((col == n_col - 1) & (slot >= 14))
-    smoothed = []
-    for c in range(n):
-        for half in range(2):
-            part = pstrip[c, half * 3 * gr : (half + 1) * 3 * gr]
-            out = jnp.dot(ysm, part, preferred_element_type=F32)
-            smoothed.append(jnp.where(outside_x, 0.0, out).astype(BF16))
-    u = jnp.dot(jnp.concatenate(smoothed, axis=0), get("bdx"), preferred_element_type=F32)
     n_rows = 6 * quarter_rows
-    u = u.astype(BF16)
-    sums = []
-    for name in ("0", "1"):
-        at = jnp.where(low, place_of["g_low" + name][0], place_of["g_high" + name][0])
-        total = None
+    count = depth + 8
+    n = count // 8
+
+    def body(low):
+        first = 0 if low else depth - LAST[low]
+
+        def load(at, lanes, lo, hi):
+            out = []
+            for z in range(first - R + lo, first - R + hi):
+                inside = 0 <= z < depth
+                out.append(layer(z, at, lanes) if inside else jnp.zeros((16, 128), F32))
+            return out
+
+        layers_to_sums(get, ysm, load, LAST[low], (rows, cols), u3, *scratch)
+        own_layers = layers_of(
+            [join(own[b].astype(F32), xs, b) for b in range(depth // 2)],
+            [join(halo[b].astype(F32), xs, depth // 2 + b) for b in range(depth // 4)],
+        )
+        beyond = [far[k].astype(F32) for k in range(EXTRA)]
+        zero = [jnp.zeros((SLOTS, 128), F32)] * R
+        if low:
+            layers = zero + own_layers + beyond[0:11]
+        else:
+            layers = beyond[1:12] + own_layers + zero
+        for z, smooth, slope in z_filter(layers, count):
+            hs[SLOTS * z : SLOTS * (z + 1)] = smooth.astype(BF16)
+            hd[SLOTS * z : SLOTS * (z + 1)] = slope.astype(BF16)
+        p01 = lax.dot_general(
+            get("wy_strip", 128), hs[...], NT, preferred_element_type=F32
+        ).astype(BF16)
+        p2 = lax.dot_general(
+            get("wy_strip_slope", 128), hd[...], NT, preferred_element_type=F32
+        ).astype(BF16)
+        groups = [slice(256 * c, 256 * (c + 1)) for c in range(n)]
+        stacks = [
+            jnp.concatenate([p[:, g] for g in groups], axis=0) for p in (p01[0:gr], p01[gr:], p2)
+        ]
+        grads = [
+            jnp.dot(stack, get(name), preferred_element_type=F32).astype(BF16).reshape(n, gr, 256)
+            for stack, name in zip(stacks, ("bdd", "bds", "bds"))
+        ]
+        for c, (a, b) in enumerate(pair_table):
+            pstrip[:, c * gr : (c + 1) * gr] = grads[a] * grads[b]
+        smoothed = []
         for c in range(n):
-            g = w[pl.ds(pl.multiple_of(at + 64 * c, 16), 64), :]
-            term = jnp.dot(u[n_rows * c : n_rows * (c + 1)], g, preferred_element_type=F32)
-            total = term if total is None else total + term
-        sums += [total[:, 0:quarter], total[:, 128 : 128 + quarter]]
-    for q in range(depth // 4):
-        total = sums[q]
-        for i in range(depth):
-            if i < FIRST:
-                u, from_low, from_high = u1[i], depth - EDGE - FIRST + i, EDGE + i
-            elif i < FIRST + EDGE:
-                k = i - FIRST
-                u, from_low, from_high = u2[k], depth - EDGE + k, k
-            else:
-                k = i - FIRST - EDGE
-                u, from_low, from_high = u3[k], k, depth - LAST + k
-            a, b = float(zs[from_low, q + 2]), float(zs[from_high, q + 2])
-            if a == 0.0 and b == 0.0:
-                continue
-            total = total + u * jnp.where(low, a, b)
-        own_ref[:, q] = total.reshape(6, quarter_rows, quarter)
+            for half in range(2):
+                part = pstrip[c, half * 3 * gr : (half + 1) * 3 * gr]
+                out = jnp.dot(ysm, part, preferred_element_type=F32)
+                smoothed.append(jnp.where(outside_x, 0.0, out).astype(BF16))
+        u = jnp.dot(jnp.concatenate(smoothed, axis=0), get("bdx"), preferred_element_type=F32)
+        u = u.astype(BF16)
+        sums = []
+        for name in ("0", "1"):
+            at = place_of[("g_low" if low else "g_high") + name][0]
+            total = None
+            for c in range(n):
+                g = w[at + 64 * c : at + 64 * (c + 1), :]
+                term = jnp.dot(u[n_rows * c : n_rows * (c + 1)], g, preferred_element_type=F32)
+                total = term if total is None else total + term
+            sums += [total[:, 0:quarter], total[:, 128 : 128 + quarter]]
+        held = held_layers(depth, low)
+        for q in range(depth // 4):
+            total = weighted(sums[q], (u1, u2, u3), held, zs[:, q + 2])
+            own_ref[:, q] = total.reshape(6, quarter_rows, quarter)
+
+    by_half(body)
 
 
 def add_kernel(own, got, out):
@@ -590,6 +602,7 @@
     n2, n4 = EXTRA // 2, EXTRA // 4
     sds = jax.ShapeDtypeStruct
     bf16 = lambda *shape: sds(shape, BF16)
+    most_first, most_last = max(FIRST.values()), max(LAST.values())
 
     def scratch_for(count):
         return [
@@ -643,8 +656,8 @@
 
     (u1,) = call(
         lambda *refs: first_kernel(place_of, n_row, *refs),
-        [sds((FIRST, n_rows, quarter), F32)],
-        [vol, yud, w], scratch_for(FIRST), "first", flops=FIRST * layer_flops,
+        [sds((most_first, n_rows, quarter), F32)],
+        [vol, yud, w], scratch_for(most_first), "first", flops=most_first * layer_flops,
     )
     u2, send = call(
         lambda *refs: near_kernel(place_of, zs, n_row, *refs),
@@ -655,25 +668,30 @@
     )
     sums = lax.ppermute(send, "gz", swap)
 
+    (far,) = call(
+        lambda zown, zcorner, *refs: beyond_kernel(
+            n_col, rows, zown, zcorner, refs[:n_side], refs[n_side]
+        ),
+        [bf16(EXTRA, SLOTS, 128)], [zown, zcorner] + zxs, [], "beyond", flops=EDGE * layer_flops,
+    )
+
     def last_body(*refs):
-        head, x_refs, zx_refs = refs[0:9], refs[9 : 9 + n_side], refs[9 + n_side : 9 + 2 * n_side]
-        last_kernel(
-            place_of, zs, n_row, n_col, *head, x_refs, zx_refs, *refs[9 + 2 * n_side :]
-        )
+        head, x_refs, tail = refs[0:8], refs[8 : 8 + n_side], refs[8 + n_side :]
+        last_kernel(place_of, zs, n_row, n_col, *head, x_refs, *tail)
 
     count = depth + 8
     (result,) = call(
         last_body,
         [sds((6, depth // 4, quarter_rows, quarter), F32)],
-        [vol, yud, own, halo, zown, zcorner, u1, u2, w] + xs + zxs,
+        [vol, yud, own, halo, far, u1, u2, w] + xs,
         [
             pltpu.VMEM((count * SLOTS, 128), BF16),
             pltpu.VMEM((count * SLOTS, 128), BF16),
             pltpu.VMEM((count // 8, 6 * gr, 256), BF16),
-            pltpu.VMEM((LAST, n_rows, quarter), F32),
+            pltpu.VMEM((most_last, n_rows, quarter), F32),
         ]
-        + scratch_for(LAST),
-        "last", flops=(LAST + 3) * layer_flops,
+        + scratch_for(most_last),
+        "last", flops=(most_last + 3) * layer_flops,
     )
     (out,) = call(add_kernel, [sds(result.shape, F32)], [result, sums], [], "add")
     return out

time: 18.9 us -> 18.6 us (0.984)
  starting transfers between devices: 9.58 us -> 9.33 us
    ppermute x1, starting transfers between devices: 0.54 us -> 1.56 us  [per_device(): zxs.append(lax.ppermute(messages[n_side + side], ('gz', 'col'), both))]
    ppermute x1, starting transfers between devices: 1.25 us -> 0.22 us  [per_device(): xs.append(lax.ppermute(messages[side], 'col', line))]
    ppermute x1, starting transfers between devices: 0.92 us -> 0.67 us  [per_device(): sums = lax.ppermute(send, 'gz', swap)]
    pallas_call x8 -> x9, Pallas kernels: 7.61 us -> 7.47 us  [call(): pl.pallas_call(body, out_shape=list(outs), in_specs=[hbm] * n_hbm + [vmem...]
where the time goes in v7:
time: 18.6 us; the launch traced here: 18.4 us
  starting transfers between devices  9.33 us (50%)
  Pallas kernels  7.47 us (40%)
  local copies, waits for them, and re-layouts  1.48 us (8%)
    pallas_call x9, Pallas kernels, call(): pl.pallas_call(body, out_shape=list(outs), in_specs=[hbm] * n_hbm + [vmem...  7.47 us
    ppermute x1, starting transfers between devices, per_device(): r2 = lax.ppermute(s2, 'row', inner)  4.55 us
    ppermute x1, starting transfers between devices, per_device(): zxs.append(lax.ppermute(messages[n_side + side], ('gz', 'col'), both))  1.56 us
    unnamed x1, local copies, waits for them, and re-layouts  1.48 us
    ppermute x1, starting transfers between devices, per_device(): zown = lax.ppermute(zmsg, 'gz', swap)  1.27 us
    ppermute x1, starting transfers between devices, per_device(): zcorner = lax.ppermute(zcmsg, 'gz', swap)  0.93 us
    ppermute x1, starting transfers between devices, per_device(): sums = lax.ppermute(send, 'gz', swap)  0.67 us
  transfers between devices with their start and end apart: 7, of which 0 were waited for; matrix products, arithmetic and copies ran while one was open for 8% of the time, Pallas kernels for 30%

profile of v7, /device:TPU:1, one launch (start us, length us, event | category | flops | bytes accessed | tf_op | source)
XLA Modules:
  0.0 18.4 jit_solution(5176097441578301457)
XLA Ops:
  0.0 1.2 %load.1 = (bf16[176,256]{1,0:T(8,128)(2,1)S(1)}, bf16[176,256]{1,0:T(8,128)(2,1)S(1)}, bf16[16,64,256]{2,1,0:T(8,128)(2,1)S(1)}) custom-call(bf16[16,64,256]{2,1,0:T(8,128)(2,1)} %vol.1), custom_call_target="tpu_custom_call" | custom-call | bytes 1228800 | tf_op jit(solution)/shard_map/load/pallas_call | solution.py:579
  1.2 0.1 collective-permute-start
  1.3 4.6 %collective-permute-start.1 = (bf16[176,256]{1,0:T(8,128)(2,1)S(1)}, bf16[176,256]{1,0:T(8,128)(2,1)S(1)}, u32[]{:S(2)}, u32[]{:S(2)}) collective-permute-start(bf16[176,256]{1,0:T(8,128)(2,1)S(1)} %get-tuple-element.20), channel_id=1, source_target_pairs={{2,4},{6,8},{10,12},{4,2},{8,6},{12,10},{3,5},{7,9},{11,13},{5,3},... | collective-permute-start | bytes 270344 | tf_op jit(solution)/shard_map/ppermute | solution.py:625
  5.9 0.3 %edges.1 = (bf16[8,32,128]{2,1,0:T(8,128)(2,1)S(1)}, bf16[480,128]{1,0:T(8,128)(2,1)S(1)}, bf16[8,16,128]{2,1,0:T(8,128)(2,1)S(1)}) custom-call(bf16[16,64,256]{2,1,0:T(8,128)(2,1)S(1)} %get-tuple-element.18.refs_0_), custom_call_target="tpu_custom_call" | custom-call | bytes 745472 | tf_op jit(solution)/shard_map/edges/pallas_call | solution.py:579
  6.2 1.3 %collective-permute-start.2 = (bf16[480,128]{1,0:T(8,128)(2,1)S(1)}, bf16[480,128]{1,0:T(8,128)(2,1)S(1)}, u32[]{:S(2)}, u32[]{:S(2)}) collective-permute-start(bf16[480,128]{1,0:T(8,128)(2,1)S(1)} %get-tuple-element.25), channel_id=1, source_target_pairs={{0,16},{16,0},{1,17},{17,1},{2,18},{18,2},{3,19},{19,3},{4,20},{20... | collective-permute-start | bytes 368648 | tf_op jit(solution)/shard_map/ppermute | solution.py:637
  7.5 1.5 %copy.6.w = bf16[3504,256]{1,0:T(8,128)(2,1)S(1)} copy(bf16[3504,256]{1,0:T(8,128)(2,1)} %constant.2.clone) | data formatting | bytes 3588096
  9.0 0.0 collective-permute-done.refs_0_
  9.0 0.0 collective-permute-done.1.refs_1_
  9.0 0.4 %pack.1 = (bf16[16,32,256]{2,1,0:T(8,128)(2,1)S(1)}, bf16[4,32,128]{2,1,0:T(8,128)(2,1)S(1)}, bf16[176,128]{1,0:T(8,128)(2,1)S(1)}, bf16[12,16,128]{2,1,0:T(8,128)(2,1)S(1)}, bf16[9,16,128]{2,1,0:T(8,128)(2,1)S(1)}) custom-call(bf16[176,256]{1,0:T(8,128)(2,1)S(1)} %collective-permute-done.refs_0_, bf16[176,256]{1,0:T(8,128)(2,1)S(1)} %collective-permute-done.1.refs_1_, ...), custom_call_target="tpu_custom_call" | custom-call | bytes 2433024 | tf_op jit(solution)/shard_map/pack/pallas_call | solution.py:579
  9.4 0.9 %collective-permute-start.3 = (bf16[176,128]{1,0:T(8,128)(2,1)S(1)}, bf16[176,128]{1,0:T(8,128)(2,1)S(1)}, u32[]{:S(2)}, u32[]{:S(2)}) collective-permute-start(bf16[176,128]{1,0:T(8,128)(2,1)S(1)} %get-tuple-element.26), channel_id=1, source_target_pairs={{0,16},{16,0},{1,17},{17,1},{2,18},{18,2},{3,19},{19,3},{4,20},{20... | collective-permute-start | bytes 135176 | tf_op jit(solution)/shard_map/ppermute | solution.py:646
  10.3 1.6 %collective-permute-start.4 = (bf16[9,16,128]{2,1,0:T(8,128)(2,1)S(1)}, bf16[9,16,128]{2,1,0:T(8,128)(2,1)S(1)}, u32[]{:S(2)}, u32[]{:S(2)}) collective-permute-start(bf16[9,16,128]{2,1,0:T(8,128)(2,1)S(1)} %get-tuple-element.27), channel_id=1, source_target_pairs={{0,17},{1,16},{16,1},{17,0},{2,19},{3,18},{18,3},{19,2},{4,21},{5,... | collective-permute-start | bytes 110600 | tf_op jit(solution)/shard_map/ppermute | solution.py:655
  11.9 0.2 %collective-permute-start.5 = (bf16[12,16,128]{2,1,0:T(8,128)(2,1)S(1)}, bf16[12,16,128]{2,1,0:T(8,128)(2,1)S(1)}, u32[]{:S(2)}, u32[]{:S(2)}) collective-permute-start(bf16[12,16,128]{2,1,0:T(8,128)(2,1)S(1)} %get-tuple-element.29), channel_id=1, source_target_pairs={{0,1},{1,0},{2,3},{3,2},{4,5},{5,4},{6,7},{7,6},{8,9},{9,8},{10,11... | collective-permute-start | bytes 147464 | tf_op jit(solution)/shard_map/ppermute | solution.py:654
  12.1 1.2 %first.1.refs_4_.refs_5_ = f32[5,96,64]{2,1,0:T(8,128)S(1)} custom-call(bf16[16,64,256]{2,1,0:T(8,128)(2,1)S(1)} %get-tuple-element.18.refs_0_, bf16[16,32,256]{2,1,0:T(8,128)(2,1)S(1)} %get-tuple-element.22.refs_1_, bf16[3504,256]{1,0:T(8,128)(2,1)S(1)} %stage.1.refs_2_.refs_5_.refs_7_), custom_call_target="tpu_custom_call" | custom-call | flops 349962240 | bytes 2703360 | tf_op jit(solution)/shard_map/first/pallas_call | solution.py:579
  13.2 0.0 collective-permute-done.2.zown.refs_2_
  13.2 0.0 collective-permute-done.3.zcorner.refs_3_
  13.3 1.1 %near.1 = (f32[3,96,64]{2,1,0:T(8,128)S(1)}, bf16[96,128]{1,0:T(8,128)(2,1)S(1)}) custom-call(bf16[16,64,256]{2,1,0:T(8,128)(2,1)S(1)} %get-tuple-element.18.refs_0_, bf16[16,32,256]{2,1,0:T(8,128)(2,1)S(1)} %get-tuple-element.22.refs_1_, bf16[480,128]{1,0:T(8,128)(2,1)S(1)} %collective-permute-done.2.zown.refs_2_, ...), custom_call_target="tpu_custom_call" | custom-call | flops 209977344 | bytes 2969600 | tf_op jit(solution)/shard_map/near/pallas_call | solution.py:579
  14.4 0.7 %collective-permute-start.6 = (bf16[96,128]{1,0:T(8,128)(2,1)S(1)}, bf16[96,128]{1,0:T(8,128)(2,1)S(1)}, u32[]{:S(2)}, u32[]{:S(2)}) collective-permute-start(bf16[96,128]{1,0:T(8,128)(2,1)S(1)} %get-tuple-element.30), channel_id=1, source_target_pairs={{0,16},{16,0},{1,17},{17,1},{2,18},{18,2},{3,19},{19,3},{4,20},{20... | collective-permute-start | bytes 73736 | tf_op jit(solution)/shard_map/ppermute | solution.py:669
  15.1 0.0 collective-permute-done.4.refs_0_
  15.1 0.1 beyond.1.refs_4_
  15.2 0.0 collective-permute-done.5.refs_8_
  15.2 2.4 %last.1.own = f32[6,4,16,64]{3,2,1,0:T(8,128)S(1)} custom-call(bf16[16,64,256]{2,1,0:T(8,128)(2,1)S(1)} %get-tuple-element.18.refs_0_, bf16[16,32,256]{2,1,0:T(8,128)(2,1)S(1)} %get-tuple-element.22.refs_1_, bf16[8,32,128]{2,1,0:T(8,128)(2,1)S(1)} %get-tuple-element.23.refs_2_, bf16[4,32,128]{2,1,0:T(8,128)(2,1)S(1)} %get-tuple-element.24.refs_3_, ...), custom_call_target="tpu_custom_call" | custom-call | flops 909901824 | bytes 3121152 | tf_op jit(solution)/shard_map/last/pallas_call | solution.py:579
  17.6 0.0 collective-permute-done.6.got
  17.6 0.8 %add.1 = f32[6,4,16,64]{3,2,1,0:T(8,128)} custom-call(f32[6,4,16,64]{3,2,1,0:T(8,128)S(1)} %last.1.own, bf16[96,128]{1,0:T(8,128)(2,1)S(1)} %collective-permute-done.6.got), custom_call_target="tpu_custom_call" | custom-call | bytes 221184 | tf_op jit(solution)/shard_map/add/pallas_call | solution.py:579
  (1 shorter events, 0.0 us)
Async XLA Ops:
  1.2 7.7 %collective-permute-start = (bf16[176,256]{1,0:T(8,128)(2,1)S(1)}, bf16[176,256]{1,0:T(8,128)(2,1)S(1)}, u32[]{:S(2)}, u32[]{:S(2)}) collective-permute-start(bf16[176,256]{1,0:T(8,128)(2,1)S(1)} %get-tuple-element.19), channel_id=1, source_target_pairs={{0,2},{2,0},{4,6},{6,4},{8,10},{10,8},{12,14},{14,12},{1,3},{3,1},... | collective-permute-start | bytes 270344 | tf_op jit(solution)/shard_map/ppermute | solution.py:626
  1.3 7.6 %collective-permute-start.1 = (bf16[176,256]{1,0:T(8,128)(2,1)S(1)}, bf16[176,256]{1,0:T(8,128)(2,1)S(1)}, u32[]{:S(2)}, u32[]{:S(2)}) collective-permute-start(bf16[176,256]{1,0:T(8,128)(2,1)S(1)} %get-tuple-element.20), channel_id=1, source_target_pairs={{2,4},{6,8},{10,12},{4,2},{8,6},{12,10},{3,5},{7,9},{11,13},{5,3},... | collective-permute-start | bytes 270344 | tf_op jit(solution)/shard_map/ppermute | solution.py:625
  6.2 7.0 %collective-permute-start.2 = (bf16[480,128]{1,0:T(8,128)(2,1)S(1)}, bf16[480,128]{1,0:T(8,128)(2,1)S(1)}, u32[]{:S(2)}, u32[]{:S(2)}) collective-permute-start(bf16[480,128]{1,0:T(8,128)(2,1)S(1)} %get-tuple-element.25), channel_id=1, source_target_pairs={{0,16},{16,0},{1,17},{17,1},{2,18},{18,2},{3,19},{19,3},{4,20},{20... | collective-permute-start | bytes 368648 | tf_op jit(solution)/shard_map/ppermute | solution.py:637
  9.4 3.9 %collective-permute-start.3 = (bf16[176,128]{1,0:T(8,128)(2,1)S(1)}, bf16[176,128]{1,0:T(8,128)(2,1)S(1)}, u32[]{:S(2)}, u32[]{:S(2)}) collective-permute-start(bf16[176,128]{1,0:T(8,128)(2,1)S(1)} %get-tuple-element.26), channel_id=1, source_target_pairs={{0,16},{16,0},{1,17},{17,1},{2,18},{18,2},{3,19},{19,3},{4,20},{20... | collective-permute-start | bytes 135176 | tf_op jit(solution)/shard_map/ppermute | solution.py:646
  10.3 4.8 %collective-permute-start.4 = (bf16[9,16,128]{2,1,0:T(8,128)(2,1)S(1)}, bf16[9,16,128]{2,1,0:T(8,128)(2,1)S(1)}, u32[]{:S(2)}, u32[]{:S(2)}) collective-permute-start(bf16[9,16,128]{2,1,0:T(8,128)(2,1)S(1)} %get-tuple-element.27), channel_id=1, source_target_pairs={{0,17},{1,16},{16,1},{17,0},{2,19},{3,18},{18,3},{19,2},{4,21},{5,... | collective-permute-start | bytes 110600 | tf_op jit(solution)/shard_map/ppermute | solution.py:655
  11.9 3.3 %collective-permute-start.5 = (bf16[12,16,128]{2,1,0:T(8,128)(2,1)S(1)}, bf16[12,16,128]{2,1,0:T(8,128)(2,1)S(1)}, u32[]{:S(2)}, u32[]{:S(2)}) collective-permute-start(bf16[12,16,128]{2,1,0:T(8,128)(2,1)S(1)} %get-tuple-element.29), channel_id=1, source_target_pairs={{0,1},{1,0},{2,3},{3,2},{4,5},{5,4},{6,7},{7,6},{8,9},{9,8},{10,11... | collective-permute-start | bytes 147464 | tf_op jit(solution)/shard_map/ppermute | solution.py:654
  14.4 3.2 %collective-permute-start.6 = (bf16[96,128]{1,0:T(8,128)(2,1)S(1)}, bf16[96,128]{1,0:T(8,128)(2,1)S(1)}, u32[]{:S(2)}, u32[]{:S(2)}) collective-permute-start(bf16[96,128]{1,0:T(8,128)(2,1)S(1)} %get-tuple-element.30), channel_id=1, source_target_pairs={{0,16},{16,0},{1,17},{17,1},{2,18},{18,2},{3,19},{19,3},{4,20},{20... | collective-permute-start | bytes 73736 | tf_op jit(solution)/shard_map/ppermute | solution.py:669

commit v8 on v7

--- a/solution.py
+++ b/solution.py
@@ -344,8 +344,8 @@
     pass
 
 
-FIRST = {True: 5, False: 3}
-LAST = {True: 8, False: 10}
+FIRST = {True: 5, False: 4}
+LAST = {True: 8, False: 9}
 GROUP = 4
 EDGE = R
 

time: 18.6 us -> 18.8 us (1.011)
  starting transfers between devices: 9.33 us -> 9.55 us
    ppermute x1, starting transfers between devices: 0.67 us -> 0.89 us  [per_device(): sums = lax.ppermute(send, 'gz', swap)]
  transfers between devices with their start and end apart: 7 -> 7, of which waited for: 0 -> 0; matrix products, arithmetic and copies ran while one was open for 8% -> 8% of each run, Pallas kernels for 30% -> 29%
where the time goes in v8:
time: 18.8 us; the launch traced here: 18.6 us
  starting transfers between devices  9.55 us (51%)
  Pallas kernels  7.48 us (40%)
  local copies, waits for them, and re-layouts  1.48 us (8%)
    pallas_call x9, Pallas kernels, call(): pl.pallas_call(body, out_shape=list(outs), in_specs=[hbm] * n_hbm + [vmem...  7.48 us
    ppermute x1, starting transfers between devices, per_device(): r2 = lax.ppermute(s2, 'row', inner)  4.55 us
    ppermute x1, starting transfers between devices, per_device(): zxs.append(lax.ppermute(messages[n_side + side], ('gz', 'col'), both))  1.56 us
    unnamed x1, local copies, waits for them, and re-layouts  1.48 us
    ppermute x1, starting transfers between devices, per_device(): zown = lax.ppermute(zmsg, 'gz', swap)  1.27 us
    ppermute x1, starting transfers between devices, per_device(): zcorner = lax.ppermute(zcmsg, 'gz', swap)  0.93 us
    ppermute x1, starting transfers between devices, per_device(): sums = lax.ppermute(send, 'gz', swap)  0.89 us
  transfers between devices with their start and end apart: 7, of which 0 were waited for; matrix products, arithmetic and copies ran while one was open for 8% of the time, Pallas kernels for 29%

profile of v8, /device:TPU:1, one launch (start us, length us, event | category | flops | bytes accessed | tf_op | source)
XLA Modules:
  0.0 18.6 jit_solution(1401739001666105196)
XLA Ops:
  0.0 1.2 %load.1 = (bf16[176,256]{1,0:T(8,128)(2,1)S(1)}, bf16[176,256]{1,0:T(8,128)(2,1)S(1)}, bf16[16,64,256]{2,1,0:T(8,128)(2,1)S(1)}) custom-call(bf16[16,64,256]{2,1,0:T(8,128)(2,1)} %vol.1), custom_call_target="tpu_custom_call" | custom-call | bytes 1228800 | tf_op jit(solution)/shard_map/load/pallas_call | solution.py:579
  1.2 0.1 collective-permute-start
  1.3 4.6 %collective-permute-start.1 = (bf16[176,256]{1,0:T(8,128)(2,1)S(1)}, bf16[176,256]{1,0:T(8,128)(2,1)S(1)}, u32[]{:S(2)}, u32[]{:S(2)}) collective-permute-start(bf16[176,256]{1,0:T(8,128)(2,1)S(1)} %get-tuple-element.20), channel_id=1, source_target_pairs={{2,4},{6,8},{10,12},{4,2},{8,6},{12,10},{3,5},{7,9},{11,13},{5,3},... | collective-permute-start | bytes 270344 | tf_op jit(solution)/shard_map/ppermute | solution.py:625
  5.9 0.3 %edges.1 = (bf16[8,32,128]{2,1,0:T(8,128)(2,1)S(1)}, bf16[480,128]{1,0:T(8,128)(2,1)S(1)}, bf16[8,16,128]{2,1,0:T(8,128)(2,1)S(1)}) custom-call(bf16[16,64,256]{2,1,0:T(8,128)(2,1)S(1)} %get-tuple-element.18.refs_0_), custom_call_target="tpu_custom_call" | custom-call | bytes 745472 | tf_op jit(solution)/shard_map/edges/pallas_call | solution.py:579
  6.2 1.3 %collective-permute-start.2 = (bf16[480,128]{1,0:T(8,128)(2,1)S(1)}, bf16[480,128]{1,0:T(8,128)(2,1)S(1)}, u32[]{:S(2)}, u32[]{:S(2)}) collective-permute-start(bf16[480,128]{1,0:T(8,128)(2,1)S(1)} %get-tuple-element.25), channel_id=1, source_target_pairs={{0,16},{16,0},{1,17},{17,1},{2,18},{18,2},{3,19},{19,3},{4,20},{20... | collective-permute-start | bytes 368648 | tf_op jit(solution)/shard_map/ppermute | solution.py:637
  7.5 1.5 %copy.6.w = bf16[3504,256]{1,0:T(8,128)(2,1)S(1)} copy(bf16[3504,256]{1,0:T(8,128)(2,1)} %constant.2.clone) | data formatting | bytes 3588096
  9.0 0.0 collective-permute-done.refs_0_
  9.0 0.0 collective-permute-done.1.refs_1_
  9.0 0.4 %pack.1 = (bf16[16,32,256]{2,1,0:T(8,128)(2,1)S(1)}, bf16[4,32,128]{2,1,0:T(8,128)(2,1)S(1)}, bf16[176,128]{1,0:T(8,128)(2,1)S(1)}, bf16[12,16,128]{2,1,0:T(8,128)(2,1)S(1)}, bf16[9,16,128]{2,1,0:T(8,128)(2,1)S(1)}) custom-call(bf16[176,256]{1,0:T(8,128)(2,1)S(1)} %collective-permute-done.refs_0_, bf16[176,256]{1,0:T(8,128)(2,1)S(1)} %collective-permute-done.1.refs_1_, ...), custom_call_target="tpu_custom_call" | custom-call | bytes 2433024 | tf_op jit(solution)/shard_map/pack/pallas_call | solution.py:579
  9.4 0.9 %collective-permute-start.3 = (bf16[176,128]{1,0:T(8,128)(2,1)S(1)}, bf16[176,128]{1,0:T(8,128)(2,1)S(1)}, u32[]{:S(2)}, u32[]{:S(2)}) collective-permute-start(bf16[176,128]{1,0:T(8,128)(2,1)S(1)} %get-tuple-element.26), channel_id=1, source_target_pairs={{0,16},{16,0},{1,17},{17,1},{2,18},{18,2},{3,19},{19,3},{4,20},{20... | collective-permute-start | bytes 135176 | tf_op jit(solution)/shard_map/ppermute | solution.py:646
  10.3 1.6 %collective-permute-start.4 = (bf16[9,16,128]{2,1,0:T(8,128)(2,1)S(1)}, bf16[9,16,128]{2,1,0:T(8,128)(2,1)S(1)}, u32[]{:S(2)}, u32[]{:S(2)}) collective-permute-start(bf16[9,16,128]{2,1,0:T(8,128)(2,1)S(1)} %get-tuple-element.27), channel_id=1, source_target_pairs={{0,17},{1,16},{16,1},{17,0},{2,19},{3,18},{18,3},{19,2},{4,21},{5,... | collective-permute-start | bytes 110600 | tf_op jit(solution)/shard_map/ppermute | solution.py:655
  11.9 0.2 %collective-permute-start.5 = (bf16[12,16,128]{2,1,0:T(8,128)(2,1)S(1)}, bf16[12,16,128]{2,1,0:T(8,128)(2,1)S(1)}, u32[]{:S(2)}, u32[]{:S(2)}) collective-permute-start(bf16[12,16,128]{2,1,0:T(8,128)(2,1)S(1)} %get-tuple-element.29), channel_id=1, source_target_pairs={{0,1},{1,0},{2,3},{3,2},{4,5},{5,4},{6,7},{7,6},{8,9},{9,8},{10,11... | collective-permute-start | bytes 147464 | tf_op jit(solution)/shard_map/ppermute | solution.py:654
  12.1 1.2 %first.1.refs_4_.refs_5_ = f32[5,96,64]{2,1,0:T(8,128)S(1)} custom-call(bf16[16,64,256]{2,1,0:T(8,128)(2,1)S(1)} %get-tuple-element.18.refs_0_, bf16[16,32,256]{2,1,0:T(8,128)(2,1)S(1)} %get-tuple-element.22.refs_1_, bf16[3504,256]{1,0:T(8,128)(2,1)S(1)} %stage.1.refs_2_.refs_5_.refs_7_), custom_call_target="tpu_custom_call" | custom-call | flops 349962240 | bytes 2703360 | tf_op jit(solution)/shard_map/first/pallas_call | solution.py:579
  13.2 0.0 collective-permute-done.2.zown.refs_2_
  13.2 0.0 collective-permute-done.3.zcorner.refs_3_
  13.3 1.1 %near.1 = (f32[3,96,64]{2,1,0:T(8,128)S(1)}, bf16[96,128]{1,0:T(8,128)(2,1)S(1)}) custom-call(bf16[16,64,256]{2,1,0:T(8,128)(2,1)S(1)} %get-tuple-element.18.refs_0_, bf16[16,32,256]{2,1,0:T(8,128)(2,1)S(1)} %get-tuple-element.22.refs_1_, bf16[480,128]{1,0:T(8,128)(2,1)S(1)} %collective-permute-done.2.zown.refs_2_, ...), custom_call_target="tpu_custom_call" | custom-call | flops 209977344 | bytes 2969600 | tf_op jit(solution)/shard_map/near/pallas_call | solution.py:579
  14.4 0.9 %collective-permute-start.6 = (bf16[96,128]{1,0:T(8,128)(2,1)S(1)}, bf16[96,128]{1,0:T(8,128)(2,1)S(1)}, u32[]{:S(2)}, u32[]{:S(2)}) collective-permute-start(bf16[96,128]{1,0:T(8,128)(2,1)S(1)} %get-tuple-element.30), channel_id=1, source_target_pairs={{0,16},{16,0},{1,17},{17,1},{2,18},{18,2},{3,19},{19,3},{4,20},{20... | collective-permute-start | bytes 73736 | tf_op jit(solution)/shard_map/ppermute | solution.py:669
  15.3 0.0 collective-permute-done.4.refs_0_
  15.3 0.1 beyond.1.refs_4_
  15.4 0.0 collective-permute-done.5.refs_8_
  15.4 2.4 %last.1.own = f32[6,4,16,64]{3,2,1,0:T(8,128)S(1)} custom-call(bf16[16,64,256]{2,1,0:T(8,128)(2,1)S(1)} %get-tuple-element.18.refs_0_, bf16[16,32,256]{2,1,0:T(8,128)(2,1)S(1)} %get-tuple-element.22.refs_1_, bf16[8,32,128]{2,1,0:T(8,128)(2,1)S(1)} %get-tuple-element.23.refs_2_, bf16[4,32,128]{2,1,0:T(8,128)(2,1)S(1)} %get-tuple-element.24.refs_3_, ...), custom_call_target="tpu_custom_call" | custom-call | flops 839909376 | bytes 3121152 | tf_op jit(solution)/shard_map/last/pallas_call | solution.py:579
  17.8 0.0 collective-permute-done.6.got
  17.8 0.8 %add.1 = f32[6,4,16,64]{3,2,1,0:T(8,128)} custom-call(f32[6,4,16,64]{3,2,1,0:T(8,128)S(1)} %last.1.own, bf16[96,128]{1,0:T(8,128)(2,1)S(1)} %collective-permute-done.6.got), custom_call_target="tpu_custom_call" | custom-call | bytes 221184 | tf_op jit(solution)/shard_map/add/pallas_call | solution.py:579
  (1 shorter events, 0.0 us)
Async XLA Ops:
  1.2 7.7 %collective-permute-start = (bf16[176,256]{1,0:T(8,128)(2,1)S(1)}, bf16[176,256]{1,0:T(8,128)(2,1)S(1)}, u32[]{:S(2)}, u32[]{:S(2)}) collective-permute-start(bf16[176,256]{1,0:T(8,128)(2,1)S(1)} %get-tuple-element.19), channel_id=1, source_target_pairs={{0,2},{2,0},{4,6},{6,4},{8,10},{10,8},{12,14},{14,12},{1,3},{3,1},... | collective-permute-start | bytes 270344 | tf_op jit(solution)/shard_map/ppermute | solution.py:626
  1.3 7.6 %collective-permute-start.1 = (bf16[176,256]{1,0:T(8,128)(2,1)S(1)}, bf16[176,256]{1,0:T(8,128)(2,1)S(1)}, u32[]{:S(2)}, u32[]{:S(2)}) collective-permute-start(bf16[176,256]{1,0:T(8,128)(2,1)S(1)} %get-tuple-element.20), channel_id=1, source_target_pairs={{2,4},{6,8},{10,12},{4,2},{8,6},{12,10},{3,5},{7,9},{11,13},{5,3},... | collective-permute-start | bytes 270344 | tf_op jit(solution)/shard_map/ppermute | solution.py:625
  6.2 7.0 %collective-permute-start.2 = (bf16[480,128]{1,0:T(8,128)(2,1)S(1)}, bf16[480,128]{1,0:T(8,128)(2,1)S(1)}, u32[]{:S(2)}, u32[]{:S(2)}) collective-permute-start(bf16[480,128]{1,0:T(8,128)(2,1)S(1)} %get-tuple-element.25), channel_id=1, source_target_pairs={{0,16},{16,0},{1,17},{17,1},{2,18},{18,2},{3,19},{19,3},{4,20},{20... | collective-permute-start | bytes 368648 | tf_op jit(solution)/shard_map/ppermute | solution.py:637
  9.4 3.9 %collective-permute-start.3 = (bf16[176,128]{1,0:T(8,128)(2,1)S(1)}, bf16[176,128]{1,0:T(8,128)(2,1)S(1)}, u32[]{:S(2)}, u32[]{:S(2)}) collective-permute-start(bf16[176,128]{1,0:T(8,128)(2,1)S(1)} %get-tuple-element.26), channel_id=1, source_target_pairs={{0,16},{16,0},{1,17},{17,1},{2,18},{18,2},{3,19},{19,3},{4,20},{20... | collective-permute-start | bytes 135176 | tf_op jit(solution)/shard_map/ppermute | solution.py:646
  10.3 5.0 %collective-permute-start.4 = (bf16[9,16,128]{2,1,0:T(8,128)(2,1)S(1)}, bf16[9,16,128]{2,1,0:T(8,128)(2,1)S(1)}, u32[]{:S(2)}, u32[]{:S(2)}) collective-permute-start(bf16[9,16,128]{2,1,0:T(8,128)(2,1)S(1)} %get-tuple-element.27), channel_id=1, source_target_pairs={{0,17},{1,16},{16,1},{17,0},{2,19},{3,18},{18,3},{19,2},{4,21},{5,... | collective-permute-start | bytes 110600 | tf_op jit(solution)/shard_map/ppermute | solution.py:655
  11.9 3.6 %collective-permute-start.5 = (bf16[12,16,128]{2,1,0:T(8,128)(2,1)S(1)}, bf16[12,16,128]{2,1,0:T(8,128)(2,1)S(1)}, u32[]{:S(2)}, u32[]{:S(2)}) collective-permute-start(bf16[12,16,128]{2,1,0:T(8,128)(2,1)S(1)} %get-tuple-element.29), channel_id=1, source_target_pairs={{0,1},{1,0},{2,3},{3,2},{4,5},{5,4},{6,7},{7,6},{8,9},{9,8},{10,11... | collective-permute-start | bytes 147464 | tf_op jit(solution)/shard_map/ppermute | solution.py:654
  14.4 3.4 %collective-permute-start.6 = (bf16[96,128]{1,0:T(8,128)(2,1)S(1)}, bf16[96,128]{1,0:T(8,128)(2,1)S(1)}, u32[]{:S(2)}, u32[]{:S(2)}) collective-permute-start(bf16[96,128]{1,0:T(8,128)(2,1)S(1)} %get-tuple-element.30), channel_id=1, source_target_pairs={{0,16},{16,0},{1,17},{17,1},{2,18},{18,2},{3,19},{19,3},{4,20},{20... | collective-permute-start | bytes 73736 | tf_op jit(solution)/shard_map/ppermute | solution.py:669

commit v9 on v7

--- a/solution.py
+++ b/solution.py
@@ -249,7 +249,7 @@
     copies[2].wait()
 
 
-def column_select(n_col, cols):
+def column_select(n_col, cols, odd):
     n_side = 1 if n_col == 2 else 2
     shape = (SLOTS + 16 * n_side, cols)
     row = lax.broadcasted_iota(jnp.int32, shape, 0)
@@ -259,18 +259,38 @@
     )
     for side in range(n_side):
         if n_col == 2:
-            first = jnp.where(lax.axis_index("col") == 0, cols - HALO, 0)
+            here = lax.axis_index("col")
+            near = jnp.where(here == 0, cols - 8, 0)
+            behind = jnp.where(here == 0, cols - NEED, -NEED)
         else:
-            first = (cols - HALO, 0)[side]
+            near = (cols - 8, 0)[side]
+            behind = (cols - NEED, -NEED)[side]
         at = row - SLOTS - 16 * side
-        picked = picked | ((at >= 0) & (at < 16) & (lane == at + first))
+        picked = picked | ((at >= 0) & (at < 8) & (lane == at + near))
+        at = at - 8 - (1 if odd else 5)
+        picked = picked | ((at >= 0) & (at < 3) & (lane == at + behind))
     return jnp.where(picked, 1.0, 0.0).astype(BF16)
 
 
-def pick_columns(select, source):
-    picked = lax.dot_general(select, source, NT, preferred_element_type=F32)
-    messages = [picked[at : at + 16].astype(BF16) for at in range(SLOTS, picked.shape[0], 16)]
-    return picked[0:SLOTS].astype(BF16), picked[8:24].astype(BF16), messages
+def pick_columns(selects, sources, n_side):
+    slots, middles = [], []
+    near, behind = [[] for _ in range(n_side)], [[] for _ in range(n_side)]
+    for b, source in enumerate(sources):
+        picked = lax.dot_general(selects[b % 2], source, NT, preferred_element_type=F32)
+        slots.append(picked[0:SLOTS].astype(BF16))
+        middles.append(picked[8:24].astype(BF16))
+        for side in range(n_side):
+            at = SLOTS + 16 * side
+            near[side].append(picked[at : at + 8])
+            part = picked[at + 8 : at + 16]
+            if b % 2:
+                behind[side][-1] = behind[side][-1] + part
+            else:
+                behind[side].append(part)
+    messages = [
+        jnp.concatenate(near[side] + behind[side], axis=0).astype(BF16) for side in range(n_side)
+    ]
+    return slots, middles, messages
 
 
 def halve(chunk, at, value):
@@ -287,13 +307,13 @@
     depth, rows, cols = vol.shape
     gz = lax.axis_index("gz")
     refs, middles = refs[:-1], refs[-1]
-    select = column_select(n_col, cols)
+    selects = [column_select(n_col, cols, odd) for odd in (False, True)]
+    sources = [vol[2 * b : 2 * b + 2].reshape(2 * rows, cols) for b in range(depth // 2)]
+    slots, middle, messages = pick_columns(selects, sources, len(refs))
     for b in range(depth // 2):
-        source = vol[2 * b : 2 * b + 2].reshape(2 * rows, cols)
-        slots, middle, messages = pick_columns(select, source)
-        own[b], middles[b] = slots, middle
-        for ref, message in zip(refs, messages):
-            ref[b] = message
+        own[b], middles[b] = slots[b], middle[b]
+    for ref, message in zip(refs, messages):
+        ref[...] = message
     base = jnp.where(gz == 0, depth - R, 0)
     halve(zmsg, 0, vol[pl.ds(base, R)].reshape(R * rows, cols))
     first = jnp.where(gz == 0, (depth - EXTRA) // 2, 0)
@@ -317,27 +337,33 @@
     ):
         out = jnp.dot(get(name), part, preferred_element_type=F32).astype(BF16)
         yud[:, at : at + HALO, :] = out.reshape(depth, HALO, cols)
-    select = column_select(n_col, cols)
+    selects = [column_select(n_col, cols, odd) for odd in (False, True)]
     pairs, quads = depth // 2, depth // 4
+    sources = [yud[4 * b : 4 * b + 4].reshape(4 * 2 * HALO, cols) for b in range(quads)]
+    slots, middle, messages = pick_columns(selects, sources, n_side)
     for b in range(quads):
-        source = yud[4 * b : 4 * b + 4].reshape(4 * 2 * HALO, cols)
-        slots, middle, messages = pick_columns(select, source)
-        halo[b] = slots
-        middles[b] = middle
-        for ref, message in zip(xmsgs, messages):
-            ref[pairs + b] = message
-    for ref, part in zip(xmsgs, xown):
-        ref[0:pairs] = part[...]
+        halo[b], middles[b] = slots[b], middle[b]
+    n2, n4 = EXTRA // 2, EXTRA // 4
+    low = gz == 0
+    first2 = jnp.where(low, pairs - n2, 0)
+    first4 = jnp.where(low, quads - n4, 0)
+    skip = 8 * (pairs - n2)
+    for x_own, message, xmsg, zxmsg in zip(xown, messages, xmsgs, zxmsgs):
+        split = x_own.shape[0]
+        xmsg[0:split] = x_own[...]
+        xmsg[split:] = message
+        zxmsg[0 : 8 * n2] = x_own[pl.ds(pl.multiple_of(8 * first2, 16), 8 * n2)]
+        zxmsg[8 * n2 : 8 * n2 + message.shape[0]] = message
+        at = 8 * n2 + message.shape[0]
+        behind = x_own[8 * pairs :]
+        sent = 4 * n2
+        zxmsg[at : at + sent] = jnp.where(
+            low, behind[skip // 2 : skip // 2 + sent], behind[0:sent]
+        )
     base = jnp.where(gz == 0, depth - R, 0)
     edge = yud[pl.ds(base, R)].reshape(R * 2 * HALO, cols)
     halve(zcorner, 0, jnp.dot(get("corner"), edge, preferred_element_type=F32).astype(BF16))
-    n2, n4 = EXTRA // 2, EXTRA // 4
-    first2 = jnp.where(gz == 0, pairs - n2, 0)
-    first4 = jnp.where(gz == 0, quads - n4, 0)
     zcorner[128:] = middles[pl.ds(first4, n4)].reshape(n4 * 16, 128)
-    for ref, message in zip(zxmsgs, xmsgs):
-        ref[0:n2] = message[pl.ds(first2, n2)]
-        ref[n2:] = message[pl.ds(pairs + first4, n4)]
 
 
 def stage_kernel(w, w_out):
@@ -433,9 +459,17 @@
     else:
         keep = (slots < 8) | (slots >= 21)
 
-    def join(part, messages, b):
-        sides = [messages[-1][b].astype(F32), messages[0][b].astype(F32)]
-        return jnp.where(keep, jnp.concatenate(sides, axis=0), part)
+    def join(part, messages, at, behind_at, b):
+        def eight(message, start, i):
+            first = start + 16 * (i // 2)
+            return message[first : first + 16].astype(F32)[8 * (i % 2) : 8 * (i % 2) + 8]
+
+        left, right = messages[0], messages[-1]
+        behind = eight(left, behind_at, b // 2)
+        if b % 2:
+            behind = pltpu.roll(behind, 4, 0)
+        rows_of = [eight(right, at, b), jnp.zeros((8, 128), F32), behind, eight(left, at, b)]
+        return jnp.where(keep, jnp.concatenate(rows_of, axis=0), part)
 
     lanes = lax.broadcasted_iota(jnp.int32, (SLOTS, 128), 1)
 
@@ -454,7 +488,7 @@
     return join, layers_of
 
 
-def beyond_kernel(n_col, rows, zown, zcorner, zxs, out):
+def beyond_kernel(n_col, n_quads, rows, zown, zcorner, zxs, out):
     join, layers_of = strip_tools(n_col, rows)
 
     def from_middle(ref, at, b):
@@ -463,12 +497,23 @@
         return jnp.concatenate([rim, middle, rim], axis=0)
 
     n2, n4 = EXTRA // 2, EXTRA // 4
-    layers = layers_of(
-        [join(from_middle(zown, 2 * R * rows, b), zxs, b) for b in range(n2)],
-        [join(from_middle(zcorner, 128, b), zxs, n2 + b) for b in range(n4)],
-    )
-    for k, layer in enumerate(layers):
-        out[k] = layer.astype(BF16)
+    far_at = 8 * n2
+    far_behind = far_at + 8 * n_quads
+    behind_at = far_behind + 4 * n_quads
+
+    def body(low):
+        first = 0 if low else n_quads - n4
+        layers = layers_of(
+            [join(from_middle(zown, 2 * R * rows, b), zxs, 0, behind_at, b) for b in range(n2)],
+            [
+                join(from_middle(zcorner, 128, b), zxs, far_at, far_behind, first + b)
+                for b in range(n4)
+            ],
+        )
+        for k, layer in enumerate(layers):
+            out[k] = layer.astype(BF16)
+
+    by_half(body)
 
 
 def last_kernel(place_of, zs, n_row, n_col, vol, yud, own, halo, far, u1, u2, w, xs, own_ref,
@@ -499,8 +544,11 @@
 
         layers_to_sums(get, ysm, load, LAST[low], (rows, cols), u3, *scratch)
         own_layers = layers_of(
-            [join(own[b].astype(F32), xs, b) for b in range(depth // 2)],
-            [join(halo[b].astype(F32), xs, depth // 2 + b) for b in range(depth // 4)],
+            [join(own[b].astype(F32), xs, 0, 4 * depth, b) for b in range(depth // 2)],
+            [
+                join(halo[b].astype(F32), xs, 6 * depth, 8 * depth, b)
+                for b in range(depth // 4)
+            ],
         )
         beyond = [far[k].astype(F32) for k in range(EXTRA)]
         zero = [jnp.zeros((SLOTS, 128), F32)] * R
@@ -630,7 +678,7 @@
     own, zmsg, *xown = call(
         lambda *refs: edges_kernel(n_col, *refs),
         [bf16(pairs, SLOTS, 128), bf16(2 * R * rows + n2 * 16, 128)]
-        + [bf16(pairs, HALO, 128)] * n_side,
+        + [bf16(12 * pairs, 128)] * n_side,
         [vol], [pltpu.VMEM((pairs, 16, 128), BF16)], "edges",
     )
     swap = [(0, 1), (1, 0)]
@@ -639,8 +687,8 @@
     yud, halo, zcmsg, *messages = call(
         lambda *refs: pack_kernel(place_of, n_col, *refs),
         [bf16(depth, 2 * HALO, cols), bf16(quads, SLOTS, 128), bf16(128 + n4 * 16, 128)]
-        + [bf16(pairs + quads, HALO, 128)] * n_side
-        + [bf16(n2 + n4, HALO, 128)] * n_side,
+        + [bf16(12 * (pairs + quads), 128)] * n_side
+        + [bf16(12 * (n2 + quads) + 8, 128)] * n_side,
         [r1, r2, w] + xown, [pltpu.VMEM((quads, 16, 128), BF16)], "pack",
     )
     zcorner = lax.ppermute(zcmsg, "gz", swap)
@@ -670,9 +718,9 @@
 
     (far,) = call(
         lambda zown, zcorner, *refs: beyond_kernel(
-            n_col, rows, zown, zcorner, refs[:n_side], refs[n_side]
+            n_col, quads, rows, zown, zcorner, refs[:n_side], refs[n_side]
         ),
-        [bf16(EXTRA, SLOTS, 128)], [zown, zcorner] + zxs, [], "beyond", flops=EDGE * layer_flops,
+        [bf16(EXTRA, SLOTS, 128)], [zown, zcorner] + zxs, [], "beyond", flops=layer_flops,
     )
 
     def last_body(*refs):

time: 18.6 us -> 18.6 us (level)
  no operation moved by 1% of the time
where the time goes in v9:
time: 18.6 us; the launch traced here: 18.4 us
  starting transfers between devices  9.34 us (50%)
  Pallas kernels  7.45 us (40%)
  local copies, waits for them, and re-layouts  1.48 us (8%)
    pallas_call x9, Pallas kernels, call(): pl.pallas_call(body, out_shape=list(outs), in_specs=[hbm] * n_hbm + [vmem...  7.45 us
    ppermute x1, starting transfers between devices, per_device(): r2 = lax.ppermute(s2, 'row', inner)  4.55 us
    ppermute x1, starting transfers between devices, per_device(): zxs.append(lax.ppermute(messages[n_side + side], ('gz', 'col'), both))  1.56 us
    unnamed x1, local copies, waits for them, and re-layouts  1.48 us
    ppermute x1, starting transfers between devices, per_device(): zown = lax.ppermute(zmsg, 'gz', swap)  1.27 us
    ppermute x1, starting transfers between devices, per_device(): zcorner = lax.ppermute(zcmsg, 'gz', swap)  0.92 us
    ppermute x1, starting transfers between devices, per_device(): sums = lax.ppermute(send, 'gz', swap)  0.67 us
  transfers between devices with their start and end apart: 7, of which 0 were waited for; matrix products, arithmetic and copies ran while one was open for 8% of the time, Pallas kernels for 30%

profile of v9, /device:TPU:1, one launch (start us, length us, event | category | flops | bytes accessed | tf_op | source)
XLA Modules:
  0.0 18.4 jit_solution(14336252352400928249)
XLA Ops:
  0.0 1.2 %load.1 = (bf16[176,256]{1,0:T(8,128)(2,1)S(1)}, bf16[176,256]{1,0:T(8,128)(2,1)S(1)}, bf16[16,64,256]{2,1,0:T(8,128)(2,1)S(1)}) custom-call(bf16[16,64,256]{2,1,0:T(8,128)(2,1)} %vol.1), custom_call_target="tpu_custom_call" | custom-call | bytes 1228800 | tf_op jit(solution)/shard_map/load/pallas_call | solution.py:627
  1.2 0.1 collective-permute-start
  1.3 4.6 %collective-permute-start.1 = (bf16[176,256]{1,0:T(8,128)(2,1)S(1)}, bf16[176,256]{1,0:T(8,128)(2,1)S(1)}, u32[]{:S(2)}, u32[]{:S(2)}) collective-permute-start(bf16[176,256]{1,0:T(8,128)(2,1)S(1)} %get-tuple-element.20), channel_id=1, source_target_pairs={{2,4},{6,8},{10,12},{4,2},{8,6},{12,10},{3,5},{7,9},{11,13},{5,3},... | collective-permute-start | bytes 270344 | tf_op jit(solution)/shard_map/ppermute | solution.py:673
  5.9 0.3 %edges.1 = (bf16[8,32,128]{2,1,0:T(8,128)(2,1)S(1)}, bf16[480,128]{1,0:T(8,128)(2,1)S(1)}, bf16[96,128]{1,0:T(8,128)(2,1)S(1)}) custom-call(bf16[16,64,256]{2,1,0:T(8,128)(2,1)S(1)} %get-tuple-element.18.refs_0_), custom_call_target="tpu_custom_call" | custom-call | bytes 737280 | tf_op jit(solution)/shard_map/edges/pallas_call | solution.py:627
  6.2 1.3 %collective-permute-start.2 = (bf16[480,128]{1,0:T(8,128)(2,1)S(1)}, bf16[480,128]{1,0:T(8,128)(2,1)S(1)}, u32[]{:S(2)}, u32[]{:S(2)}) collective-permute-start(bf16[480,128]{1,0:T(8,128)(2,1)S(1)} %get-tuple-element.25), channel_id=1, source_target_pairs={{0,16},{16,0},{1,17},{17,1},{2,18},{18,2},{3,19},{19,3},{4,20},{20... | collective-permute-start | bytes 368648 | tf_op jit(solution)/shard_map/ppermute | solution.py:685
  7.5 1.5 %copy.6.w = bf16[3504,256]{1,0:T(8,128)(2,1)S(1)} copy(bf16[3504,256]{1,0:T(8,128)(2,1)} %constant.2.clone) | data formatting | bytes 3588096
  9.0 0.0 collective-permute-done.refs_0_
  9.0 0.0 collective-permute-done.1.refs_1_
  9.0 0.4 %pack.1 = (bf16[16,32,256]{2,1,0:T(8,128)(2,1)S(1)}, bf16[4,32,128]{2,1,0:T(8,128)(2,1)S(1)}, bf16[176,128]{1,0:T(8,128)(2,1)S(1)}, bf16[144,128]{1,0:T(8,128)(2,1)S(1)}, bf16[128,128]{1,0:T(8,128)(2,1)S(1)}) custom-call(bf16[176,256]{1,0:T(8,128)(2,1)S(1)} %collective-permute-done.refs_0_, bf16[176,256]{1,0:T(8,128)(2,1)S(1)} %collective-permute-done.1.refs_1_, ...), custom_call_target="tpu_custom_call" | custom-call | bytes 2408448 | tf_op jit(solution)/shard_map/pack/pallas_call | solution.py:627
  9.4 0.9 %collective-permute-start.3 = (bf16[176,128]{1,0:T(8,128)(2,1)S(1)}, bf16[176,128]{1,0:T(8,128)(2,1)S(1)}, u32[]{:S(2)}, u32[]{:S(2)}) collective-permute-start(bf16[176,128]{1,0:T(8,128)(2,1)S(1)} %get-tuple-element.26), channel_id=1, source_target_pairs={{0,16},{16,0},{1,17},{17,1},{2,18},{18,2},{3,19},{19,3},{4,20},{20... | collective-permute-start | bytes 135176 | tf_op jit(solution)/shard_map/ppermute | solution.py:694
  10.3 1.6 %collective-permute-start.4 = (bf16[128,128]{1,0:T(8,128)(2,1)S(1)}, bf16[128,128]{1,0:T(8,128)(2,1)S(1)}, u32[]{:S(2)}, u32[]{:S(2)}) collective-permute-start(bf16[128,128]{1,0:T(8,128)(2,1)S(1)} %get-tuple-element.27), channel_id=1, source_target_pairs={{0,17},{1,16},{16,1},{17,0},{2,19},{3,18},{18,3},{19,2},{4,21},{5,... | collective-permute-start | bytes 98312 | tf_op jit(solution)/shard_map/ppermute | solution.py:703
  11.8 0.2 %collective-permute-start.5 = (bf16[144,128]{1,0:T(8,128)(2,1)S(1)}, bf16[144,128]{1,0:T(8,128)(2,1)S(1)}, u32[]{:S(2)}, u32[]{:S(2)}) collective-permute-start(bf16[144,128]{1,0:T(8,128)(2,1)S(1)} %get-tuple-element.29), channel_id=1, source_target_pairs={{0,1},{1,0},{2,3},{3,2},{4,5},{5,4},{6,7},{7,6},{8,9},{9,8},{10,11... | collective-permute-start | bytes 110600 | tf_op jit(solution)/shard_map/ppermute | solution.py:702
  12.1 1.1 %first.1.refs_4_.refs_5_ = f32[5,96,64]{2,1,0:T(8,128)S(1)} custom-call(bf16[16,64,256]{2,1,0:T(8,128)(2,1)S(1)} %get-tuple-element.18.refs_0_, bf16[16,32,256]{2,1,0:T(8,128)(2,1)S(1)} %get-tuple-element.22.refs_1_, bf16[3504,256]{1,0:T(8,128)(2,1)S(1)} %stage.1.refs_2_.refs_5_.refs_7_), custom_call_target="tpu_custom_call" | custom-call | flops 349962240 | bytes 2703360 | tf_op jit(solution)/shard_map/first/pallas_call | solution.py:627
  13.2 0.0 collective-permute-done.2.zown.refs_2_
  13.2 0.0 collective-permute-done.3.zcorner.refs_3_
  13.3 1.1 %near.1 = (f32[3,96,64]{2,1,0:T(8,128)S(1)}, bf16[96,128]{1,0:T(8,128)(2,1)S(1)}) custom-call(bf16[16,64,256]{2,1,0:T(8,128)(2,1)S(1)} %get-tuple-element.18.refs_0_, bf16[16,32,256]{2,1,0:T(8,128)(2,1)S(1)} %get-tuple-element.22.refs_1_, bf16[480,128]{1,0:T(8,128)(2,1)S(1)} %collective-permute-done.2.zown.refs_2_, ...), custom_call_target="tpu_custom_call" | custom-call | flops 209977344 | bytes 2969600 | tf_op jit(solution)/shard_map/near/pallas_call | solution.py:627
  14.4 0.7 %collective-permute-start.6 = (bf16[96,128]{1,0:T(8,128)(2,1)S(1)}, bf16[96,128]{1,0:T(8,128)(2,1)S(1)}, u32[]{:S(2)}, u32[]{:S(2)}) collective-permute-start(bf16[96,128]{1,0:T(8,128)(2,1)S(1)} %get-tuple-element.30), channel_id=1, source_target_pairs={{0,16},{16,0},{1,17},{17,1},{2,18},{18,2},{3,19},{19,3},{4,20},{20... | collective-permute-start | bytes 73736 | tf_op jit(solution)/shard_map/ppermute | solution.py:717
  15.1 0.0 collective-permute-done.4.refs_0_
  15.1 0.1 beyond.1.refs_4_
  15.2 0.0 collective-permute-done.5.refs_8_
  15.2 2.4 %last.1.own = f32[6,4,16,64]{3,2,1,0:T(8,128)S(1)} custom-call(bf16[16,64,256]{2,1,0:T(8,128)(2,1)S(1)} %get-tuple-element.18.refs_0_, bf16[16,32,256]{2,1,0:T(8,128)(2,1)S(1)} %get-tuple-element.22.refs_1_, bf16[8,32,128]{2,1,0:T(8,128)(2,1)S(1)} %get-tuple-element.23.refs_2_, bf16[4,32,128]{2,1,0:T(8,128)(2,1)S(1)} %get-tuple-element.24.refs_3_, ...), custom_call_target="tpu_custom_call" | custom-call | flops 909901824 | bytes 3108864 | tf_op jit(solution)/shard_map/last/pallas_call | solution.py:627
  17.6 0.0 collective-permute-done.6.got
  17.6 0.8 %add.1 = f32[6,4,16,64]{3,2,1,0:T(8,128)} custom-call(f32[6,4,16,64]{3,2,1,0:T(8,128)S(1)} %last.1.own, bf16[96,128]{1,0:T(8,128)(2,1)S(1)} %collective-permute-done.6.got), custom_call_target="tpu_custom_call" | custom-call | bytes 221184 | tf_op jit(solution)/shard_map/add/pallas_call | solution.py:627
  (1 shorter events, 0.0 us)
Async XLA Ops:
  1.2 7.7 %collective-permute-start = (bf16[176,256]{1,0:T(8,128)(2,1)S(1)}, bf16[176,256]{1,0:T(8,128)(2,1)S(1)}, u32[]{:S(2)}, u32[]{:S(2)}) collective-permute-start(bf16[176,256]{1,0:T(8,128)(2,1)S(1)} %get-tuple-element.19), channel_id=1, source_target_pairs={{0,2},{2,0},{4,6},{6,4},{8,10},{10,8},{12,14},{14,12},{1,3},{3,1},... | collective-permute-start | bytes 270344 | tf_op jit(solution)/shard_map/ppermute | solution.py:674
  1.3 7.6 %collective-permute-start.1 = (bf16[176,256]{1,0:T(8,128)(2,1)S(1)}, bf16[176,256]{1,0:T(8,128)(2,1)S(1)}, u32[]{:S(2)}, u32[]{:S(2)}) collective-permute-start(bf16[176,256]{1,0:T(8,128)(2,1)S(1)} %get-tuple-element.20), channel_id=1, source_target_pairs={{2,4},{6,8},{10,12},{4,2},{8,6},{12,10},{3,5},{7,9},{11,13},{5,3},... | collective-permute-start | bytes 270344 | tf_op jit(solution)/shard_map/ppermute | solution.py:673
  6.2 7.0 %collective-permute-start.2 = (bf16[480,128]{1,0:T(8,128)(2,1)S(1)}, bf16[480,128]{1,0:T(8,128)(2,1)S(1)}, u32[]{:S(2)}, u32[]{:S(2)}) collective-permute-start(bf16[480,128]{1,0:T(8,128)(2,1)S(1)} %get-tuple-element.25), channel_id=1, source_target_pairs={{0,16},{16,0},{1,17},{17,1},{2,18},{18,2},{3,19},{19,3},{4,20},{20... | collective-permute-start | bytes 368648 | tf_op jit(solution)/shard_map/ppermute | solution.py:685
  9.4 3.9 %collective-permute-start.3 = (bf16[176,128]{1,0:T(8,128)(2,1)S(1)}, bf16[176,128]{1,0:T(8,128)(2,1)S(1)}, u32[]{:S(2)}, u32[]{:S(2)}) collective-permute-start(bf16[176,128]{1,0:T(8,128)(2,1)S(1)} %get-tuple-element.26), channel_id=1, source_target_pairs={{0,16},{16,0},{1,17},{17,1},{2,18},{18,2},{3,19},{19,3},{4,20},{20... | collective-permute-start | bytes 135176 | tf_op jit(solution)/shard_map/ppermute | solution.py:694
  10.3 4.8 %collective-permute-start.4 = (bf16[128,128]{1,0:T(8,128)(2,1)S(1)}, bf16[128,128]{1,0:T(8,128)(2,1)S(1)}, u32[]{:S(2)}, u32[]{:S(2)}) collective-permute-start(bf16[128,128]{1,0:T(8,128)(2,1)S(1)} %get-tuple-element.27), channel_id=1, source_target_pairs={{0,17},{1,16},{16,1},{17,0},{2,19},{3,18},{18,3},{19,2},{4,21},{5,... | collective-permute-start | bytes 98312 | tf_op jit(solution)/shard_map/ppermute | solution.py:703
  11.8 3.3 %collective-permute-start.5 = (bf16[144,128]{1,0:T(8,128)(2,1)S(1)}, bf16[144,128]{1,0:T(8,128)(2,1)S(1)}, u32[]{:S(2)}, u32[]{:S(2)}) collective-permute-start(bf16[144,128]{1,0:T(8,128)(2,1)S(1)} %get-tuple-element.29), channel_id=1, source_target_pairs={{0,1},{1,0},{2,3},{3,2},{4,5},{5,4},{6,7},{7,6},{8,9},{9,8},{10,11... | collective-permute-start | bytes 110600 | tf_op jit(solution)/shard_map/ppermute | solution.py:702
  14.4 3.2 %collective-permute-start.6 = (bf16[96,128]{1,0:T(8,128)(2,1)S(1)}, bf16[96,128]{1,0:T(8,128)(2,1)S(1)}, u32[]{:S(2)}, u32[]{:S(2)}) collective-permute-start(bf16[96,128]{1,0:T(8,128)(2,1)S(1)} %get-tuple-element.30), channel_id=1, source_target_pairs={{0,16},{16,0},{1,17},{17,1},{2,18},{18,2},{3,19},{19,3},{4,20},{20... | collective-permute-start | bytes 73736 | tf_op jit(solution)/shard_map/ppermute | solution.py:717

commit v10 on v9

--- a/solution.py
+++ b/solution.py
@@ -372,7 +372,7 @@
 
 FIRST = {True: 5, False: 3}
 LAST = {True: 8, False: 10}
-GROUP = 4
+GROUP = 2
 EDGE = R
 
 
@@ -414,17 +414,22 @@
     return total
 
 
-def near_kernel(place_of, zs, n_row, vol, yud, zown, zcorner, u1, w, u_ref, send_ref, zext, *scratch):
+def near_kernel(place_of, zs, n_row, vol, yud, zown, zcorner, u1, w, u_ref, send_ref, corner, *scratch):
     depth, rows, cols = vol.shape
     n_zq = zs.shape[1]
     get = getter(place_of, w)
     ysm = row_mask(get, n_row, rows, rows + 16, rows // 4)
-    corner = jnp.dot(
+    corner[...] = jnp.dot(
         get("corner_back"), joined_halves(zcorner, 0, 64), preferred_element_type=F32
     ).astype(BF16).reshape(R, 2 * HALO, cols)
-    zext[:, 0:HALO] = corner[:, 0:HALO]
-    zext[:, HALO : HALO + rows] = joined_halves(zown, 0, R * rows).reshape(R, rows, cols)
-    zext[:, HALO + rows :] = corner[:, HALO:]
+
+    def layer_beyond(k, at, lanes):
+        if HALO <= at < HALO + rows:
+            first = lanes.start // 128 * R * rows + k * rows + at - HALO
+            return zown[first : first + 16].astype(F32)
+        first = at if at < HALO else at - rows
+        return corner[k, first : first + 16, lanes].astype(F32)
+
     layer = block_loader(vol, yud, rows)
 
     def body(low):
@@ -439,7 +444,7 @@
                 elif (k < R) == low:
                     out.append(layer(outer + k % R, at, lanes))
                 else:
-                    out.append(zext[k % R, at : at + 16, lanes].astype(F32))
+                    out.append(layer_beyond(k % R, at, lanes))
             return out
 
         layers_to_sums(get, ysm, load, EDGE, (rows, cols), u_ref, *scratch)
@@ -711,7 +716,7 @@
         lambda *refs: near_kernel(place_of, zs, n_row, *refs),
         [sds((EDGE, n_rows, quarter), F32), bf16(n_rows, 2 * quarter)],
         [vol, yud, zown, zcorner, u1, w],
-        [pltpu.VMEM((R, ext, cols), BF16)] + scratch_for(EDGE),
+        [pltpu.VMEM((R, 2 * HALO, cols), BF16)] + scratch_for(EDGE),
         "near", flops=EDGE * layer_flops,
     )
     sums = lax.ppermute(send, "gz", swap)

time: 18.6 us -> 18.7 us (level)
  no operation moved by 1% of the time
where the time goes in v10:
time: 18.7 us; the launch traced here: 18.5 us
  starting transfers between devices  9.35 us (50%)
  Pallas kernels  7.55 us (40%)
  local copies, waits for them, and re-layouts  1.48 us (8%)
    pallas_call x9, Pallas kernels, call(): pl.pallas_call(body, out_shape=list(outs), in_specs=[hbm] * n_hbm + [vmem...  7.55 us
    ppermute x1, starting transfers between devices, per_device(): r2 = lax.ppermute(s2, 'row', inner)  4.55 us
    ppermute x1, starting transfers between devices, per_device(): zxs.append(lax.ppermute(messages[n_side + side], ('gz', 'col'), both))  1.56 us
    unnamed x1, local copies, waits for them, and re-layouts  1.48 us
    ppermute x1, starting transfers between devices, per_device(): zown = lax.ppermute(zmsg, 'gz', swap)  1.27 us
    ppermute x1, starting transfers between devices, per_device(): zcorner = lax.ppermute(zcmsg, 'gz', swap)  0.92 us
    ppermute x1, starting transfers between devices, per_device(): sums = lax.ppermute(send, 'gz', swap)  0.69 us
  transfers between devices with their start and end apart: 7, of which 0 were waited for; matrix products, arithmetic and copies ran while one was open for 8% of the time, Pallas kernels for 30%

profile of v10, /device:TPU:1, one launch (start us, length us, event | category | flops | bytes accessed | tf_op | source)
XLA Modules:
  0.0 18.5 jit_solution(7313002848777997323)
XLA Ops:
  0.0 1.2 %load.1 = (bf16[176,256]{1,0:T(8,128)(2,1)S(1)}, bf16[176,256]{1,0:T(8,128)(2,1)S(1)}, bf16[16,64,256]{2,1,0:T(8,128)(2,1)S(1)}) custom-call(bf16[16,64,256]{2,1,0:T(8,128)(2,1)} %vol.1), custom_call_target="tpu_custom_call" | custom-call | bytes 1228800 | tf_op jit(solution)/shard_map/load/pallas_call | solution.py:632
  1.2 0.1 collective-permute-start
  1.3 4.6 %collective-permute-start.1 = (bf16[176,256]{1,0:T(8,128)(2,1)S(1)}, bf16[176,256]{1,0:T(8,128)(2,1)S(1)}, u32[]{:S(2)}, u32[]{:S(2)}) collective-permute-start(bf16[176,256]{1,0:T(8,128)(2,1)S(1)} %get-tuple-element.20), channel_id=1, source_target_pairs={{2,4},{6,8},{10,12},{4,2},{8,6},{12,10},{3,5},{7,9},{11,13},{5,3},... | collective-permute-start | bytes 270344 | tf_op jit(solution)/shard_map/ppermute | solution.py:678
  5.9 0.3 %edges.1 = (bf16[8,32,128]{2,1,0:T(8,128)(2,1)S(1)}, bf16[480,128]{1,0:T(8,128)(2,1)S(1)}, bf16[96,128]{1,0:T(8,128)(2,1)S(1)}) custom-call(bf16[16,64,256]{2,1,0:T(8,128)(2,1)S(1)} %get-tuple-element.18.refs_0_), custom_call_target="tpu_custom_call" | custom-call | bytes 737280 | tf_op jit(solution)/shard_map/edges/pallas_call | solution.py:632
  6.2 1.3 %collective-permute-start.2 = (bf16[480,128]{1,0:T(8,128)(2,1)S(1)}, bf16[480,128]{1,0:T(8,128)(2,1)S(1)}, u32[]{:S(2)}, u32[]{:S(2)}) collective-permute-start(bf16[480,128]{1,0:T(8,128)(2,1)S(1)} %get-tuple-element.25), channel_id=1, source_target_pairs={{0,16},{16,0},{1,17},{17,1},{2,18},{18,2},{3,19},{19,3},{4,20},{20... | collective-permute-start | bytes 368648 | tf_op jit(solution)/shard_map/ppermute | solution.py:690
  7.5 1.5 %copy.6.w = bf16[3504,256]{1,0:T(8,128)(2,1)S(1)} copy(bf16[3504,256]{1,0:T(8,128)(2,1)} %constant.2.clone) | data formatting | bytes 3588096
  9.0 0.0 collective-permute-done.refs_0_
  9.0 0.0 collective-permute-done.1.refs_1_
  9.0 0.4 %pack.1 = (bf16[16,32,256]{2,1,0:T(8,128)(2,1)S(1)}, bf16[4,32,128]{2,1,0:T(8,128)(2,1)S(1)}, bf16[176,128]{1,0:T(8,128)(2,1)S(1)}, bf16[144,128]{1,0:T(8,128)(2,1)S(1)}, bf16[128,128]{1,0:T(8,128)(2,1)S(1)}) custom-call(bf16[176,256]{1,0:T(8,128)(2,1)S(1)} %collective-permute-done.refs_0_, bf16[176,256]{1,0:T(8,128)(2,1)S(1)} %collective-permute-done.1.refs_1_, ...), custom_call_target="tpu_custom_call" | custom-call | bytes 2408448 | tf_op jit(solution)/shard_map/pack/pallas_call | solution.py:632
  9.4 0.9 %collective-permute-start.3 = (bf16[176,128]{1,0:T(8,128)(2,1)S(1)}, bf16[176,128]{1,0:T(8,128)(2,1)S(1)}, u32[]{:S(2)}, u32[]{:S(2)}) collective-permute-start(bf16[176,128]{1,0:T(8,128)(2,1)S(1)} %get-tuple-element.26), channel_id=1, source_target_pairs={{0,16},{16,0},{1,17},{17,1},{2,18},{18,2},{3,19},{19,3},{4,20},{20... | collective-permute-start | bytes 135176 | tf_op jit(solution)/shard_map/ppermute | solution.py:699
  10.3 1.6 %collective-permute-start.4 = (bf16[128,128]{1,0:T(8,128)(2,1)S(1)}, bf16[128,128]{1,0:T(8,128)(2,1)S(1)}, u32[]{:S(2)}, u32[]{:S(2)}) collective-permute-start(bf16[128,128]{1,0:T(8,128)(2,1)S(1)} %get-tuple-element.27), channel_id=1, source_target_pairs={{0,17},{1,16},{16,1},{17,0},{2,19},{3,18},{18,3},{19,2},{4,21},{5,... | collective-permute-start | bytes 98312 | tf_op jit(solution)/shard_map/ppermute | solution.py:708
  11.8 0.2 %collective-permute-start.5 = (bf16[144,128]{1,0:T(8,128)(2,1)S(1)}, bf16[144,128]{1,0:T(8,128)(2,1)S(1)}, u32[]{:S(2)}, u32[]{:S(2)}) collective-permute-start(bf16[144,128]{1,0:T(8,128)(2,1)S(1)} %get-tuple-element.29), channel_id=1, source_target_pairs={{0,1},{1,0},{2,3},{3,2},{4,5},{5,4},{6,7},{7,6},{8,9},{9,8},{10,11... | collective-permute-start | bytes 110600 | tf_op jit(solution)/shard_map/ppermute | solution.py:707
  12.1 1.2 %first.1.refs_4_.refs_5_ = f32[5,96,64]{2,1,0:T(8,128)S(1)} custom-call(bf16[16,64,256]{2,1,0:T(8,128)(2,1)S(1)} %get-tuple-element.18.refs_0_, bf16[16,32,256]{2,1,0:T(8,128)(2,1)S(1)} %get-tuple-element.22.refs_1_, bf16[3504,256]{1,0:T(8,128)(2,1)S(1)} %stage.1.refs_2_.refs_5_.refs_7_), custom_call_target="tpu_custom_call" | custom-call | flops 349962240 | bytes 2703360 | tf_op jit(solution)/shard_map/first/pallas_call | solution.py:632
  13.3 0.0 collective-permute-done.2.zown.refs_2_
  13.3 0.0 collective-permute-done.3.zcorner.refs_3_
  13.3 1.2 %near.1 = (f32[3,96,64]{2,1,0:T(8,128)S(1)}, bf16[96,128]{1,0:T(8,128)(2,1)S(1)}) custom-call(bf16[16,64,256]{2,1,0:T(8,128)(2,1)S(1)} %get-tuple-element.18.refs_0_, bf16[16,32,256]{2,1,0:T(8,128)(2,1)S(1)} %get-tuple-element.22.refs_1_, bf16[480,128]{1,0:T(8,128)(2,1)S(1)} %collective-permute-done.2.zown.refs_2_, ...), custom_call_target="tpu_custom_call" | custom-call | flops 209977344 | bytes 2969600 | tf_op jit(solution)/shard_map/near/pallas_call | solution.py:632
  14.4 0.7 %collective-permute-start.6 = (bf16[96,128]{1,0:T(8,128)(2,1)S(1)}, bf16[96,128]{1,0:T(8,128)(2,1)S(1)}, u32[]{:S(2)}, u32[]{:S(2)}) collective-permute-start(bf16[96,128]{1,0:T(8,128)(2,1)S(1)} %get-tuple-element.30), channel_id=1, source_target_pairs={{0,16},{16,0},{1,17},{17,1},{2,18},{18,2},{3,19},{19,3},{4,20},{20... | collective-permute-start | bytes 73736 | tf_op jit(solution)/shard_map/ppermute | solution.py:722
  15.1 0.0 collective-permute-done.4.refs_0_
  15.1 0.1 beyond.1.refs_4_
  15.3 0.0 collective-permute-done.5.refs_8_
  15.3 2.4 %last.1.own = f32[6,4,16,64]{3,2,1,0:T(8,128)S(1)} custom-call(bf16[16,64,256]{2,1,0:T(8,128)(2,1)S(1)} %get-tuple-element.18.refs_0_, bf16[16,32,256]{2,1,0:T(8,128)(2,1)S(1)} %get-tuple-element.22.refs_1_, bf16[8,32,128]{2,1,0:T(8,128)(2,1)S(1)} %get-tuple-element.23.refs_2_, bf16[4,32,128]{2,1,0:T(8,128)(2,1)S(1)} %get-tuple-element.24.refs_3_, ...), custom_call_target="tpu_custom_call" | custom-call | flops 909901824 | bytes 3108864 | tf_op jit(solution)/shard_map/last/pallas_call | solution.py:632
  17.7 0.0 collective-permute-done.6.got
  17.7 0.8 %add.1 = f32[6,4,16,64]{3,2,1,0:T(8,128)} custom-call(f32[6,4,16,64]{3,2,1,0:T(8,128)S(1)} %last.1.own, bf16[96,128]{1,0:T(8,128)(2,1)S(1)} %collective-permute-done.6.got), custom_call_target="tpu_custom_call" | custom-call | bytes 221184 | tf_op jit(solution)/shard_map/add/pallas_call | solution.py:632
  (1 shorter events, 0.0 us)
Async XLA Ops:
  1.2 7.7 %collective-permute-start = (bf16[176,256]{1,0:T(8,128)(2,1)S(1)}, bf16[176,256]{1,0:T(8,128)(2,1)S(1)}, u32[]{:S(2)}, u32[]{:S(2)}) collective-permute-start(bf16[176,256]{1,0:T(8,128)(2,1)S(1)} %get-tuple-element.19), channel_id=1, source_target_pairs={{0,2},{2,0},{4,6},{6,4},{8,10},{10,8},{12,14},{14,12},{1,3},{3,1},... | collective-permute-start | bytes 270344 | tf_op jit(solution)/shard_map/ppermute | solution.py:679
  1.3 7.6 %collective-permute-start.1 = (bf16[176,256]{1,0:T(8,128)(2,1)S(1)}, bf16[176,256]{1,0:T(8,128)(2,1)S(1)}, u32[]{:S(2)}, u32[]{:S(2)}) collective-permute-start(bf16[176,256]{1,0:T(8,128)(2,1)S(1)} %get-tuple-element.20), channel_id=1, source_target_pairs={{2,4},{6,8},{10,12},{4,2},{8,6},{12,10},{3,5},{7,9},{11,13},{5,3},... | collective-permute-start | bytes 270344 | tf_op jit(solution)/shard_map/ppermute | solution.py:678
  6.2 7.1 %collective-permute-start.2 = (bf16[480,128]{1,0:T(8,128)(2,1)S(1)}, bf16[480,128]{1,0:T(8,128)(2,1)S(1)}, u32[]{:S(2)}, u32[]{:S(2)}) collective-permute-start(bf16[480,128]{1,0:T(8,128)(2,1)S(1)} %get-tuple-element.25), channel_id=1, source_target_pairs={{0,16},{16,0},{1,17},{17,1},{2,18},{18,2},{3,19},{19,3},{4,20},{20... | collective-permute-start | bytes 368648 | tf_op jit(solution)/shard_map/ppermute | solution.py:690
  9.4 3.9 %collective-permute-start.3 = (bf16[176,128]{1,0:T(8,128)(2,1)S(1)}, bf16[176,128]{1,0:T(8,128)(2,1)S(1)}, u32[]{:S(2)}, u32[]{:S(2)}) collective-permute-start(bf16[176,128]{1,0:T(8,128)(2,1)S(1)} %get-tuple-element.26), channel_id=1, source_target_pairs={{0,16},{16,0},{1,17},{17,1},{2,18},{18,2},{3,19},{19,3},{4,20},{20... | collective-permute-start | bytes 135176 | tf_op jit(solution)/shard_map/ppermute | solution.py:699
  10.3 4.8 %collective-permute-start.4 = (bf16[128,128]{1,0:T(8,128)(2,1)S(1)}, bf16[128,128]{1,0:T(8,128)(2,1)S(1)}, u32[]{:S(2)}, u32[]{:S(2)}) collective-permute-start(bf16[128,128]{1,0:T(8,128)(2,1)S(1)} %get-tuple-element.27), channel_id=1, source_target_pairs={{0,17},{1,16},{16,1},{17,0},{2,19},{3,18},{18,3},{19,2},{4,21},{5,... | collective-permute-start | bytes 98312 | tf_op jit(solution)/shard_map/ppermute | solution.py:708
  11.8 3.4 %collective-permute-start.5 = (bf16[144,128]{1,0:T(8,128)(2,1)S(1)}, bf16[144,128]{1,0:T(8,128)(2,1)S(1)}, u32[]{:S(2)}, u32[]{:S(2)}) collective-permute-start(bf16[144,128]{1,0:T(8,128)(2,1)S(1)} %get-tuple-element.29), channel_id=1, source_target_pairs={{0,1},{1,0},{2,3},{3,2},{4,5},{5,4},{6,7},{7,6},{8,9},{9,8},{10,11... | collective-permute-start | bytes 110600 | tf_op jit(solution)/shard_map/ppermute | solution.py:707
  14.4 3.3 %collective-permute-start.6 = (bf16[96,128]{1,0:T(8,128)(2,1)S(1)}, bf16[96,128]{1,0:T(8,128)(2,1)S(1)}, u32[]{:S(2)}, u32[]{:S(2)}) collective-permute-start(bf16[96,128]{1,0:T(8,128)(2,1)S(1)} %get-tuple-element.30), channel_id=1, source_target_pairs={{0,16},{16,0},{1,17},{17,1},{2,18},{18,2},{3,19},{19,3},{4,20},{20... | collective-permute-start | bytes 73736 | tf_op jit(solution)/shard_map/ppermute | solution.py:722

commit v11 on v9

--- a/solution.py
+++ b/solution.py
@@ -370,9 +370,9 @@
     pass
 
 
-FIRST = {True: 5, False: 3}
-LAST = {True: 8, False: 10}
-GROUP = 4
+FIRST = {True: 6, False: 3}
+LAST = {True: 7, False: 10}
+GROUP = 3
 EDGE = R
 
 

time: 18.6 us -> 18.5 us (level)
  no operation moved by 1% of the time
where the time goes in v11:
time: 18.5 us; the launch traced here: 18.3 us
  starting transfers between devices  9.19 us (50%)
  Pallas kernels  7.56 us (41%)
  local copies, waits for them, and re-layouts  1.48 us (8%)
    pallas_call x9, Pallas kernels, call(): pl.pallas_call(body, out_shape=list(outs), in_specs=[hbm] * n_hbm + [vmem...  7.56 us
    ppermute x1, starting transfers between devices, per_device(): r2 = lax.ppermute(s2, 'row', inner)  4.55 us
    ppermute x1, starting transfers between devices, per_device(): zxs.append(lax.ppermute(messages[n_side + side], ('gz', 'col'), both))  1.56 us
    unnamed x1, local copies, waits for them, and re-layouts  1.48 us
    ppermute x1, starting transfers between devices, per_device(): zown = lax.ppermute(zmsg, 'gz', swap)  1.27 us
    ppermute x1, starting transfers between devices, per_device(): zcorner = lax.ppermute(zcmsg, 'gz', swap)  0.92 us
    ppermute x1, starting transfers between devices, per_device(): sums = lax.ppermute(send, 'gz', swap)  0.52 us
  transfers between devices with their start and end apart: 7, of which 0 were waited for; matrix products, arithmetic and copies ran while one was open for 8% of the time, Pallas kernels for 30%

profile of v11, /device:TPU:1, one launch (start us, length us, event | category | flops | bytes accessed | tf_op | source)
XLA Modules:
  0.0 18.3 jit_solution(1731809020169715021)
XLA Ops:
  0.0 1.2 %load.1 = (bf16[176,256]{1,0:T(8,128)(2,1)S(1)}, bf16[176,256]{1,0:T(8,128)(2,1)S(1)}, bf16[16,64,256]{2,1,0:T(8,128)(2,1)S(1)}) custom-call(bf16[16,64,256]{2,1,0:T(8,128)(2,1)} %vol.1), custom_call_target="tpu_custom_call" | custom-call | bytes 1228800 | tf_op jit(solution)/shard_map/load/pallas_call | solution.py:627
  1.2 0.1 collective-permute-start
  1.3 4.6 %collective-permute-start.1 = (bf16[176,256]{1,0:T(8,128)(2,1)S(1)}, bf16[176,256]{1,0:T(8,128)(2,1)S(1)}, u32[]{:S(2)}, u32[]{:S(2)}) collective-permute-start(bf16[176,256]{1,0:T(8,128)(2,1)S(1)} %get-tuple-element.20), channel_id=1, source_target_pairs={{2,4},{6,8},{10,12},{4,2},{8,6},{12,10},{3,5},{7,9},{11,13},{5,3},... | collective-permute-start | bytes 270344 | tf_op jit(solution)/shard_map/ppermute | solution.py:673
  5.9 0.3 %edges.1 = (bf16[8,32,128]{2,1,0:T(8,128)(2,1)S(1)}, bf16[480,128]{1,0:T(8,128)(2,1)S(1)}, bf16[96,128]{1,0:T(8,128)(2,1)S(1)}) custom-call(bf16[16,64,256]{2,1,0:T(8,128)(2,1)S(1)} %get-tuple-element.18.refs_0_), custom_call_target="tpu_custom_call" | custom-call | bytes 737280 | tf_op jit(solution)/shard_map/edges/pallas_call | solution.py:627
  6.2 1.3 %collective-permute-start.2 = (bf16[480,128]{1,0:T(8,128)(2,1)S(1)}, bf16[480,128]{1,0:T(8,128)(2,1)S(1)}, u32[]{:S(2)}, u32[]{:S(2)}) collective-permute-start(bf16[480,128]{1,0:T(8,128)(2,1)S(1)} %get-tuple-element.25), channel_id=1, source_target_pairs={{0,16},{16,0},{1,17},{17,1},{2,18},{18,2},{3,19},{19,3},{4,20},{20... | collective-permute-start | bytes 368648 | tf_op jit(solution)/shard_map/ppermute | solution.py:685
  7.5 1.5 %copy.6.w = bf16[3504,256]{1,0:T(8,128)(2,1)S(1)} copy(bf16[3504,256]{1,0:T(8,128)(2,1)} %constant.2.clone) | data formatting | bytes 3588096
  9.0 0.0 collective-permute-done.refs_0_
  9.0 0.0 collective-permute-done.1.refs_1_
  9.0 0.4 %pack.1 = (bf16[16,32,256]{2,1,0:T(8,128)(2,1)S(1)}, bf16[4,32,128]{2,1,0:T(8,128)(2,1)S(1)}, bf16[176,128]{1,0:T(8,128)(2,1)S(1)}, bf16[144,128]{1,0:T(8,128)(2,1)S(1)}, bf16[128,128]{1,0:T(8,128)(2,1)S(1)}) custom-call(bf16[176,256]{1,0:T(8,128)(2,1)S(1)} %collective-permute-done.refs_0_, bf16[176,256]{1,0:T(8,128)(2,1)S(1)} %collective-permute-done.1.refs_1_, ...), custom_call_target="tpu_custom_call" | custom-call | bytes 2408448 | tf_op jit(solution)/shard_map/pack/pallas_call | solution.py:627
  9.4 0.9 %collective-permute-start.3 = (bf16[176,128]{1,0:T(8,128)(2,1)S(1)}, bf16[176,128]{1,0:T(8,128)(2,1)S(1)}, u32[]{:S(2)}, u32[]{:S(2)}) collective-permute-start(bf16[176,128]{1,0:T(8,128)(2,1)S(1)} %get-tuple-element.26), channel_id=1, source_target_pairs={{0,16},{16,0},{1,17},{17,1},{2,18},{18,2},{3,19},{19,3},{4,20},{20... | collective-permute-start | bytes 135176 | tf_op jit(solution)/shard_map/ppermute | solution.py:694
  10.3 1.6 %collective-permute-start.4 = (bf16[128,128]{1,0:T(8,128)(2,1)S(1)}, bf16[128,128]{1,0:T(8,128)(2,1)S(1)}, u32[]{:S(2)}, u32[]{:S(2)}) collective-permute-start(bf16[128,128]{1,0:T(8,128)(2,1)S(1)} %get-tuple-element.27), channel_id=1, source_target_pairs={{0,17},{1,16},{16,1},{17,0},{2,19},{3,18},{18,3},{19,2},{4,21},{5,... | collective-permute-start | bytes 98312 | tf_op jit(solution)/shard_map/ppermute | solution.py:703
  11.8 0.2 %collective-permute-start.5 = (bf16[144,128]{1,0:T(8,128)(2,1)S(1)}, bf16[144,128]{1,0:T(8,128)(2,1)S(1)}, u32[]{:S(2)}, u32[]{:S(2)}) collective-permute-start(bf16[144,128]{1,0:T(8,128)(2,1)S(1)} %get-tuple-element.29), channel_id=1, source_target_pairs={{0,1},{1,0},{2,3},{3,2},{4,5},{5,4},{6,7},{7,6},{8,9},{9,8},{10,11... | collective-permute-start | bytes 110600 | tf_op jit(solution)/shard_map/ppermute | solution.py:702
  12.1 1.3 %first.1.refs_4_.refs_5_ = f32[6,96,64]{2,1,0:T(8,128)S(1)} custom-call(bf16[16,64,256]{2,1,0:T(8,128)(2,1)S(1)} %get-tuple-element.18.refs_0_, bf16[16,32,256]{2,1,0:T(8,128)(2,1)S(1)} %get-tuple-element.22.refs_1_, bf16[3504,256]{1,0:T(8,128)(2,1)S(1)} %stage.1.refs_2_.refs_5_.refs_7_), custom_call_target="tpu_custom_call" | custom-call | flops 419954688 | bytes 2727936 | tf_op jit(solution)/shard_map/first/pallas_call | solution.py:627
  13.4 0.0 collective-permute-done.2.zown.refs_2_
  13.4 0.0 collective-permute-done.3.zcorner.refs_3_
  13.4 1.1 %near.1 = (f32[3,96,64]{2,1,0:T(8,128)S(1)}, bf16[96,128]{1,0:T(8,128)(2,1)S(1)}) custom-call(bf16[16,64,256]{2,1,0:T(8,128)(2,1)S(1)} %get-tuple-element.18.refs_0_, bf16[16,32,256]{2,1,0:T(8,128)(2,1)S(1)} %get-tuple-element.22.refs_1_, bf16[480,128]{1,0:T(8,128)(2,1)S(1)} %collective-permute-done.2.zown.refs_2_, ...), custom_call_target="tpu_custom_call" | custom-call | flops 209977344 | bytes 2994176 | tf_op jit(solution)/shard_map/near/pallas_call | solution.py:627
  14.5 0.5 %collective-permute-start.6 = (bf16[96,128]{1,0:T(8,128)(2,1)S(1)}, bf16[96,128]{1,0:T(8,128)(2,1)S(1)}, u32[]{:S(2)}, u32[]{:S(2)}) collective-permute-start(bf16[96,128]{1,0:T(8,128)(2,1)S(1)} %get-tuple-element.30), channel_id=1, source_target_pairs={{0,16},{16,0},{1,17},{17,1},{2,18},{18,2},{3,19},{19,3},{4,20},{20... | collective-permute-start | bytes 73736 | tf_op jit(solution)/shard_map/ppermute | solution.py:717
  15.1 0.0 collective-permute-done.4.refs_0_
  15.1 0.1 beyond.1.refs_4_
  15.2 0.0 collective-permute-done.5.refs_8_
  15.2 2.4 %last.1.own = f32[6,4,16,64]{3,2,1,0:T(8,128)S(1)} custom-call(bf16[16,64,256]{2,1,0:T(8,128)(2,1)S(1)} %get-tuple-element.18.refs_0_, bf16[16,32,256]{2,1,0:T(8,128)(2,1)S(1)} %get-tuple-element.22.refs_1_, bf16[8,32,128]{2,1,0:T(8,128)(2,1)S(1)} %get-tuple-element.23.refs_2_, bf16[4,32,128]{2,1,0:T(8,128)(2,1)S(1)} %get-tuple-element.24.refs_3_, ...), custom_call_target="tpu_custom_call" | custom-call | flops 909901824 | bytes 3133440 | tf_op jit(solution)/shard_map/last/pallas_call | solution.py:627
  17.6 0.0 collective-permute-done.6.got
  17.6 0.8 %add.1 = f32[6,4,16,64]{3,2,1,0:T(8,128)} custom-call(f32[6,4,16,64]{3,2,1,0:T(8,128)S(1)} %last.1.own, bf16[96,128]{1,0:T(8,128)(2,1)S(1)} %collective-permute-done.6.got), custom_call_target="tpu_custom_call" | custom-call | bytes 221184 | tf_op jit(solution)/shard_map/add/pallas_call | solution.py:627
  (1 shorter events, 0.0 us)
Async XLA Ops:
  1.2 7.7 %collective-permute-start = (bf16[176,256]{1,0:T(8,128)(2,1)S(1)}, bf16[176,256]{1,0:T(8,128)(2,1)S(1)}, u32[]{:S(2)}, u32[]{:S(2)}) collective-permute-start(bf16[176,256]{1,0:T(8,128)(2,1)S(1)} %get-tuple-element.19), channel_id=1, source_target_pairs={{0,2},{2,0},{4,6},{6,4},{8,10},{10,8},{12,14},{14,12},{1,3},{3,1},... | collective-permute-start | bytes 270344 | tf_op jit(solution)/shard_map/ppermute | solution.py:674
  1.3 7.6 %collective-permute-start.1 = (bf16[176,256]{1,0:T(8,128)(2,1)S(1)}, bf16[176,256]{1,0:T(8,128)(2,1)S(1)}, u32[]{:S(2)}, u32[]{:S(2)}) collective-permute-start(bf16[176,256]{1,0:T(8,128)(2,1)S(1)} %get-tuple-element.20), channel_id=1, source_target_pairs={{2,4},{6,8},{10,12},{4,2},{8,6},{12,10},{3,5},{7,9},{11,13},{5,3},... | collective-permute-start | bytes 270344 | tf_op jit(solution)/shard_map/ppermute | solution.py:673
  6.2 7.2 %collective-permute-start.2 = (bf16[480,128]{1,0:T(8,128)(2,1)S(1)}, bf16[480,128]{1,0:T(8,128)(2,1)S(1)}, u32[]{:S(2)}, u32[]{:S(2)}) collective-permute-start(bf16[480,128]{1,0:T(8,128)(2,1)S(1)} %get-tuple-element.25), channel_id=1, source_target_pairs={{0,16},{16,0},{1,17},{17,1},{2,18},{18,2},{3,19},{19,3},{4,20},{20... | collective-permute-start | bytes 368648 | tf_op jit(solution)/shard_map/ppermute | solution.py:685
  9.4 4.0 %collective-permute-start.3 = (bf16[176,128]{1,0:T(8,128)(2,1)S(1)}, bf16[176,128]{1,0:T(8,128)(2,1)S(1)}, u32[]{:S(2)}, u32[]{:S(2)}) collective-permute-start(bf16[176,128]{1,0:T(8,128)(2,1)S(1)} %get-tuple-element.26), channel_id=1, source_target_pairs={{0,16},{16,0},{1,17},{17,1},{2,18},{18,2},{3,19},{19,3},{4,20},{20... | collective-permute-start | bytes 135176 | tf_op jit(solution)/shard_map/ppermute | solution.py:694
  10.3 4.8 %collective-permute-start.4 = (bf16[128,128]{1,0:T(8,128)(2,1)S(1)}, bf16[128,128]{1,0:T(8,128)(2,1)S(1)}, u32[]{:S(2)}, u32[]{:S(2)}) collective-permute-start(bf16[128,128]{1,0:T(8,128)(2,1)S(1)} %get-tuple-element.27), channel_id=1, source_target_pairs={{0,17},{1,16},{16,1},{17,0},{2,19},{3,18},{18,3},{19,2},{4,21},{5,... | collective-permute-start | bytes 98312 | tf_op jit(solution)/shard_map/ppermute | solution.py:703
  11.8 3.3 %collective-permute-start.5 = (bf16[144,128]{1,0:T(8,128)(2,1)S(1)}, bf16[144,128]{1,0:T(8,128)(2,1)S(1)}, u32[]{:S(2)}, u32[]{:S(2)}) collective-permute-start(bf16[144,128]{1,0:T(8,128)(2,1)S(1)} %get-tuple-element.29), channel_id=1, source_target_pairs={{0,1},{1,0},{2,3},{3,2},{4,5},{5,4},{6,7},{7,6},{8,9},{9,8},{10,11... | collective-permute-start | bytes 110600 | tf_op jit(solution)/shard_map/ppermute | solution.py:702
  14.5 3.0 %collective-permute-start.6 = (bf16[96,128]{1,0:T(8,128)(2,1)S(1)}, bf16[96,128]{1,0:T(8,128)(2,1)S(1)}, u32[]{:S(2)}, u32[]{:S(2)}) collective-permute-start(bf16[96,128]{1,0:T(8,128)(2,1)S(1)} %get-tuple-element.30), channel_id=1, source_target_pairs={{0,16},{16,0},{1,17},{17,1},{2,18},{18,2},{3,19},{19,3},{4,20},{20... | collective-permute-start | bytes 73736 | tf_op jit(solution)/shard_map/ppermute | solution.py:717

commit v12 on v9

--- a/solution.py
+++ b/solution.py
@@ -542,7 +542,6 @@
                 out.append(layer(z, at, lanes) if inside else jnp.zeros((16, 128), F32))
             return out
 
-        layers_to_sums(get, ysm, load, LAST[low], (rows, cols), u3, *scratch)
         own_layers = layers_of(
             [join(own[b].astype(F32), xs, 0, 4 * depth, b) for b in range(depth // 2)],
             [
@@ -592,6 +591,7 @@
                 term = jnp.dot(u[n_rows * c : n_rows * (c + 1)], g, preferred_element_type=F32)
                 total = term if total is None else total + term
             sums += [total[:, 0:quarter], total[:, 128 : 128 + quarter]]
+        layers_to_sums(get, ysm, load, LAST[low], (rows, cols), u3, *scratch)
         held = held_layers(depth, low)
         for q in range(depth // 4):
             total = weighted(sums[q], (u1, u2, u3), held, zs[:, q + 2])

time: 18.6 us -> 18.7 us (level)
  no operation moved by 1% of the time
where the time goes in v12:
time: 18.7 us; the launch traced here: 18.5 us
  starting transfers between devices  9.34 us (50%)
  Pallas kernels  7.61 us (41%)
  local copies, waits for them, and re-layouts  1.48 us (8%)
    pallas_call x9, Pallas kernels, call(): pl.pallas_call(body, out_shape=list(outs), in_specs=[hbm] * n_hbm + [vmem...  7.61 us
    ppermute x1, starting transfers between devices, per_device(): r2 = lax.ppermute(s2, 'row', inner)  4.55 us
    ppermute x1, starting transfers between devices, per_device(): zxs.append(lax.ppermute(messages[n_side + side], ('gz', 'col'), both))  1.56 us
    unnamed x1, local copies, waits for them, and re-layouts  1.48 us
    ppermute x1, starting transfers between devices, per_device(): zown = lax.ppermute(zmsg, 'gz', swap)  1.27 us
    ppermute x1, starting transfers between devices, per_device(): zcorner = lax.ppermute(zcmsg, 'gz', swap)  0.92 us
    ppermute x1, starting transfers between devices, per_device(): sums = lax.ppermute(send, 'gz', swap)  0.67 us
  transfers between devices with their start and end apart: 7, of which 0 were waited for; matrix products, arithmetic and copies ran while one was open for 8% of the time, Pallas kernels for 30%

profile of v12, /device:TPU:1, one launch (start us, length us, event | category | flops | bytes accessed | tf_op | source)
XLA Modules:
  0.0 18.5 jit_solution(15838766820643964686)
XLA Ops:
  0.0 1.2 %load.1 = (bf16[176,256]{1,0:T(8,128)(2,1)S(1)}, bf16[176,256]{1,0:T(8,128)(2,1)S(1)}, bf16[16,64,256]{2,1,0:T(8,128)(2,1)S(1)}) custom-call(bf16[16,64,256]{2,1,0:T(8,128)(2,1)} %vol.1), custom_call_target="tpu_custom_call" | custom-call | bytes 1228800 | tf_op jit(solution)/shard_map/load/pallas_call | solution.py:627
  1.2 0.1 collective-permute-start
  1.3 4.6 %collective-permute-start.1 = (bf16[176,256]{1,0:T(8,128)(2,1)S(1)}, bf16[176,256]{1,0:T(8,128)(2,1)S(1)}, u32[]{:S(2)}, u32[]{:S(2)}) collective-permute-start(bf16[176,256]{1,0:T(8,128)(2,1)S(1)} %get-tuple-element.20), channel_id=1, source_target_pairs={{2,4},{6,8},{10,12},{4,2},{8,6},{12,10},{3,5},{7,9},{11,13},{5,3},... | collective-permute-start | bytes 270344 | tf_op jit(solution)/shard_map/ppermute | solution.py:673
  5.9 0.3 %edges.1 = (bf16[8,32,128]{2,1,0:T(8,128)(2,1)S(1)}, bf16[480,128]{1,0:T(8,128)(2,1)S(1)}, bf16[96,128]{1,0:T(8,128)(2,1)S(1)}) custom-call(bf16[16,64,256]{2,1,0:T(8,128)(2,1)S(1)} %get-tuple-element.18.refs_0_), custom_call_target="tpu_custom_call" | custom-call | bytes 737280 | tf_op jit(solution)/shard_map/edges/pallas_call | solution.py:627
  6.2 1.3 %collective-permute-start.2 = (bf16[480,128]{1,0:T(8,128)(2,1)S(1)}, bf16[480,128]{1,0:T(8,128)(2,1)S(1)}, u32[]{:S(2)}, u32[]{:S(2)}) collective-permute-start(bf16[480,128]{1,0:T(8,128)(2,1)S(1)} %get-tuple-element.25), channel_id=1, source_target_pairs={{0,16},{16,0},{1,17},{17,1},{2,18},{18,2},{3,19},{19,3},{4,20},{20... | collective-permute-start | bytes 368648 | tf_op jit(solution)/shard_map/ppermute | solution.py:685
  7.5 1.5 %copy.6.w = bf16[3504,256]{1,0:T(8,128)(2,1)S(1)} copy(bf16[3504,256]{1,0:T(8,128)(2,1)} %constant.2.clone) | data formatting | bytes 3588096
  9.0 0.0 collective-permute-done.refs_0_
  9.0 0.0 collective-permute-done.1.refs_1_
  9.0 0.4 %pack.1 = (bf16[16,32,256]{2,1,0:T(8,128)(2,1)S(1)}, bf16[4,32,128]{2,1,0:T(8,128)(2,1)S(1)}, bf16[176,128]{1,0:T(8,128)(2,1)S(1)}, bf16[144,128]{1,0:T(8,128)(2,1)S(1)}, bf16[128,128]{1,0:T(8,128)(2,1)S(1)}) custom-call(bf16[176,256]{1,0:T(8,128)(2,1)S(1)} %collective-permute-done.refs_0_, bf16[176,256]{1,0:T(8,128)(2,1)S(1)} %collective-permute-done.1.refs_1_, ...), custom_call_target="tpu_custom_call" | custom-call | bytes 2408448 | tf_op jit(solution)/shard_map/pack/pallas_call | solution.py:627
  9.4 0.9 %collective-permute-start.3 = (bf16[176,128]{1,0:T(8,128)(2,1)S(1)}, bf16[176,128]{1,0:T(8,128)(2,1)S(1)}, u32[]{:S(2)}, u32[]{:S(2)}) collective-permute-start(bf16[176,128]{1,0:T(8,128)(2,1)S(1)} %get-tuple-element.26), channel_id=1, source_target_pairs={{0,16},{16,0},{1,17},{17,1},{2,18},{18,2},{3,19},{19,3},{4,20},{20... | collective-permute-start | bytes 135176 | tf_op jit(solution)/shard_map/ppermute | solution.py:694
  10.3 1.6 %collective-permute-start.4 = (bf16[128,128]{1,0:T(8,128)(2,1)S(1)}, bf16[128,128]{1,0:T(8,128)(2,1)S(1)}, u32[]{:S(2)}, u32[]{:S(2)}) collective-permute-start(bf16[128,128]{1,0:T(8,128)(2,1)S(1)} %get-tuple-element.27), channel_id=1, source_target_pairs={{0,17},{1,16},{16,1},{17,0},{2,19},{3,18},{18,3},{19,2},{4,21},{5,... | collective-permute-start | bytes 98312 | tf_op jit(solution)/shard_map/ppermute | solution.py:703
  11.8 0.2 %collective-permute-start.5 = (bf16[144,128]{1,0:T(8,128)(2,1)S(1)}, bf16[144,128]{1,0:T(8,128)(2,1)S(1)}, u32[]{:S(2)}, u32[]{:S(2)}) collective-permute-start(bf16[144,128]{1,0:T(8,128)(2,1)S(1)} %get-tuple-element.29), channel_id=1, source_target_pairs={{0,1},{1,0},{2,3},{3,2},{4,5},{5,4},{6,7},{7,6},{8,9},{9,8},{10,11... | collective-permute-start | bytes 110600 | tf_op jit(solution)/shard_map/ppermute | solution.py:702
  12.1 1.1 %first.1.refs_4_.refs_5_ = f32[5,96,64]{2,1,0:T(8,128)S(1)} custom-call(bf16[16,64,256]{2,1,0:T(8,128)(2,1)S(1)} %get-tuple-element.18.refs_0_, bf16[16,32,256]{2,1,0:T(8,128)(2,1)S(1)} %get-tuple-element.22.refs_1_, bf16[3504,256]{1,0:T(8,128)(2,1)S(1)} %stage.1.refs_2_.refs_5_.refs_7_), custom_call_target="tpu_custom_call" | custom-call | flops 349962240 | bytes 2703360 | tf_op jit(solution)/shard_map/first/pallas_call | solution.py:627
  13.2 0.0 collective-permute-done.2.zown.refs_2_
  13.2 0.0 collective-permute-done.3.zcorner.refs_3_
  13.3 1.1 %near.1 = (f32[3,96,64]{2,1,0:T(8,128)S(1)}, bf16[96,128]{1,0:T(8,128)(2,1)S(1)}) custom-call(bf16[16,64,256]{2,1,0:T(8,128)(2,1)S(1)} %get-tuple-element.18.refs_0_, bf16[16,32,256]{2,1,0:T(8,128)(2,1)S(1)} %get-tuple-element.22.refs_1_, bf16[480,128]{1,0:T(8,128)(2,1)S(1)} %collective-permute-done.2.zown.refs_2_, ...), custom_call_target="tpu_custom_call" | custom-call | flops 209977344 | bytes 2969600 | tf_op jit(solution)/shard_map/near/pallas_call | solution.py:627
  14.4 0.7 %collective-permute-start.6 = (bf16[96,128]{1,0:T(8,128)(2,1)S(1)}, bf16[96,128]{1,0:T(8,128)(2,1)S(1)}, u32[]{:S(2)}, u32[]{:S(2)}) collective-permute-start(bf16[96,128]{1,0:T(8,128)(2,1)S(1)} %get-tuple-element.30), channel_id=1, source_target_pairs={{0,16},{16,0},{1,17},{17,1},{2,18},{18,2},{3,19},{19,3},{4,20},{20... | collective-permute-start | bytes 73736 | tf_op jit(solution)/shard_map/ppermute | solution.py:717
  15.1 0.0 collective-permute-done.4.refs_0_
  15.1 0.1 beyond.1.refs_4_
  15.2 0.0 collective-permute-done.5.refs_8_
  15.2 2.6 %last.1.own = f32[6,4,16,64]{3,2,1,0:T(8,128)S(1)} custom-call(bf16[16,64,256]{2,1,0:T(8,128)(2,1)S(1)} %get-tuple-element.18.refs_0_, bf16[16,32,256]{2,1,0:T(8,128)(2,1)S(1)} %get-tuple-element.22.refs_1_, bf16[8,32,128]{2,1,0:T(8,128)(2,1)S(1)} %get-tuple-element.23.refs_2_, bf16[4,32,128]{2,1,0:T(8,128)(2,1)S(1)} %get-tuple-element.24.refs_3_, ...), custom_call_target="tpu_custom_call" | custom-call | flops 909901824 | bytes 3108864 | tf_op jit(solution)/shard_map/last/pallas_call | solution.py:627
  17.8 0.0 collective-permute-done.6.got
  17.8 0.8 %add.1 = f32[6,4,16,64]{3,2,1,0:T(8,128)} custom-call(f32[6,4,16,64]{3,2,1,0:T(8,128)S(1)} %last.1.own, bf16[96,128]{1,0:T(8,128)(2,1)S(1)} %collective-permute-done.6.got), custom_call_target="tpu_custom_call" | custom-call | bytes 221184 | tf_op jit(solution)/shard_map/add/pallas_call | solution.py:627
  (1 shorter events, 0.0 us)
Async XLA Ops:
  1.2 7.7 %collective-permute-start = (bf16[176,256]{1,0:T(8,128)(2,1)S(1)}, bf16[176,256]{1,0:T(8,128)(2,1)S(1)}, u32[]{:S(2)}, u32[]{:S(2)}) collective-permute-start(bf16[176,256]{1,0:T(8,128)(2,1)S(1)} %get-tuple-element.19), channel_id=1, source_target_pairs={{0,2},{2,0},{4,6},{6,4},{8,10},{10,8},{12,14},{14,12},{1,3},{3,1},... | collective-permute-start | bytes 270344 | tf_op jit(solution)/shard_map/ppermute | solution.py:674
  1.3 7.6 %collective-permute-start.1 = (bf16[176,256]{1,0:T(8,128)(2,1)S(1)}, bf16[176,256]{1,0:T(8,128)(2,1)S(1)}, u32[]{:S(2)}, u32[]{:S(2)}) collective-permute-start(bf16[176,256]{1,0:T(8,128)(2,1)S(1)} %get-tuple-element.20), channel_id=1, source_target_pairs={{2,4},{6,8},{10,12},{4,2},{8,6},{12,10},{3,5},{7,9},{11,13},{5,3},... | collective-permute-start | bytes 270344 | tf_op jit(solution)/shard_map/ppermute | solution.py:673
  6.2 7.0 %collective-permute-start.2 = (bf16[480,128]{1,0:T(8,128)(2,1)S(1)}, bf16[480,128]{1,0:T(8,128)(2,1)S(1)}, u32[]{:S(2)}, u32[]{:S(2)}) collective-permute-start(bf16[480,128]{1,0:T(8,128)(2,1)S(1)} %get-tuple-element.25), channel_id=1, source_target_pairs={{0,16},{16,0},{1,17},{17,1},{2,18},{18,2},{3,19},{19,3},{4,20},{20... | collective-permute-start | bytes 368648 | tf_op jit(solution)/shard_map/ppermute | solution.py:685
  9.4 3.9 %collective-permute-start.3 = (bf16[176,128]{1,0:T(8,128)(2,1)S(1)}, bf16[176,128]{1,0:T(8,128)(2,1)S(1)}, u32[]{:S(2)}, u32[]{:S(2)}) collective-permute-start(bf16[176,128]{1,0:T(8,128)(2,1)S(1)} %get-tuple-element.26), channel_id=1, source_target_pairs={{0,16},{16,0},{1,17},{17,1},{2,18},{18,2},{3,19},{19,3},{4,20},{20... | collective-permute-start | bytes 135176 | tf_op jit(solution)/shard_map/ppermute | solution.py:694
  10.3 4.8 %collective-permute-start.4 = (bf16[128,128]{1,0:T(8,128)(2,1)S(1)}, bf16[128,128]{1,0:T(8,128)(2,1)S(1)}, u32[]{:S(2)}, u32[]{:S(2)}) collective-permute-start(bf16[128,128]{1,0:T(8,128)(2,1)S(1)} %get-tuple-element.27), channel_id=1, source_target_pairs={{0,17},{1,16},{16,1},{17,0},{2,19},{3,18},{18,3},{19,2},{4,21},{5,... | collective-permute-start | bytes 98312 | tf_op jit(solution)/shard_map/ppermute | solution.py:703
  11.8 3.3 %collective-permute-start.5 = (bf16[144,128]{1,0:T(8,128)(2,1)S(1)}, bf16[144,128]{1,0:T(8,128)(2,1)S(1)}, u32[]{:S(2)}, u32[]{:S(2)}) collective-permute-start(bf16[144,128]{1,0:T(8,128)(2,1)S(1)} %get-tuple-element.29), channel_id=1, source_target_pairs={{0,1},{1,0},{2,3},{3,2},{4,5},{5,4},{6,7},{7,6},{8,9},{9,8},{10,11... | collective-permute-start | bytes 110600 | tf_op jit(solution)/shard_map/ppermute | solution.py:702
  14.4 3.4 %collective-permute-start.6 = (bf16[96,128]{1,0:T(8,128)(2,1)S(1)}, bf16[96,128]{1,0:T(8,128)(2,1)S(1)}, u32[]{:S(2)}, u32[]{:S(2)}) collective-permute-start(bf16[96,128]{1,0:T(8,128)(2,1)S(1)} %get-tuple-element.30), channel_id=1, source_target_pairs={{0,16},{16,0},{1,17},{17,1},{2,18},{18,2},{3,19},{19,3},{4,20},{20... | collective-permute-start | bytes 73736 | tf_op jit(solution)/shard_map/ppermute | solution.py:717

commit v13 on v12

--- a/solution.py
+++ b/solution.py
@@ -146,7 +146,7 @@
     return jnp.where(outside, 0.0, get("ysm").astype(F32)).astype(BF16)
 
 
-def layers_to_sums(get, ysm, load, count, shape, u_ref, zf, planes, prod, sm):
+def layers_to_sums(get, ysm, load, count, shape, u_ref, zf, planes, prod, sm, between=()):
     rows, cols = shape
     ext = rows + 2 * HALO
     gr = rows + 16
@@ -192,6 +192,7 @@
                 out = jnp.dot(ysm, part, preferred_element_type=F32)
                 sm[z, half * half_rows : (half + 1) * half_rows] = out.astype(BF16)
 
+    between = iter(between)
     n_group = -(-count // GROUP)
     ends = [count * i // n_group for i in range(n_group + 1)]
     stages = (z_filters, y_filters, x_filters, y_smoothing)
@@ -200,6 +201,7 @@
             i = step - k
             if 0 <= i < n_group:
                 stage(ends[i], ends[i + 1] - ends[i])
+        next(between, None)
     out = jnp.dot(
         sm[0:count].reshape(count * n_rows, cols), get("xsm"), preferred_element_type=F32
     )
@@ -542,56 +544,69 @@
                 out.append(layer(z, at, lanes) if inside else jnp.zeros((16, 128), F32))
             return out
 
-        own_layers = layers_of(
-            [join(own[b].astype(F32), xs, 0, 4 * depth, b) for b in range(depth // 2)],
-            [
-                join(halo[b].astype(F32), xs, 6 * depth, 8 * depth, b)
-                for b in range(depth // 4)
-            ],
+        sums = []
+
+        def strips_by_stage():
+            own_layers = layers_of(
+                [join(own[b].astype(F32), xs, 0, 4 * depth, b) for b in range(depth // 2)],
+                [
+                    join(halo[b].astype(F32), xs, 6 * depth, 8 * depth, b)
+                    for b in range(depth // 4)
+                ],
+            )
+            beyond = [far[k].astype(F32) for k in range(EXTRA)]
+            zero = [jnp.zeros((SLOTS, 128), F32)] * R
+            if low:
+                layers = zero + own_layers + beyond[0:11]
+            else:
+                layers = beyond[1:12] + own_layers + zero
+            for z, smooth, slope in z_filter(layers, count):
+                hs[SLOTS * z : SLOTS * (z + 1)] = smooth.astype(BF16)
+                hd[SLOTS * z : SLOTS * (z + 1)] = slope.astype(BF16)
+            yield
+            p01 = lax.dot_general(
+                get("wy_strip", 128), hs[...], NT, preferred_element_type=F32
+            ).astype(BF16)
+            p2 = lax.dot_general(
+                get("wy_strip_slope", 128), hd[...], NT, preferred_element_type=F32
+            ).astype(BF16)
+            yield
+            groups = [slice(256 * c, 256 * (c + 1)) for c in range(n)]
+            stacks = [
+                jnp.concatenate([p[:, g] for g in groups], axis=0) for p in (p01[0:gr], p01[gr:], p2)
+            ]
+            grads = [
+                jnp.dot(stack, get(name), preferred_element_type=F32).astype(BF16).reshape(n, gr, 256)
+                for stack, name in zip(stacks, ("bdd", "bds", "bds"))
+            ]
+            yield
+            for c, (a, b) in enumerate(pair_table):
+                pstrip[:, c * gr : (c + 1) * gr] = grads[a] * grads[b]
+            yield
+            smoothed = []
+            for c in range(n):
+                for half in range(2):
+                    part = pstrip[c, half * 3 * gr : (half + 1) * 3 * gr]
+                    out = jnp.dot(ysm, part, preferred_element_type=F32)
+                    smoothed.append(jnp.where(outside_x, 0.0, out).astype(BF16))
+            yield
+            u = jnp.dot(jnp.concatenate(smoothed, axis=0), get("bdx"), preferred_element_type=F32)
+            u = u.astype(BF16)
+            for name in ("0", "1"):
+                at = place_of[("g_low" if low else "g_high") + name][0]
+                total = None
+                for c in range(n):
+                    g = w[at + 64 * c : at + 64 * (c + 1), :]
+                    term = jnp.dot(u[n_rows * c : n_rows * (c + 1)], g, preferred_element_type=F32)
+                    total = term if total is None else total + term
+                sums.extend([total[:, 0:quarter], total[:, 128 : 128 + quarter]])
+
+        stages = strips_by_stage()
+        layers_to_sums(
+            get, ysm, load, LAST[low], (rows, cols), u3, *scratch, between=stages
         )
-        beyond = [far[k].astype(F32) for k in range(EXTRA)]
-        zero = [jnp.zeros((SLOTS, 128), F32)] * R
-        if low:
-            layers = zero + own_layers + beyond[0:11]
-        else:
-            layers = beyond[1:12] + own_layers + zero
-        for z, smooth, slope in z_filter(layers, count):
-            hs[SLOTS * z : SLOTS * (z + 1)] = smooth.astype(BF16)
-            hd[SLOTS * z : SLOTS * (z + 1)] = slope.astype(BF16)
-        p01 = lax.dot_general(
-            get("wy_strip", 128), hs[...], NT, preferred_element_type=F32
-        ).astype(BF16)
-        p2 = lax.dot_general(
-            get("wy_strip_slope", 128), hd[...], NT, preferred_element_type=F32
-        ).astype(BF16)
-        groups = [slice(256 * c, 256 * (c + 1)) for c in range(n)]
-        stacks = [
-            jnp.concatenate([p[:, g] for g in groups], axis=0) for p in (p01[0:gr], p01[gr:], p2)
-        ]
-        grads = [
-            jnp.dot(stack, get(name), preferred_element_type=F32).astype(BF16).reshape(n, gr, 256)
-            for stack, name in zip(stacks, ("bdd", "bds", "bds"))
-        ]
-        for c, (a, b) in enumerate(pair_table):
-            pstrip[:, c * gr : (c + 1) * gr] = grads[a] * grads[b]
-        smoothed = []
-        for c in range(n):
-            for half in range(2):
-                part = pstrip[c, half * 3 * gr : (half + 1) * 3 * gr]
-                out = jnp.dot(ysm, part, preferred_element_type=F32)
-                smoothed.append(jnp.where(outside_x, 0.0, out).astype(BF16))
-        u = jnp.dot(jnp.concatenate(smoothed, axis=0), get("bdx"), preferred_element_type=F32)
-        u = u.astype(BF16)
-        sums = []
-        for name in ("0", "1"):
-            at = place_of[("g_low" if low else "g_high") + name][0]
-            total = None
-            for c in range(n):
-                g = w[at + 64 * c : at + 64 * (c + 1), :]
-                term = jnp.dot(u[n_rows * c : n_rows * (c + 1)], g, preferred_element_type=F32)
-                total = term if total is None else total + term
-            sums += [total[:, 0:quarter], total[:, 128 : 128 + quarter]]
-        layers_to_sums(get, ysm, load, LAST[low], (rows, cols), u3, *scratch)
+        for _ in stages:
+            pass
         held = held_layers(depth, low)
         for q in range(depth // 4):
             total = weighted(sums[q], (u1, u2, u3), held, zs[:, q + 2])

time: 18.7 us -> 18.7 us (level)
  no operation moved by 1% of the time
where the time goes in v13:
time: 18.7 us; the launch traced here: 18.6 us
  starting transfers between devices  9.34 us (50%)
  Pallas kernels  7.63 us (41%)
  local copies, waits for them, and re-layouts  1.48 us (8%)
    pallas_call x9, Pallas kernels, call(): pl.pallas_call(body, out_shape=list(outs), in_specs=[hbm] * n_hbm + [vmem...  7.63 us
    ppermute x1, starting transfers between devices, per_device(): r2 = lax.ppermute(s2, 'row', inner)  4.55 us
    ppermute x1, starting transfers between devices, per_device(): zxs.append(lax.ppermute(messages[n_side + side], ('gz', 'col'), both))  1.56 us
    unnamed x1, local copies, waits for them, and re-layouts  1.48 us
    ppermute x1, starting transfers between devices, per_device(): zown = lax.ppermute(zmsg, 'gz', swap)  1.27 us
    ppermute x1, starting transfers between devices, per_device(): zcorner = lax.ppermute(zcmsg, 'gz', swap)  0.92 us
    ppermute x1, starting transfers between devices, per_device(): sums = lax.ppermute(send, 'gz', swap)  0.67 us
  transfers between devices with their start and end apart: 7, of which 0 were waited for; matrix products, arithmetic and copies ran while one was open for 8% of the time, Pallas kernels for 30%

profile of v13, /device:TPU:1, one launch (start us, length us, event | category | flops | bytes accessed | tf_op | source)
XLA Modules:
  0.0 18.6 jit_solution(1858541962300012475)
XLA Ops:
  0.0 1.2 %load.1 = (bf16[176,256]{1,0:T(8,128)(2,1)S(1)}, bf16[176,256]{1,0:T(8,128)(2,1)S(1)}, bf16[16,64,256]{2,1,0:T(8,128)(2,1)S(1)}) custom-call(bf16[16,64,256]{2,1,0:T(8,128)(2,1)} %vol.1), custom_call_target="tpu_custom_call" | custom-call | bytes 1228800 | tf_op jit(solution)/shard_map/load/pallas_call | solution.py:642
  1.2 0.1 collective-permute-start
  1.3 4.6 %collective-permute-start.1 = (bf16[176,256]{1,0:T(8,128)(2,1)S(1)}, bf16[176,256]{1,0:T(8,128)(2,1)S(1)}, u32[]{:S(2)}, u32[]{:S(2)}) collective-permute-start(bf16[176,256]{1,0:T(8,128)(2,1)S(1)} %get-tuple-element.20), channel_id=1, source_target_pairs={{2,4},{6,8},{10,12},{4,2},{8,6},{12,10},{3,5},{7,9},{11,13},{5,3},... | collective-permute-start | bytes 270344 | tf_op jit(solution)/shard_map/ppermute | solution.py:688
  5.9 0.3 %edges.1 = (bf16[8,32,128]{2,1,0:T(8,128)(2,1)S(1)}, bf16[480,128]{1,0:T(8,128)(2,1)S(1)}, bf16[96,128]{1,0:T(8,128)(2,1)S(1)}) custom-call(bf16[16,64,256]{2,1,0:T(8,128)(2,1)S(1)} %get-tuple-element.18.refs_0_), custom_call_target="tpu_custom_call" | custom-call | bytes 737280 | tf_op jit(solution)/shard_map/edges/pallas_call | solution.py:642
  6.2 1.3 %collective-permute-start.2 = (bf16[480,128]{1,0:T(8,128)(2,1)S(1)}, bf16[480,128]{1,0:T(8,128)(2,1)S(1)}, u32[]{:S(2)}, u32[]{:S(2)}) collective-permute-start(bf16[480,128]{1,0:T(8,128)(2,1)S(1)} %get-tuple-element.25), channel_id=1, source_target_pairs={{0,16},{16,0},{1,17},{17,1},{2,18},{18,2},{3,19},{19,3},{4,20},{20... | collective-permute-start | bytes 368648 | tf_op jit(solution)/shard_map/ppermute | solution.py:700
  7.5 1.5 %copy.6.w = bf16[3504,256]{1,0:T(8,128)(2,1)S(1)} copy(bf16[3504,256]{1,0:T(8,128)(2,1)} %constant.2.clone) | data formatting | bytes 3588096
  9.0 0.0 collective-permute-done.refs_0_
  9.0 0.0 collective-permute-done.1.refs_1_
  9.0 0.4 %pack.1 = (bf16[16,32,256]{2,1,0:T(8,128)(2,1)S(1)}, bf16[4,32,128]{2,1,0:T(8,128)(2,1)S(1)}, bf16[176,128]{1,0:T(8,128)(2,1)S(1)}, bf16[144,128]{1,0:T(8,128)(2,1)S(1)}, bf16[128,128]{1,0:T(8,128)(2,1)S(1)}) custom-call(bf16[176,256]{1,0:T(8,128)(2,1)S(1)} %collective-permute-done.refs_0_, bf16[176,256]{1,0:T(8,128)(2,1)S(1)} %collective-permute-done.1.refs_1_, ...), custom_call_target="tpu_custom_call" | custom-call | bytes 2408448 | tf_op jit(solution)/shard_map/pack/pallas_call | solution.py:642
  9.4 0.9 %collective-permute-start.3 = (bf16[176,128]{1,0:T(8,128)(2,1)S(1)}, bf16[176,128]{1,0:T(8,128)(2,1)S(1)}, u32[]{:S(2)}, u32[]{:S(2)}) collective-permute-start(bf16[176,128]{1,0:T(8,128)(2,1)S(1)} %get-tuple-element.26), channel_id=1, source_target_pairs={{0,16},{16,0},{1,17},{17,1},{2,18},{18,2},{3,19},{19,3},{4,20},{20... | collective-permute-start | bytes 135176 | tf_op jit(solution)/shard_map/ppermute | solution.py:709
  10.3 1.6 %collective-permute-start.4 = (bf16[128,128]{1,0:T(8,128)(2,1)S(1)}, bf16[128,128]{1,0:T(8,128)(2,1)S(1)}, u32[]{:S(2)}, u32[]{:S(2)}) collective-permute-start(bf16[128,128]{1,0:T(8,128)(2,1)S(1)} %get-tuple-element.27), channel_id=1, source_target_pairs={{0,17},{1,16},{16,1},{17,0},{2,19},{3,18},{18,3},{19,2},{4,21},{5,... | collective-permute-start | bytes 98312 | tf_op jit(solution)/shard_map/ppermute | solution.py:718
  11.8 0.2 %collective-permute-start.5 = (bf16[144,128]{1,0:T(8,128)(2,1)S(1)}, bf16[144,128]{1,0:T(8,128)(2,1)S(1)}, u32[]{:S(2)}, u32[]{:S(2)}) collective-permute-start(bf16[144,128]{1,0:T(8,128)(2,1)S(1)} %get-tuple-element.29), channel_id=1, source_target_pairs={{0,1},{1,0},{2,3},{3,2},{4,5},{5,4},{6,7},{7,6},{8,9},{9,8},{10,11... | collective-permute-start | bytes 110600 | tf_op jit(solution)/shard_map/ppermute | solution.py:717
  12.1 1.1 %first.1.refs_4_.refs_5_ = f32[5,96,64]{2,1,0:T(8,128)S(1)} custom-call(bf16[16,64,256]{2,1,0:T(8,128)(2,1)S(1)} %get-tuple-element.18.refs_0_, bf16[16,32,256]{2,1,0:T(8,128)(2,1)S(1)} %get-tuple-element.22.refs_1_, bf16[3504,256]{1,0:T(8,128)(2,1)S(1)} %stage.1.refs_2_.refs_5_.refs_7_), custom_call_target="tpu_custom_call" | custom-call | flops 349962240 | bytes 2703360 | tf_op jit(solution)/shard_map/first/pallas_call | solution.py:642
  13.2 0.0 collective-permute-done.2.zown.refs_2_
  13.2 0.0 collective-permute-done.3.zcorner.refs_3_
  13.3 1.1 %near.1 = (f32[3,96,64]{2,1,0:T(8,128)S(1)}, bf16[96,128]{1,0:T(8,128)(2,1)S(1)}) custom-call(bf16[16,64,256]{2,1,0:T(8,128)(2,1)S(1)} %get-tuple-element.18.refs_0_, bf16[16,32,256]{2,1,0:T(8,128)(2,1)S(1)} %get-tuple-element.22.refs_1_, bf16[480,128]{1,0:T(8,128)(2,1)S(1)} %collective-permute-done.2.zown.refs_2_, ...), custom_call_target="tpu_custom_call" | custom-call | flops 209977344 | bytes 2969600 | tf_op jit(solution)/shard_map/near/pallas_call | solution.py:642
  14.4 0.7 %collective-permute-start.6 = (bf16[96,128]{1,0:T(8,128)(2,1)S(1)}, bf16[96,128]{1,0:T(8,128)(2,1)S(1)}, u32[]{:S(2)}, u32[]{:S(2)}) collective-permute-start(bf16[96,128]{1,0:T(8,128)(2,1)S(1)} %get-tuple-element.30), channel_id=1, source_target_pairs={{0,16},{16,0},{1,17},{17,1},{2,18},{18,2},{3,19},{19,3},{4,20},{20... | collective-permute-start | bytes 73736 | tf_op jit(solution)/shard_map/ppermute | solution.py:732
  15.1 0.0 collective-permute-done.4.refs_0_
  15.1 0.1 beyond.1.refs_4_
  15.2 0.0 collective-permute-done.5.refs_8_
  15.2 2.6 %last.1.own = f32[6,4,16,64]{3,2,1,0:T(8,128)S(1)} custom-call(bf16[16,64,256]{2,1,0:T(8,128)(2,1)S(1)} %get-tuple-element.18.refs_0_, bf16[16,32,256]{2,1,0:T(8,128)(2,1)S(1)} %get-tuple-element.22.refs_1_, bf16[8,32,128]{2,1,0:T(8,128)(2,1)S(1)} %get-tuple-element.23.refs_2_, bf16[4,32,128]{2,1,0:T(8,128)(2,1)S(1)} %get-tuple-element.24.refs_3_, ...), custom_call_target="tpu_custom_call" | custom-call | flops 909901824 | bytes 3108864 | tf_op jit(solution)/shard_map/last/pallas_call | solution.py:642
  17.8 0.0 collective-permute-done.6.got
  17.8 0.8 %add.1 = f32[6,4,16,64]{3,2,1,0:T(8,128)} custom-call(f32[6,4,16,64]{3,2,1,0:T(8,128)S(1)} %last.1.own, bf16[96,128]{1,0:T(8,128)(2,1)S(1)} %collective-permute-done.6.got), custom_call_target="tpu_custom_call" | custom-call | bytes 221184 | tf_op jit(solution)/shard_map/add/pallas_call | solution.py:642
  (1 shorter events, 0.0 us)
Async XLA Ops:
  1.2 7.7 %collective-permute-start = (bf16[176,256]{1,0:T(8,128)(2,1)S(1)}, bf16[176,256]{1,0:T(8,128)(2,1)S(1)}, u32[]{:S(2)}, u32[]{:S(2)}) collective-permute-start(bf16[176,256]{1,0:T(8,128)(2,1)S(1)} %get-tuple-element.19), channel_id=1, source_target_pairs={{0,2},{2,0},{4,6},{6,4},{8,10},{10,8},{12,14},{14,12},{1,3},{3,1},... | collective-permute-start | bytes 270344 | tf_op jit(solution)/shard_map/ppermute | solution.py:689
  1.3 7.6 %collective-permute-start.1 = (bf16[176,256]{1,0:T(8,128)(2,1)S(1)}, bf16[176,256]{1,0:T(8,128)(2,1)S(1)}, u32[]{:S(2)}, u32[]{:S(2)}) collective-permute-start(bf16[176,256]{1,0:T(8,128)(2,1)S(1)} %get-tuple-element.20), channel_id=1, source_target_pairs={{2,4},{6,8},{10,12},{4,2},{8,6},{12,10},{3,5},{7,9},{11,13},{5,3},... | collective-permute-start | bytes 270344 | tf_op jit(solution)/shard_map/ppermute | solution.py:688
  6.2 7.0 %collective-permute-start.2 = (bf16[480,128]{1,0:T(8,128)(2,1)S(1)}, bf16[480,128]{1,0:T(8,128)(2,1)S(1)}, u32[]{:S(2)}, u32[]{:S(2)}) collective-permute-start(bf16[480,128]{1,0:T(8,128)(2,1)S(1)} %get-tuple-element.25), channel_id=1, source_target_pairs={{0,16},{16,0},{1,17},{17,1},{2,18},{18,2},{3,19},{19,3},{4,20},{20... | collective-permute-start | bytes 368648 | tf_op jit(solution)/shard_map/ppermute | solution.py:700
  9.4 3.9 %collective-permute-start.3 = (bf16[176,128]{1,0:T(8,128)(2,1)S(1)}, bf16[176,128]{1,0:T(8,128)(2,1)S(1)}, u32[]{:S(2)}, u32[]{:S(2)}) collective-permute-start(bf16[176,128]{1,0:T(8,128)(2,1)S(1)} %get-tuple-element.26), channel_id=1, source_target_pairs={{0,16},{16,0},{1,17},{17,1},{2,18},{18,2},{3,19},{19,3},{4,20},{20... | collective-permute-start | bytes 135176 | tf_op jit(solution)/shard_map/ppermute | solution.py:709
  10.3 4.8 %collective-permute-start.4 = (bf16[128,128]{1,0:T(8,128)(2,1)S(1)}, bf16[128,128]{1,0:T(8,128)(2,1)S(1)}, u32[]{:S(2)}, u32[]{:S(2)}) collective-permute-start(bf16[128,128]{1,0:T(8,128)(2,1)S(1)} %get-tuple-element.27), channel_id=1, source_target_pairs={{0,17},{1,16},{16,1},{17,0},{2,19},{3,18},{18,3},{19,2},{4,21},{5,... | collective-permute-start | bytes 98312 | tf_op jit(solution)/shard_map/ppermute | solution.py:718
  11.8 3.3 %collective-permute-start.5 = (bf16[144,128]{1,0:T(8,128)(2,1)S(1)}, bf16[144,128]{1,0:T(8,128)(2,1)S(1)}, u32[]{:S(2)}, u32[]{:S(2)}) collective-permute-start(bf16[144,128]{1,0:T(8,128)(2,1)S(1)} %get-tuple-element.29), channel_id=1, source_target_pairs={{0,1},{1,0},{2,3},{3,2},{4,5},{5,4},{6,7},{7,6},{8,9},{9,8},{10,11... | collective-permute-start | bytes 110600 | tf_op jit(solution)/shard_map/ppermute | solution.py:717
  14.4 3.4 %collective-permute-start.6 = (bf16[96,128]{1,0:T(8,128)(2,1)S(1)}, bf16[96,128]{1,0:T(8,128)(2,1)S(1)}, u32[]{:S(2)}, u32[]{:S(2)}) collective-permute-start(bf16[96,128]{1,0:T(8,128)(2,1)S(1)} %get-tuple-element.30), channel_id=1, source_target_pairs={{0,16},{16,0},{1,17},{17,1},{2,18},{18,2},{3,19},{19,3},{4,20},{20... | collective-permute-start | bytes 73736 | tf_op jit(solution)/shard_map/ppermute | solution.py:732

commit v14 on v9

--- a/solution.py
+++ b/solution.py
@@ -355,11 +355,9 @@
         zxmsg[0 : 8 * n2] = x_own[pl.ds(pl.multiple_of(8 * first2, 16), 8 * n2)]
         zxmsg[8 * n2 : 8 * n2 + message.shape[0]] = message
         at = 8 * n2 + message.shape[0]
-        behind = x_own[8 * pairs :]
-        sent = 4 * n2
-        zxmsg[at : at + sent] = jnp.where(
-            low, behind[skip // 2 : skip // 2 + sent], behind[0:sent]
-        )
+        behind = x_own[8 * pairs :].astype(F32)
+        turned = jnp.concatenate([behind[skip // 2 :], behind[0 : skip // 2]], axis=0)
+        zxmsg[at : at + 4 * pairs] = jnp.where(low, turned, behind).astype(BF16)
     base = jnp.where(gz == 0, depth - R, 0)
     edge = yud[pl.ds(base, R)].reshape(R * 2 * HALO, cols)
     halve(zcorner, 0, jnp.dot(get("corner"), edge, preferred_element_type=F32).astype(BF16))

time: 18.6 us -> 18.6 us (level)
  no operation moved by 1% of the time
where the time goes in v14:
time: 18.6 us; the launch traced here: 18.4 us
  starting transfers between devices  9.34 us (50%)
  Pallas kernels  7.45 us (40%)
  local copies, waits for them, and re-layouts  1.48 us (8%)
    pallas_call x9, Pallas kernels, call(): pl.pallas_call(body, out_shape=list(outs), in_specs=[hbm] * n_hbm + [vmem...  7.45 us
    ppermute x1, starting transfers between devices, per_device(): r2 = lax.ppermute(s2, 'row', inner)  4.55 us
    ppermute x1, starting transfers between devices, per_device(): zxs.append(lax.ppermute(messages[n_side + side], ('gz', 'col'), both))  1.56 us
    unnamed x1, local copies, waits for them, and re-layouts  1.48 us
    ppermute x1, starting transfers between devices, per_device(): zown = lax.ppermute(zmsg, 'gz', swap)  1.27 us
    ppermute x1, starting transfers between devices, per_device(): zcorner = lax.ppermute(zcmsg, 'gz', swap)  0.92 us
    ppermute x1, starting transfers between devices, per_device(): sums = lax.ppermute(send, 'gz', swap)  0.67 us
  transfers between devices with their start and end apart: 7, of which 0 were waited for; matrix products, arithmetic and copies ran while one was open for 8% of the time, Pallas kernels for 30%

profile of v14, /device:TPU:1, one launch (start us, length us, event | category | flops | bytes accessed | tf_op | source)
XLA Modules:
  0.0 18.4 jit_solution(3700114659836020028)
XLA Ops:
  0.0 1.2 %load.1 = (bf16[176,256]{1,0:T(8,128)(2,1)S(1)}, bf16[176,256]{1,0:T(8,128)(2,1)S(1)}, bf16[16,64,256]{2,1,0:T(8,128)(2,1)S(1)}) custom-call(bf16[16,64,256]{2,1,0:T(8,128)(2,1)} %vol.1), custom_call_target="tpu_custom_call" | custom-call | bytes 1228800 | tf_op jit(solution)/shard_map/load/pallas_call | solution.py:625
  1.2 0.1 collective-permute-start
  1.3 4.6 %collective-permute-start.1 = (bf16[176,256]{1,0:T(8,128)(2,1)S(1)}, bf16[176,256]{1,0:T(8,128)(2,1)S(1)}, u32[]{:S(2)}, u32[]{:S(2)}) collective-permute-start(bf16[176,256]{1,0:T(8,128)(2,1)S(1)} %get-tuple-element.20), channel_id=1, source_target_pairs={{2,4},{6,8},{10,12},{4,2},{8,6},{12,10},{3,5},{7,9},{11,13},{5,3},... | collective-permute-start | bytes 270344 | tf_op jit(solution)/shard_map/ppermute | solution.py:671
  5.9 0.3 %edges.1 = (bf16[8,32,128]{2,1,0:T(8,128)(2,1)S(1)}, bf16[480,128]{1,0:T(8,128)(2,1)S(1)}, bf16[96,128]{1,0:T(8,128)(2,1)S(1)}) custom-call(bf16[16,64,256]{2,1,0:T(8,128)(2,1)S(1)} %get-tuple-element.18.refs_0_), custom_call_target="tpu_custom_call" | custom-call | bytes 737280 | tf_op jit(solution)/shard_map/edges/pallas_call | solution.py:625
  6.2 1.3 %collective-permute-start.2 = (bf16[480,128]{1,0:T(8,128)(2,1)S(1)}, bf16[480,128]{1,0:T(8,128)(2,1)S(1)}, u32[]{:S(2)}, u32[]{:S(2)}) collective-permute-start(bf16[480,128]{1,0:T(8,128)(2,1)S(1)} %get-tuple-element.25), channel_id=1, source_target_pairs={{0,16},{16,0},{1,17},{17,1},{2,18},{18,2},{3,19},{19,3},{4,20},{20... | collective-permute-start | bytes 368648 | tf_op jit(solution)/shard_map/ppermute | solution.py:683
  7.5 1.5 %copy.6.w = bf16[3504,256]{1,0:T(8,128)(2,1)S(1)} copy(bf16[3504,256]{1,0:T(8,128)(2,1)} %constant.2.clone) | data formatting | bytes 3588096
  9.0 0.0 collective-permute-done.refs_0_
  9.0 0.0 collective-permute-done.1.refs_1_
  9.0 0.4 %pack.1 = (bf16[16,32,256]{2,1,0:T(8,128)(2,1)S(1)}, bf16[4,32,128]{2,1,0:T(8,128)(2,1)S(1)}, bf16[176,128]{1,0:T(8,128)(2,1)S(1)}, bf16[144,128]{1,0:T(8,128)(2,1)S(1)}, bf16[128,128]{1,0:T(8,128)(2,1)S(1)}) custom-call(bf16[176,256]{1,0:T(8,128)(2,1)S(1)} %collective-permute-done.refs_0_, bf16[176,256]{1,0:T(8,128)(2,1)S(1)} %collective-permute-done.1.refs_1_, ...), custom_call_target="tpu_custom_call" | custom-call | bytes 2408448 | tf_op jit(solution)/shard_map/pack/pallas_call | solution.py:625
  9.4 0.9 %collective-permute-start.3 = (bf16[176,128]{1,0:T(8,128)(2,1)S(1)}, bf16[176,128]{1,0:T(8,128)(2,1)S(1)}, u32[]{:S(2)}, u32[]{:S(2)}) collective-permute-start(bf16[176,128]{1,0:T(8,128)(2,1)S(1)} %get-tuple-element.26), channel_id=1, source_target_pairs={{0,16},{16,0},{1,17},{17,1},{2,18},{18,2},{3,19},{19,3},{4,20},{20... | collective-permute-start | bytes 135176 | tf_op jit(solution)/shard_map/ppermute | solution.py:692
  10.3 1.6 %collective-permute-start.4 = (bf16[128,128]{1,0:T(8,128)(2,1)S(1)}, bf16[128,128]{1,0:T(8,128)(2,1)S(1)}, u32[]{:S(2)}, u32[]{:S(2)}) collective-permute-start(bf16[128,128]{1,0:T(8,128)(2,1)S(1)} %get-tuple-element.27), channel_id=1, source_target_pairs={{0,17},{1,16},{16,1},{17,0},{2,19},{3,18},{18,3},{19,2},{4,21},{5,... | collective-permute-start | bytes 98312 | tf_op jit(solution)/shard_map/ppermute | solution.py:701
  11.8 0.2 %collective-permute-start.5 = (bf16[144,128]{1,0:T(8,128)(2,1)S(1)}, bf16[144,128]{1,0:T(8,128)(2,1)S(1)}, u32[]{:S(2)}, u32[]{:S(2)}) collective-permute-start(bf16[144,128]{1,0:T(8,128)(2,1)S(1)} %get-tuple-element.29), channel_id=1, source_target_pairs={{0,1},{1,0},{2,3},{3,2},{4,5},{5,4},{6,7},{7,6},{8,9},{9,8},{10,11... | collective-permute-start | bytes 110600 | tf_op jit(solution)/shard_map/ppermute | solution.py:700
  12.1 1.1 %first.1.refs_4_.refs_5_ = f32[5,96,64]{2,1,0:T(8,128)S(1)} custom-call(bf16[16,64,256]{2,1,0:T(8,128)(2,1)S(1)} %get-tuple-element.18.refs_0_, bf16[16,32,256]{2,1,0:T(8,128)(2,1)S(1)} %get-tuple-element.22.refs_1_, bf16[3504,256]{1,0:T(8,128)(2,1)S(1)} %stage.1.refs_2_.refs_5_.refs_7_), custom_call_target="tpu_custom_call" | custom-call | flops 349962240 | bytes 2703360 | tf_op jit(solution)/shard_map/first/pallas_call | solution.py:625
  13.2 0.0 collective-permute-done.2.zown.refs_2_
  13.2 0.0 collective-permute-done.3.zcorner.refs_3_
  13.3 1.1 %near.1 = (f32[3,96,64]{2,1,0:T(8,128)S(1)}, bf16[96,128]{1,0:T(8,128)(2,1)S(1)}) custom-call(bf16[16,64,256]{2,1,0:T(8,128)(2,1)S(1)} %get-tuple-element.18.refs_0_, bf16[16,32,256]{2,1,0:T(8,128)(2,1)S(1)} %get-tuple-element.22.refs_1_, bf16[480,128]{1,0:T(8,128)(2,1)S(1)} %collective-permute-done.2.zown.refs_2_, ...), custom_call_target="tpu_custom_call" | custom-call | flops 209977344 | bytes 2969600 | tf_op jit(solution)/shard_map/near/pallas_call | solution.py:625
  14.4 0.7 %collective-permute-start.6 = (bf16[96,128]{1,0:T(8,128)(2,1)S(1)}, bf16[96,128]{1,0:T(8,128)(2,1)S(1)}, u32[]{:S(2)}, u32[]{:S(2)}) collective-permute-start(bf16[96,128]{1,0:T(8,128)(2,1)S(1)} %get-tuple-element.30), channel_id=1, source_target_pairs={{0,16},{16,0},{1,17},{17,1},{2,18},{18,2},{3,19},{19,3},{4,20},{20... | collective-permute-start | bytes 73736 | tf_op jit(solution)/shard_map/ppermute | solution.py:715
  15.1 0.0 collective-permute-done.4.refs_0_
  15.1 0.1 beyond.1.refs_4_
  15.2 0.0 collective-permute-done.5.refs_8_
  15.2 2.4 %last.1.own = f32[6,4,16,64]{3,2,1,0:T(8,128)S(1)} custom-call(bf16[16,64,256]{2,1,0:T(8,128)(2,1)S(1)} %get-tuple-element.18.refs_0_, bf16[16,32,256]{2,1,0:T(8,128)(2,1)S(1)} %get-tuple-element.22.refs_1_, bf16[8,32,128]{2,1,0:T(8,128)(2,1)S(1)} %get-tuple-element.23.refs_2_, bf16[4,32,128]{2,1,0:T(8,128)(2,1)S(1)} %get-tuple-element.24.refs_3_, ...), custom_call_target="tpu_custom_call" | custom-call | flops 909901824 | bytes 3108864 | tf_op jit(solution)/shard_map/last/pallas_call | solution.py:625
  17.6 0.0 collective-permute-done.6.got
  17.6 0.8 %add.1 = f32[6,4,16,64]{3,2,1,0:T(8,128)} custom-call(f32[6,4,16,64]{3,2,1,0:T(8,128)S(1)} %last.1.own, bf16[96,128]{1,0:T(8,128)(2,1)S(1)} %collective-permute-done.6.got), custom_call_target="tpu_custom_call" | custom-call | bytes 221184 | tf_op jit(solution)/shard_map/add/pallas_call | solution.py:625
  (1 shorter events, 0.0 us)
Async XLA Ops:
  1.2 7.7 %collective-permute-start = (bf16[176,256]{1,0:T(8,128)(2,1)S(1)}, bf16[176,256]{1,0:T(8,128)(2,1)S(1)}, u32[]{:S(2)}, u32[]{:S(2)}) collective-permute-start(bf16[176,256]{1,0:T(8,128)(2,1)S(1)} %get-tuple-element.19), channel_id=1, source_target_pairs={{0,2},{2,0},{4,6},{6,4},{8,10},{10,8},{12,14},{14,12},{1,3},{3,1},... | collective-permute-start | bytes 270344 | tf_op jit(solution)/shard_map/ppermute | solution.py:672
  1.3 7.6 %collective-permute-start.1 = (bf16[176,256]{1,0:T(8,128)(2,1)S(1)}, bf16[176,256]{1,0:T(8,128)(2,1)S(1)}, u32[]{:S(2)}, u32[]{:S(2)}) collective-permute-start(bf16[176,256]{1,0:T(8,128)(2,1)S(1)} %get-tuple-element.20), channel_id=1, source_target_pairs={{2,4},{6,8},{10,12},{4,2},{8,6},{12,10},{3,5},{7,9},{11,13},{5,3},... | collective-permute-start | bytes 270344 | tf_op jit(solution)/shard_map/ppermute | solution.py:671
  6.2 7.0 %collective-permute-start.2 = (bf16[480,128]{1,0:T(8,128)(2,1)S(1)}, bf16[480,128]{1,0:T(8,128)(2,1)S(1)}, u32[]{:S(2)}, u32[]{:S(2)}) collective-permute-start(bf16[480,128]{1,0:T(8,128)(2,1)S(1)} %get-tuple-element.25), channel_id=1, source_target_pairs={{0,16},{16,0},{1,17},{17,1},{2,18},{18,2},{3,19},{19,3},{4,20},{20... | collective-permute-start | bytes 368648 | tf_op jit(solution)/shard_map/ppermute | solution.py:683
  9.4 3.9 %collective-permute-start.3 = (bf16[176,128]{1,0:T(8,128)(2,1)S(1)}, bf16[176,128]{1,0:T(8,128)(2,1)S(1)}, u32[]{:S(2)}, u32[]{:S(2)}) collective-permute-start(bf16[176,128]{1,0:T(8,128)(2,1)S(1)} %get-tuple-element.26), channel_id=1, source_target_pairs={{0,16},{16,0},{1,17},{17,1},{2,18},{18,2},{3,19},{19,3},{4,20},{20... | collective-permute-start | bytes 135176 | tf_op jit(solution)/shard_map/ppermute | solution.py:692
  10.3 4.8 %collective-permute-start.4 = (bf16[128,128]{1,0:T(8,128)(2,1)S(1)}, bf16[128,128]{1,0:T(8,128)(2,1)S(1)}, u32[]{:S(2)}, u32[]{:S(2)}) collective-permute-start(bf16[128,128]{1,0:T(8,128)(2,1)S(1)} %get-tuple-element.27), channel_id=1, source_target_pairs={{0,17},{1,16},{16,1},{17,0},{2,19},{3,18},{18,3},{19,2},{4,21},{5,... | collective-permute-start | bytes 98312 | tf_op jit(solution)/shard_map/ppermute | solution.py:701
  11.8 3.3 %collective-permute-start.5 = (bf16[144,128]{1,0:T(8,128)(2,1)S(1)}, bf16[144,128]{1,0:T(8,128)(2,1)S(1)}, u32[]{:S(2)}, u32[]{:S(2)}) collective-permute-start(bf16[144,128]{1,0:T(8,128)(2,1)S(1)} %get-tuple-element.29), channel_id=1, source_target_pairs={{0,1},{1,0},{2,3},{3,2},{4,5},{5,4},{6,7},{7,6},{8,9},{9,8},{10,11... | collective-permute-start | bytes 110600 | tf_op jit(solution)/shard_map/ppermute | solution.py:700
  14.4 3.2 %collective-permute-start.6 = (bf16[96,128]{1,0:T(8,128)(2,1)S(1)}, bf16[96,128]{1,0:T(8,128)(2,1)S(1)}, u32[]{:S(2)}, u32[]{:S(2)}) collective-permute-start(bf16[96,128]{1,0:T(8,128)(2,1)S(1)} %get-tuple-element.30), channel_id=1, source_target_pairs={{0,16},{16,0},{1,17},{17,1},{2,18},{18,2},{3,19},{19,3},{4,20},{20... | collective-permute-start | bytes 73736 | tf_op jit(solution)/shard_map/ppermute | solution.py:715

commit v15 on v14

--- a/solution.py
+++ b/solution.py
@@ -368,8 +368,8 @@
     pass
 
 
-FIRST = {True: 5, False: 3}
-LAST = {True: 8, False: 10}
+FIRST = {True: 5, False: 2}
+LAST = {True: 8, False: 11}
 GROUP = 4
 EDGE = R
 

time: 18.6 us -> 18.5 us (level)
  no operation moved by 1% of the time
where the time goes in v15:
time: 18.5 us; the launch traced here: 18.3 us
  starting transfers between devices  9.26 us (50%)
  Pallas kernels  7.45 us (40%)
  local copies, waits for them, and re-layouts  1.48 us (8%)
    pallas_call x9, Pallas kernels, call(): pl.pallas_call(body, out_shape=list(outs), in_specs=[hbm] * n_hbm + [vmem...  7.45 us
    ppermute x1, starting transfers between devices, per_device(): r2 = lax.ppermute(s2, 'row', inner)  4.55 us
    ppermute x1, starting transfers between devices, per_device(): zxs.append(lax.ppermute(messages[n_side + side], ('gz', 'col'), both))  1.56 us
    unnamed x1, local copies, waits for them, and re-layouts  1.48 us
    ppermute x1, starting transfers between devices, per_device(): zown = lax.ppermute(zmsg, 'gz', swap)  1.27 us
    ppermute x1, starting transfers between devices, per_device(): zcorner = lax.ppermute(zcmsg, 'gz', swap)  0.92 us
    ppermute x1, starting transfers between devices, per_device(): sums = lax.ppermute(send, 'gz', swap)  0.6 us
  transfers between devices with their start and end apart: 7, of which 0 were waited for; matrix products, arithmetic and copies ran while one was open for 8% of the time, Pallas kernels for 30%

profile of v15, /device:TPU:1, one launch (start us, length us, event | category | flops | bytes accessed | tf_op | source)
XLA Modules:
  0.0 18.3 jit_solution(6960593191910800333)
XLA Ops:
  0.0 1.2 %load.1 = (bf16[176,256]{1,0:T(8,128)(2,1)S(1)}, bf16[176,256]{1,0:T(8,128)(2,1)S(1)}, bf16[16,64,256]{2,1,0:T(8,128)(2,1)S(1)}) custom-call(bf16[16,64,256]{2,1,0:T(8,128)(2,1)} %vol.1), custom_call_target="tpu_custom_call" | custom-call | bytes 1228800 | tf_op jit(solution)/shard_map/load/pallas_call | solution.py:625
  1.2 0.1 collective-permute-start
  1.3 4.6 %collective-permute-start.1 = (bf16[176,256]{1,0:T(8,128)(2,1)S(1)}, bf16[176,256]{1,0:T(8,128)(2,1)S(1)}, u32[]{:S(2)}, u32[]{:S(2)}) collective-permute-start(bf16[176,256]{1,0:T(8,128)(2,1)S(1)} %get-tuple-element.20), channel_id=1, source_target_pairs={{2,4},{6,8},{10,12},{4,2},{8,6},{12,10},{3,5},{7,9},{11,13},{5,3},... | collective-permute-start | bytes 270344 | tf_op jit(solution)/shard_map/ppermute | solution.py:671
  5.9 0.3 %edges.1 = (bf16[8,32,128]{2,1,0:T(8,128)(2,1)S(1)}, bf16[480,128]{1,0:T(8,128)(2,1)S(1)}, bf16[96,128]{1,0:T(8,128)(2,1)S(1)}) custom-call(bf16[16,64,256]{2,1,0:T(8,128)(2,1)S(1)} %get-tuple-element.18.refs_0_), custom_call_target="tpu_custom_call" | custom-call | bytes 737280 | tf_op jit(solution)/shard_map/edges/pallas_call | solution.py:625
  6.2 1.3 %collective-permute-start.2 = (bf16[480,128]{1,0:T(8,128)(2,1)S(1)}, bf16[480,128]{1,0:T(8,128)(2,1)S(1)}, u32[]{:S(2)}, u32[]{:S(2)}) collective-permute-start(bf16[480,128]{1,0:T(8,128)(2,1)S(1)} %get-tuple-element.25), channel_id=1, source_target_pairs={{0,16},{16,0},{1,17},{17,1},{2,18},{18,2},{3,19},{19,3},{4,20},{20... | collective-permute-start | bytes 368648 | tf_op jit(solution)/shard_map/ppermute | solution.py:683
  7.5 1.5 %copy.6.w = bf16[3504,256]{1,0:T(8,128)(2,1)S(1)} copy(bf16[3504,256]{1,0:T(8,128)(2,1)} %constant.2.clone) | data formatting | bytes 3588096
  9.0 0.0 collective-permute-done.refs_0_
  9.0 0.0 collective-permute-done.1.refs_1_
  9.0 0.4 %pack.1 = (bf16[16,32,256]{2,1,0:T(8,128)(2,1)S(1)}, bf16[4,32,128]{2,1,0:T(8,128)(2,1)S(1)}, bf16[176,128]{1,0:T(8,128)(2,1)S(1)}, bf16[144,128]{1,0:T(8,128)(2,1)S(1)}, bf16[128,128]{1,0:T(8,128)(2,1)S(1)}) custom-call(bf16[176,256]{1,0:T(8,128)(2,1)S(1)} %collective-permute-done.refs_0_, bf16[176,256]{1,0:T(8,128)(2,1)S(1)} %collective-permute-done.1.refs_1_, ...), custom_call_target="tpu_custom_call" | custom-call | bytes 2408448 | tf_op jit(solution)/shard_map/pack/pallas_call | solution.py:625
  9.4 0.9 %collective-permute-start.3 = (bf16[176,128]{1,0:T(8,128)(2,1)S(1)}, bf16[176,128]{1,0:T(8,128)(2,1)S(1)}, u32[]{:S(2)}, u32[]{:S(2)}) collective-permute-start(bf16[176,128]{1,0:T(8,128)(2,1)S(1)} %get-tuple-element.26), channel_id=1, source_target_pairs={{0,16},{16,0},{1,17},{17,1},{2,18},{18,2},{3,19},{19,3},{4,20},{20... | collective-permute-start | bytes 135176 | tf_op jit(solution)/shard_map/ppermute | solution.py:692
  10.3 1.6 %collective-permute-start.4 = (bf16[128,128]{1,0:T(8,128)(2,1)S(1)}, bf16[128,128]{1,0:T(8,128)(2,1)S(1)}, u32[]{:S(2)}, u32[]{:S(2)}) collective-permute-start(bf16[128,128]{1,0:T(8,128)(2,1)S(1)} %get-tuple-element.27), channel_id=1, source_target_pairs={{0,17},{1,16},{16,1},{17,0},{2,19},{3,18},{18,3},{19,2},{4,21},{5,... | collective-permute-start | bytes 98312 | tf_op jit(solution)/shard_map/ppermute | solution.py:701
  11.8 0.2 %collective-permute-start.5 = (bf16[144,128]{1,0:T(8,128)(2,1)S(1)}, bf16[144,128]{1,0:T(8,128)(2,1)S(1)}, u32[]{:S(2)}, u32[]{:S(2)}) collective-permute-start(bf16[144,128]{1,0:T(8,128)(2,1)S(1)} %get-tuple-element.29), channel_id=1, source_target_pairs={{0,1},{1,0},{2,3},{3,2},{4,5},{5,4},{6,7},{7,6},{8,9},{9,8},{10,11... | collective-permute-start | bytes 110600 | tf_op jit(solution)/shard_map/ppermute | solution.py:700
  12.1 1.1 %first.1.refs_4_.refs_5_ = f32[5,96,64]{2,1,0:T(8,128)S(1)} custom-call(bf16[16,64,256]{2,1,0:T(8,128)(2,1)S(1)} %get-tuple-element.18.refs_0_, bf16[16,32,256]{2,1,0:T(8,128)(2,1)S(1)} %get-tuple-element.22.refs_1_, bf16[3504,256]{1,0:T(8,128)(2,1)S(1)} %stage.1.refs_2_.refs_5_.refs_7_), custom_call_target="tpu_custom_call" | custom-call | flops 349962240 | bytes 2703360 | tf_op jit(solution)/shard_map/first/pallas_call | solution.py:625
  13.2 0.0 collective-permute-done.2.zown.refs_2_
  13.2 0.0 collective-permute-done.3.zcorner.refs_3_
  13.3 1.1 %near.1 = (f32[3,96,64]{2,1,0:T(8,128)S(1)}, bf16[96,128]{1,0:T(8,128)(2,1)S(1)}) custom-call(bf16[16,64,256]{2,1,0:T(8,128)(2,1)S(1)} %get-tuple-element.18.refs_0_, bf16[16,32,256]{2,1,0:T(8,128)(2,1)S(1)} %get-tuple-element.22.refs_1_, bf16[480,128]{1,0:T(8,128)(2,1)S(1)} %collective-permute-done.2.zown.refs_2_, ...), custom_call_target="tpu_custom_call" | custom-call | flops 209977344 | bytes 2969600 | tf_op jit(solution)/shard_map/near/pallas_call | solution.py:625
  14.4 0.6 %collective-permute-start.6 = (bf16[96,128]{1,0:T(8,128)(2,1)S(1)}, bf16[96,128]{1,0:T(8,128)(2,1)S(1)}, u32[]{:S(2)}, u32[]{:S(2)}) collective-permute-start(bf16[96,128]{1,0:T(8,128)(2,1)S(1)} %get-tuple-element.30), channel_id=1, source_target_pairs={{0,16},{16,0},{1,17},{17,1},{2,18},{18,2},{3,19},{19,3},{4,20},{20... | collective-permute-start | bytes 73736 | tf_op jit(solution)/shard_map/ppermute | solution.py:715
  15.0 0.0 collective-permute-done.4.refs_0_
  15.0 0.1 beyond.1.refs_4_
  15.1 0.0 collective-permute-done.5.refs_8_
  15.1 2.4 %last.1.own = f32[6,4,16,64]{3,2,1,0:T(8,128)S(1)} custom-call(bf16[16,64,256]{2,1,0:T(8,128)(2,1)S(1)} %get-tuple-element.18.refs_0_, bf16[16,32,256]{2,1,0:T(8,128)(2,1)S(1)} %get-tuple-element.22.refs_1_, bf16[8,32,128]{2,1,0:T(8,128)(2,1)S(1)} %get-tuple-element.23.refs_2_, bf16[4,32,128]{2,1,0:T(8,128)(2,1)S(1)} %get-tuple-element.24.refs_3_, ...), custom_call_target="tpu_custom_call" | custom-call | flops 979894272 | bytes 3108864 | tf_op jit(solution)/shard_map/last/pallas_call | solution.py:625
  17.5 0.0 collective-permute-done.6.got
  17.5 0.8 %add.1 = f32[6,4,16,64]{3,2,1,0:T(8,128)} custom-call(f32[6,4,16,64]{3,2,1,0:T(8,128)S(1)} %last.1.own, bf16[96,128]{1,0:T(8,128)(2,1)S(1)} %collective-permute-done.6.got), custom_call_target="tpu_custom_call" | custom-call | bytes 221184 | tf_op jit(solution)/shard_map/add/pallas_call | solution.py:625
  (1 shorter events, 0.0 us)
Async XLA Ops:
  1.2 7.7 %collective-permute-start = (bf16[176,256]{1,0:T(8,128)(2,1)S(1)}, bf16[176,256]{1,0:T(8,128)(2,1)S(1)}, u32[]{:S(2)}, u32[]{:S(2)}) collective-permute-start(bf16[176,256]{1,0:T(8,128)(2,1)S(1)} %get-tuple-element.19), channel_id=1, source_target_pairs={{0,2},{2,0},{4,6},{6,4},{8,10},{10,8},{12,14},{14,12},{1,3},{3,1},... | collective-permute-start | bytes 270344 | tf_op jit(solution)/shard_map/ppermute | solution.py:672
  1.3 7.6 %collective-permute-start.1 = (bf16[176,256]{1,0:T(8,128)(2,1)S(1)}, bf16[176,256]{1,0:T(8,128)(2,1)S(1)}, u32[]{:S(2)}, u32[]{:S(2)}) collective-permute-start(bf16[176,256]{1,0:T(8,128)(2,1)S(1)} %get-tuple-element.20), channel_id=1, source_target_pairs={{2,4},{6,8},{10,12},{4,2},{8,6},{12,10},{3,5},{7,9},{11,13},{5,3},... | collective-permute-start | bytes 270344 | tf_op jit(solution)/shard_map/ppermute | solution.py:671
  6.2 7.0 %collective-permute-start.2 = (bf16[480,128]{1,0:T(8,128)(2,1)S(1)}, bf16[480,128]{1,0:T(8,128)(2,1)S(1)}, u32[]{:S(2)}, u32[]{:S(2)}) collective-permute-start(bf16[480,128]{1,0:T(8,128)(2,1)S(1)} %get-tuple-element.25), channel_id=1, source_target_pairs={{0,16},{16,0},{1,17},{17,1},{2,18},{18,2},{3,19},{19,3},{4,20},{20... | collective-permute-start | bytes 368648 | tf_op jit(solution)/shard_map/ppermute | solution.py:683
  9.4 3.9 %collective-permute-start.3 = (bf16[176,128]{1,0:T(8,128)(2,1)S(1)}, bf16[176,128]{1,0:T(8,128)(2,1)S(1)}, u32[]{:S(2)}, u32[]{:S(2)}) collective-permute-start(bf16[176,128]{1,0:T(8,128)(2,1)S(1)} %get-tuple-element.26), channel_id=1, source_target_pairs={{0,16},{16,0},{1,17},{17,1},{2,18},{18,2},{3,19},{19,3},{4,20},{20... | collective-permute-start | bytes 135176 | tf_op jit(solution)/shard_map/ppermute | solution.py:692
  10.3 4.7 %collective-permute-start.4 = (bf16[128,128]{1,0:T(8,128)(2,1)S(1)}, bf16[128,128]{1,0:T(8,128)(2,1)S(1)}, u32[]{:S(2)}, u32[]{:S(2)}) collective-permute-start(bf16[128,128]{1,0:T(8,128)(2,1)S(1)} %get-tuple-element.27), channel_id=1, source_target_pairs={{0,17},{1,16},{16,1},{17,0},{2,19},{3,18},{18,3},{19,2},{4,21},{5,... | collective-permute-start | bytes 98312 | tf_op jit(solution)/shard_map/ppermute | solution.py:701
  11.8 3.3 %collective-permute-start.5 = (bf16[144,128]{1,0:T(8,128)(2,1)S(1)}, bf16[144,128]{1,0:T(8,128)(2,1)S(1)}, u32[]{:S(2)}, u32[]{:S(2)}) collective-permute-start(bf16[144,128]{1,0:T(8,128)(2,1)S(1)} %get-tuple-element.29), channel_id=1, source_target_pairs={{0,1},{1,0},{2,3},{3,2},{4,5},{5,4},{6,7},{7,6},{8,9},{9,8},{10,11... | collective-permute-start | bytes 110600 | tf_op jit(solution)/shard_map/ppermute | solution.py:700
  14.4 3.1 %collective-permute-start.6 = (bf16[96,128]{1,0:T(8,128)(2,1)S(1)}, bf16[96,128]{1,0:T(8,128)(2,1)S(1)}, u32[]{:S(2)}, u32[]{:S(2)}) collective-permute-start(bf16[96,128]{1,0:T(8,128)(2,1)S(1)} %get-tuple-element.30), channel_id=1, source_target_pairs={{0,16},{16,0},{1,17},{17,1},{2,18},{18,2},{3,19},{19,3},{4,20},{20... | collective-permute-start | bytes 73736 | tf_op jit(solution)/shard_map/ppermute | solution.py:715
